TPU v7x, 512 devices: a whole 4x4x16 slice. The times are simulated.
512 devices in a mesh: col: 16 (over z_lo, x), slab: 32 (over y, z_hi, core).
Axes of the slice: x: 4, y: 4, z: 16 (z_hi: 4, z_lo: 4; z = z_hi * 4 + z_lo), core: 2. Of those that a mesh axis runs over, the one named last changes fastest.
Arguments:
- p_star: float32 [128, 256, 256], P('col', 'slab'), may hold values from 0 to 3
- u_star: float32 [128, 256, 256], P('col', 'slab'), may hold values from -6 to 6
- v_star: float32 [128, 256, 256], P('col', 'slab'), may hold values from -6 to 6
- w_star: float32 [128, 256, 256], P('col', 'slab'), may hold values from -6 to 6
- flags: int32 [128, 256, 256], P('col', 'slab'), may hold values from 0 to 2
- panel_cell: int32 [131072], P(('col', 'slab')), may hold values from 0 to 16383
- panel_section: int32 [131072], P(('col', 'slab')), may hold values from 0 to 127, as said below
- panel_geom: float32 [3, 131072], P(None, ('col', 'slab')), may hold values from -0.12 to 0.12
Outputs:
- pressure: float32 [128, 256, 256], P('col', 'slab')
- vertical_velocity: float32 [128, 256, 256], P('col', 'slab')
- section_loads: float32 [3, 128], P(None, 'slab')
Inputs may be any that keep to these rules, and one draw needn't show every extreme that they name: `panel_section`: panel i belongs to the block of device i // 256, devices counted with col slowest; with s that device's slab index, its section lies between 4 * s - 2 and 4 * s + 5.
All inputs are finite; a program needn't handle non-finite values.
Results may differ from a plain program's by a relative error of at most 0.0014.
Values sent between devices are 32-bit elements; how exact they have to be, the bound alone decides.
No kernel may reach another device: no remote copies, remote signals or barrier semaphores. Data moves between devices by JAX's collectives and lax.ppermute only.
A program may use at most 64 MiB of HBM per device.

v0:
```python
import jax
import jax.numpy as jnp
from jax import lax
from jax.sharding import PartitionSpec as P

SEC_DEV = 4
EOS_ITERS = 3


KAPPA_SCALE = 0.01
AIR_DENSITY = 0.1
GAMMA_HORIZ = 0.001
DIVERGENCE_SCALE = 0.005


def with_halo(x, sides, width):
    for axis, dim in sides:
        devices, length = (lax.axis_size(axis), x.shape[dim])
        up = [(i, (i + 1) % devices) for i in range(devices - 1)]
        down = [(j, i) for i, j in up]
        last = lax.slice_in_dim(x, length - width, length, axis=dim)
        leading = lax.slice_in_dim(x, 0, width, axis=dim)
        before = lax.ppermute(last, axis, up)
        after = lax.ppermute(leading, axis, down)
        x = jnp.concatenate([before, x, after], axis=dim)
    return x


def carried_in(x, axis, combine, identity, reverse):
    devices, mine = (lax.axis_size(axis), lax.axis_index(axis))
    everything = jax.tree.map(lambda part: lax.all_gather(part, axis), x)
    start = jax.tree.map(
        lambda part, zero: jnp.broadcast_to(jnp.asarray(zero, part.dtype), part.shape), x, identity
    )

    def lap(k, before):
        at = devices - 1 - k if reverse else k
        reached = at > mine if reverse else at < mine
        new = combine(before, jax.tree.map(lambda part: part[at], everything))
        return jax.tree.map(lambda a, b: jnp.where(reached, a, b), new, before)

    return lax.fori_loop(0, devices, lap, start)


def equation_of_state(p_star, flags):
    air_frac = jnp.where(
        flags == 1, jnp.float32(1.0), jnp.where(flags == 2, jnp.float32(0.5), jnp.float32(0.0))
    )
    water_density = jnp.ones_like(p_star)
    for newton in range(EOS_ITERS):
        square_term = water_density * water_density
        cube_term = square_term * water_density
        sixth_power = cube_term * cube_term
        seventh_power = sixth_power * water_density
        water_density = water_density - (seventh_power - 1.0 - p_star) / (7.0 * sixth_power)
    shifted = 1.0 + p_star
    air_density = AIR_DENSITY * jnp.power(shifted, 1.0 / 1.4)
    density = air_frac * air_density + (1.0 - air_frac) * water_density
    compress_coef = KAPPA_SCALE * (air_frac / (1.4 * shifted) + (1.0 - air_frac) / (7.0 * shifted))
    return (density, compress_coef)


def normalize(matrix):
    reduce_axes = tuple(range(matrix.ndim - 2))
    return matrix / jnp.max(jnp.abs(matrix), axis=reduce_axes, keepdims=True)


def matmul_three(left_side, right_side):
    return jnp.sum(left_side[:, :, None] * right_side[None, :, :], axis=1)


def combine_matrix(earlier, later):
    return normalize(matmul_three(later, earlier))


def combine_affine(earlier, later):
    return (later[0] + later[1] * earlier[0], later[1] * earlier[1])


def compose(near_band, diagonal, far_band, source):
    identity = jnp.broadcast_to(
        jnp.eye(3, dtype=jnp.float32)[:, :, None, None], (3, 3) + diagonal.shape[1:]
    )

    def advance(current, coeffs):
        near_row, diag_row, far_row, source_row = coeffs
        first_row = far_row * current[2]
        second_row = source_row * current[2] - near_row * current[1]
        third_row = diag_row * current[2] - near_row * current[0]
        return (normalize(jnp.stack([first_row, second_row, third_row])), None)

    composed, unused = lax.scan(
        advance, identity, (near_band, diagonal, far_band, source), reverse=False
    )
    return composed


def sweep(sub_band, diagonal, super_band, source, start_ratio, start_shift):

    def forward_step(current, coeffs):
        ratio_prev, shift_prev = current
        sub_row, diag_row, super_row, source_row = coeffs
        pivot_value = diag_row - sub_row * ratio_prev
        ratio_row = super_row / pivot_value
        shift_row = (source_row - sub_row * shift_prev) / pivot_value
        return ((ratio_row, shift_row), (ratio_row, shift_row))

    finals, (ratios, shifts) = lax.scan(
        forward_step, (start_ratio, start_shift), (sub_band, diagonal, super_band, source)
    )
    return (ratios, shifts)


def back_substitute(ratios, shifts, above_value):

    def back_step(following, coeffs):
        ratio_row, shift_row = coeffs
        value_row = shift_row - ratio_row * following
        return (value_row, value_row)

    last_value, solution = lax.scan(back_step, above_value, (ratios, shifts), reverse=True)
    return solution


def per_device(p_star, u_star, v_star, w_star, flags, panel_cell, panel_section, panel_geom):
    depth_cells = p_star.shape[0]
    col_count = lax.axis_size("col")
    col_index = lax.axis_index("col")
    horizontal = with_halo(jnp.stack([p_star, u_star]), (("slab", 2),), 1)
    density, compress_coef = equation_of_state(p_star, flags)
    vertical = with_halo(jnp.stack([density, w_star]), (("col", 1),), 1)
    pressure_x = horizontal[0]
    velocity_x = horizontal[1]
    pad_y = jnp.pad(p_star, ((0, 0), (0, 0), (1, 1)))
    laplacian = (
        pressure_x[:, 2:] + pressure_x[:, :-2] + pad_y[:, :, 2:] + pad_y[:, :, :-2] - 4.0 * p_star
    )
    v_pad = jnp.pad(v_star, ((0, 0), (0, 0), (1, 1)))
    vertical_w = vertical[1]
    divergence = (
        (velocity_x[:, 2:] - velocity_x[:, :-2]) * 0.5
        + (v_pad[:, :, 2:] - v_pad[:, :, :-2]) * 0.5
        + (vertical_w[2:] - vertical_w[:-2]) * 0.5
    )
    source = compress_coef * p_star + GAMMA_HORIZ * laplacian - DIVERGENCE_SCALE * divergence
    density_ext = vertical[0]
    face_coef = 2.0 / (density_ext[:-1] + density_ext[1:])
    row_index = lax.broadcasted_iota(jnp.int32, (depth_cells, 1, 1), 0)
    lower_face = jnp.where((row_index == 0) & (col_index == 0), jnp.float32(0.0), face_coef[:-1])
    upper_face = jnp.where(
        (row_index == depth_cells - 1) & (col_index == col_count - 1),
        jnp.float32(0.0),
        face_coef[1:],
    )
    diagonal = compress_coef + lower_face + upper_face
    sub_band = -lower_face
    super_band = -upper_face
    forward = compose(sub_band, diagonal, super_band, source)
    identity = jnp.broadcast_to(jnp.eye(3, dtype=jnp.float32)[:, :, None, None], forward.shape)
    prefix = carried_in(forward, "col", combine_matrix, identity, False)
    incoming = prefix[:, 2]
    start_ratio = incoming[0] / incoming[2]
    start_shift = incoming[1] / incoming[2]
    ratios, shifts = sweep(sub_band, diagonal, super_band, source, start_ratio, start_shift)

    def affine_step(current, coeffs):
        ratio_row, shift_row = coeffs
        return ((shift_row - ratio_row * current[0], -ratio_row * current[1]), None)

    zero_row = jnp.zeros_like(diagonal[0])
    one_row = jnp.ones_like(diagonal[0])
    (offset_term, factor_term), unused = lax.scan(
        affine_step, (zero_row, one_row), (ratios, shifts), reverse=True
    )
    beyond = carried_in(
        (offset_term, factor_term), "col", combine_affine, (zero_row, one_row), True
    )
    above_value = beyond[0]
    solution = back_substitute(ratios, shifts, above_value)
    below_value = start_shift - start_ratio * solution[0]
    above = jnp.concatenate([solution[1:], above_value[None]], 0)
    below = jnp.concatenate([below_value[None], solution[:-1]], 0)
    vertical_velocity = w_star - 0.5 * (
        upper_face * (above - solution) + lower_face * (solution - below)
    )
    flat_pressure = solution.reshape(-1)
    sampled = flat_pressure[panel_cell]
    panel_terms = panel_geom * sampled[None, :]
    section_count = SEC_DEV * lax.axis_size("slab")
    onehot = (
        panel_section[:, None] == lax.broadcasted_iota(jnp.int32, (1, section_count), 1)
    ).astype(jnp.float32)
    partial_loads = jnp.dot(
        panel_terms, onehot, precision=lax.Precision.HIGHEST, preferred_element_type=jnp.float32
    )
    totals = lax.psum(partial_loads, ("col", "slab"))
    section_loads = lax.dynamic_slice_in_dim(totals, lax.axis_index("slab") * SEC_DEV, SEC_DEV, 1)
    return (solution, vertical_velocity, section_loads)


def solution(mesh):
    in_specs = (
        P("col", "slab", None),
        P("col", "slab", None),
        P("col", "slab", None),
        P("col", "slab", None),
        P("col", "slab", None),
        P(("col", "slab")),
        P(("col", "slab")),
        P(None, ("col", "slab")),
    )
    out_specs = (P("col", "slab", None), P("col", "slab", None), P(None, "slab"))
    return jax.shard_map(
        per_device, mesh=mesh, in_specs=in_specs, out_specs=out_specs, check_vma=False
    )
```

profile of v0, /device:TPU:1, one launch (start us, length us, event | category | flops | bytes accessed | tf_op | source)
XLA Modules:
  0.0 331.8 jit_solution(1948185032001143021)
XLA Ops:
  7.2 1.0 fusion.46
  8.2 0.8 pad_maximum_fusion.6
  9.0 3.9 %collective-permute-start = (f32[2,1,8,256]{3,2,1,0:T(8,128)S(1)}, f32[2,1,8,256]{3,2,1,0:T(8,128)S(1)}, u32[]{:S(2)}, u32[]{:S(2)}) collective-permute-start(f32[2,1,8,256]{3,2,1,0:T(8,128)S(1)} %get-tuple-element.639), channel_id=1, source_target_pairs={{0,32},{32,64},{64,96},{96,128},{128,160},{160,192},{192,224},{224... | collective-permute-start | bytes 49160 | tf_op jit(solution)/shard_map/ppermute | solution.py:23
  12.9 1.3 collective-permute-start.1
  14.2 1.0 pad_maximum_fusion.4
  15.2 9.7 %collective-permute-start.2 = (f32[2,8,1,256]{3,2,1,0:T(1,128)S(1)}, f32[2,8,1,256]{3,2,1,0:T(1,128)S(1)}, u32[]{:S(2)}, u32[]{:S(2)}) collective-permute-start(f32[2,8,1,256]{3,2,1,0:T(1,128)S(1)} %get-tuple-element.635), channel_id=1, source_target_pairs={{0,1},{1,2},{2,3},{3,4},{4,5},{5,6},{6,7},{7,8},{8,9},{9,10},{10,1... | collective-permute-start | bytes 49160 | tf_op jit(solution)/shard_map/ppermute | solution.py:23
  24.9 1.9 collective-permute-start.3
  26.9 7.0 %collective-permute-done.3 = f32[2,8,1,256]{3,2,1,0:T(1,128)S(1)} collective-permute-done((f32[2,8,1,256]{3,2,1,0:T(1,128)S(1)}, f32[2,8,1,256]{3,2,1,0:T(1,128)S(1)}, u32[]{:S(2)}, u32[]{:S(2)}) %collective-permute-start.3) | collective-permute-done | bytes 16416 | tf_op jit(solution)/shard_map/ppermute | solution.py:24
  33.8 0.9 pad_maximum_fusion.1
  35.2 0.9 while.88
  36.8 76.9 %all-gather.5.cloned.1.call-done = f32[48,3,8,256]{3,2,1,0:T(8,128)} async-done(((f32[3,3,8,256]{3,2,1,0:T(8,128)}), f32[48,3,8,256]{3,2,1,0:T(8,128)}) %all-gather.5.cloned.1.call-update) | async-done | bytes 1179664 | tf_op jit(solution)/shard_map/all_gather | solution.py:31
  113.8 15.6 %while.89 = (s32[]{:T(128)}, f32[3,3,8,256]{3,2,1,0:T(8,128)S(1)}, s32[]{:T(128)}, f32[16,3,3,8,256]{4,3,2,1,0:T(8,128)}, s32[]{:T(128)}) while((s32[]{:T(128)}, f32[3,3,8,256]{3,2,1,0:T(8,128)S(1)}, s32[]{:T(128)}, f32[16,3,3,8,256]{4,3,2,1,0:T(8,128)}, s32[]{:T(128)}) %tuple.216), condition=%wide.region_6.7_spmd, body=%wide.region_3.6_spmd.sunk | while | flops 163843 | bytes 680011 | solution.py:42
  113.8 0.9 dynamic-slice_bitcast_fusion.10
  114.8 0.9 dynamic-slice_bitcast_fusion.10
  115.7 0.9 dynamic-slice_bitcast_fusion.10
  116.7 0.9 dynamic-slice_bitcast_fusion.10
  117.7 0.9 dynamic-slice_bitcast_fusion.10
  118.7 0.9 dynamic-slice_bitcast_fusion.10
  119.6 0.9 dynamic-slice_bitcast_fusion.10
  120.6 0.9 dynamic-slice_bitcast_fusion.10
  121.6 0.9 dynamic-slice_bitcast_fusion.10
  122.6 0.9 dynamic-slice_bitcast_fusion.10
  123.6 0.9 dynamic-slice_bitcast_fusion.10
  124.5 0.9 dynamic-slice_bitcast_fusion.10
  125.5 0.9 dynamic-slice_bitcast_fusion.10
  126.5 0.9 dynamic-slice_bitcast_fusion.10
  127.5 0.9 dynamic-slice_bitcast_fusion.10
  128.4 0.9 dynamic-slice_bitcast_fusion.10
  130.1 35.5 %all-gather.1 = f32[128,256]{1,0:T(8,128)S(1)} all-gather(f32[8,256]{1,0:T(8,128)S(1)} %get-tuple-element.505), channel_id=3, replica_groups=mesh['col'=16,'slab'=32] {'col'}, dimensions={0}, use_global_device_ids=true | all-gather | bytes 139264 | tf_op jit(solution)/shard_map/all_gather | solution.py:31
  165.6 30.5 %all-gather.2 = f32[128,256]{1,0:T(8,128)S(1)} all-gather(f32[8,256]{1,0:T(8,128)S(1)} %get-tuple-element.506), channel_id=4, replica_groups=mesh['col'=16,'slab'=32] {'col'}, dimensions={0}, use_global_device_ids=true | all-gather | bytes 139264 | tf_op jit(solution)/shard_map/all_gather | solution.py:31
  197.2 1.7 gather_fusion
  199.2 124.4 %psum.7 = f32[3,128]{1,0:T(4,128)S(1)} all-reduce(f32[3,128]{1,0:T(4,128)S(1)} %fusion.8), channel_id=1, replica_groups=mesh['col'=16,'slab'=32] {'col','slab'}, use_global_device_ids=true, to_apply=%region_15.16 | all-reduce | flops 384 | bytes 3072 | tf_op jit(solution)/shard_map/psum | solution.py:196
  (178 shorter events, 6.2 us)
Async XLA Ops:
  7.2 27.6 %copy-start.2 = (f32[8,8,256]{2,1,0:T(8,128)S(1)}, f32[8,8,256]{2,1,0:T(8,128)}, u32[]{:S(2)}) copy-start(f32[8,8,256]{2,1,0:T(8,128)} %param.23) | copy-start | bytes 196612
  7.2 106.5 %all-gather.5.cloned.1.call-start = ((), (), s32[]{:S(2)}) async-start(), calls=%async_computation | async-start | bytes 1253376 | tf_op jit(solution)/shard_map/all_gather | solution.py:31
  8.2 26.8 %copy-start.3 = (f32[8,8,256]{2,1,0:T(8,128)S(1)}, f32[8,8,256]{2,1,0:T(8,128)}, u32[]{:S(2)}) copy-start(f32[8,8,256]{2,1,0:T(8,128)} %param.20) | copy-start | bytes 196612
  8.2 26.8 %copy-start.4 = (f32[8,8,256]{2,1,0:T(8,128)S(1)}, f32[8,8,256]{2,1,0:T(8,128)}, u32[]{:S(2)}) copy-start(f32[8,8,256]{2,1,0:T(8,128)} %param.22) | copy-start | bytes 196612
  9.0 25.8 %collective-permute-start = (f32[2,1,8,256]{3,2,1,0:T(8,128)S(1)}, f32[2,1,8,256]{3,2,1,0:T(8,128)S(1)}, u32[]{:S(2)}, u32[]{:S(2)}) collective-permute-start(f32[2,1,8,256]{3,2,1,0:T(8,128)S(1)} %get-tuple-element.639), channel_id=1, source_target_pairs={{0,32},{32,64},{64,96},{96,128},{128,160},{160,192},{192,224},{224... | collective-permute-start | bytes 49160 | tf_op jit(solution)/shard_map/ppermute | solution.py:23
  12.9 21.9 %collective-permute-start.1 = (f32[2,1,8,256]{3,2,1,0:T(8,128)S(1)}, f32[2,1,8,256]{3,2,1,0:T(8,128)S(1)}, u32[]{:S(2)}, u32[]{:S(2)}) collective-permute-start(f32[2,1,8,256]{3,2,1,0:T(8,128)S(1)} %get-tuple-element.640), channel_id=1, source_target_pairs={{32,0},{64,32},{96,64},{128,96},{160,128},{192,160},{224,192},{256... | collective-permute-start | bytes 49160 | tf_op jit(solution)/shard_map/ppermute | solution.py:24
  15.2 11.6 %collective-permute-start.2 = (f32[2,8,1,256]{3,2,1,0:T(1,128)S(1)}, f32[2,8,1,256]{3,2,1,0:T(1,128)S(1)}, u32[]{:S(2)}, u32[]{:S(2)}) collective-permute-start(f32[2,8,1,256]{3,2,1,0:T(1,128)S(1)} %get-tuple-element.635), channel_id=1, source_target_pairs={{0,1},{1,2},{2,3},{3,4},{4,5},{5,6},{6,7},{7,8},{8,9},{9,10},{10,1... | collective-permute-start | bytes 49160 | tf_op jit(solution)/shard_map/ppermute | solution.py:23
  24.9 9.0 %collective-permute-start.3 = (f32[2,8,1,256]{3,2,1,0:T(1,128)S(1)}, f32[2,8,1,256]{3,2,1,0:T(1,128)S(1)}, u32[]{:S(2)}, u32[]{:S(2)}) collective-permute-start(f32[2,8,1,256]{3,2,1,0:T(1,128)S(1)} %get-tuple-element.636), channel_id=1, source_target_pairs={{1,0},{2,1},{3,2},{4,3},{5,4},{6,5},{7,6},{8,7},{9,8},{10,9},{11,1... | collective-permute-start | bytes 49160 | tf_op jit(solution)/shard_map/ppermute | solution.py:24
  35.2 1.5 copy-start.5
  36.1 0.6 copy-start
  196.1 2.8 copy-start.6
  196.1 2.8 copy-start.7
  197.1 127.8 %copy-start.1 = (f32[8,8,256]{2,1,0:T(8,128)}, f32[8,8,256]{2,1,0:T(8,128)S(1)}, u32[]{:S(2)}) copy-start(f32[8,8,256]{2,1,0:T(8,128)S(1)} %get-tuple-element.498) | copy-start | bytes 196612
Sparse Core Ops, SparseCore 0:
  36.9 76.7 all-gather.4
where the time goes:
time: 333 us; the launch traced here: 332 us
  blocking collectives  190 us (57%)
  waiting for transfers between devices  83.9 us (25%)
  local copies, waits for them, and re-layouts  17.7 us (5%)
  starting transfers between devices  16.8 us (5%)
  between operations  14.4 us (4%)
  other arithmetic  6.28 us (2%)
    psum x1, blocking collectives, per_device(): totals = lax.psum(partial_loads, ('col', 'slab'))  124 us
    all_gather x1, waiting for transfers between devices, carried_in(): everything = jax.tree.map(lambda part: lax.all_gather(part, axis), x)  76.9 us
    all_gather x2, blocking collectives, carried_in(): everything = jax.tree.map(lambda part: lax.all_gather(part, axis), x)  66 us
    mul x16, local copies, waits for them, and re-layouts, matmul_three(): return jnp.sum(left_side[:, :, None] * right_side[None, :, :], axis=1)  14.3 us
    ppermute x2, starting transfers between devices, with_halo(): before = lax.ppermute(last, axis, up)  13.6 us
    ppermute x2, waiting for transfers between devices, with_halo(): after = lax.ppermute(leading, axis, down)  6.99 us
  transfers between devices with their start and end apart: 5, of which 2 were waited for; matrix products, arithmetic and copies ran while one was open for 1% of the time, Pallas kernels for 0%

commit v1 on v0

v1 whole, which is shorter than its diff:
```python
import functools

import jax
import jax.numpy as jnp
from jax import lax
from jax.experimental import pallas as pl
from jax.experimental.pallas import tpu as pltpu
from jax.sharding import PartitionSpec as P

SEC_DEV = 4
EOS_ITERS = 3
KAPPA_SCALE = 0.01
AIR_DENSITY = 0.1
GAMMA_HORIZ = 0.001
DIVERGENCE_SCALE = 0.005
HALF_DIV = 0.5 * DIVERGENCE_SCALE

CZ = 8
CX = 8
NY = 256
LANES = 128
COLS = 16
PANELS_DEV = 256
REACH = 2
SEND_ROWS = 24
BACK_ROWS = 8

F32 = jnp.float32


def row_iota(shape):
    return lax.broadcasted_iota(jnp.int32, shape, 0)


def lane_iota(shape):
    return lax.broadcasted_iota(jnp.int32, shape, 1)


def level(ref, z):
    return ref[z * CX : (z + 1) * CX, :]


def split_three(x):
    high = x.astype(jnp.bfloat16)
    rest = x - high.astype(F32)
    middle = rest.astype(jnp.bfloat16)
    low = (rest - middle.astype(F32)).astype(jnp.bfloat16)
    return high, middle, low


def pick(fields, onehot, row_mask):
    total = None
    for part in split_three(fields):
        term = jnp.dot(part, onehot, preferred_element_type=F32)
        total = term if total is None else total + term
    return jnp.sum(jnp.where(row_mask, total, 0.0), axis=0, keepdims=True)


def panel_masks(cell):
    onehot = (row_iota((NY, PANELS_DEV)) == (cell & (NY - 1))).astype(F32)
    row_mask = row_iota((CZ * CX, PANELS_DEV)) == (cell >> 8)
    return onehot.astype(jnp.bfloat16), row_mask


def condense(ground, edges):
    first, here, link = ground[0], ground[1], edges[0]
    to_first, to_next, inverse = [], [], []
    for j in range(1, len(ground) - 1):
        edge = edges[j]
        inv = 1.0 / (here + link + edge)
        a, b = link * inv, edge * inv
        first = first + a * here
        here = ground[j + 1] + b * here
        link = link * b
        to_first.append(a)
        to_next.append(b)
        inverse.append(inv)
    return first, here, link, to_first, to_next, inverse


def condense_source(source, to_first, to_next, inverse):
    first, here = source[0], source[1]
    offsets = []
    for j in range(1, len(source) - 1):
        a, b = to_first[j - 1], to_next[j - 1]
        offsets.append(here * inverse[j - 1])
        first = first + a * here
        here = source[j + 1] + b * here
    return first, here, offsets


def expand(first, last, to_first, to_next, offsets):
    values = [last]
    for a, b, offset in zip(reversed(to_first), reversed(to_next), reversed(offsets)):
        values.append(offset + a * first + b * values[-1])
    values.append(first)
    return values[::-1]


def section_rows(terms):
    rows = []
    for term in terms:
        sums = jnp.sum(term, axis=1, keepdims=True)
        on_diagonal = row_iota((8, LANES)) == lane_iota((8, LANES))
        rows.append(jnp.sum(jnp.where(on_diagonal, sums, 0.0), axis=0, keepdims=True))
    return rows


def edge_kernel(p_ref, u_ref, pair_ref, other_ref):
    even = lax.rem(lax.axis_index("slab"), 2) == 0

    def plane(ref, x):
        return ref[:, x, :]

    leading = GAMMA_HORIZ * plane(p_ref, 0) - HALF_DIV * plane(u_ref, 0)
    trailing = GAMMA_HORIZ * plane(p_ref, CX - 1) + HALF_DIV * plane(u_ref, CX - 1)
    pair_ref[...] = jnp.where(even, trailing, leading)
    other_ref[...] = jnp.where(even, leading, trailing)


A_AT, B_AT, I_AT, FACE_AT, PORT_AT = 0, 6, 12, 18, 25
MAT_LEVELS = 30


def matrix_kernel(p_ref, u_ref, v_ref, w_ref, flags_ref, cell_ref, mat_ref, src_ref, panel_ref):
    shape = (CX, NY)
    rows, lanes = row_iota(shape), lane_iota(shape)
    densities, kappas = [], []
    for z in range(CZ):
        p, flags = level(p_ref, z), level(flags_ref, z)
        air = jnp.where(flags == 1, 1.0, jnp.where(flags == 2, 0.5, 0.0)).astype(F32)
        water = jnp.ones_like(p)
        for _ in range(EOS_ITERS):
            square = water * water
            cube = square * water
            sixth = cube * cube
            water = water - (sixth * water - 1.0 - p) / (7.0 * sixth)
        shifted = 1.0 + p
        air_density = AIR_DENSITY * jnp.exp(jnp.log(shifted) * (1.0 / 1.4))
        densities.append(air * air_density + (1.0 - air) * water)
        kappa = KAPPA_SCALE * (air / (1.4 * shifted) + (1.0 - air) / (7.0 * shifted))
        kappas.append(kappa)

        u, v = level(u_ref, z), level(v_ref, z)

        def beside(x, axis, step):
            size = shape[axis]
            moved = pltpu.roll(x, (-step) % size, axis)
            at = rows if axis == 0 else lanes
            return jnp.where(at == (size - 1 if step > 0 else 0), 0.0, moved)

        laplacian = (
            beside(p, 0, 1) + beside(p, 0, -1) + beside(p, 1, 1) + beside(p, 1, -1) - 4.0 * p
        )
        divergence = 0.5 * (beside(u, 0, 1) - beside(u, 0, -1)) + 0.5 * (
            beside(v, 1, 1) - beside(v, 1, -1)
        )
        if z == 0:
            w_difference = level(w_ref, 1)
        elif z == CZ - 1:
            w_difference = -level(w_ref, CZ - 2)
        else:
            w_difference = level(w_ref, z + 1) - level(w_ref, z - 1)
        divergence = divergence + 0.5 * w_difference
        src_ref[z * CX : (z + 1) * CX, :] = (
            kappa * p + GAMMA_HORIZ * laplacian - DIVERGENCE_SCALE * divergence
        )
    faces = [2.0 / (densities[z] + densities[z + 1]) for z in range(CZ - 1)]
    first, last, link, to_first, to_next, inverse = condense(kappas, faces)
    stored = to_first + to_next + inverse + faces + [first, last, link, densities[0], densities[-1]]
    for at, value in enumerate(stored):
        mat_ref[at * CX : (at + 1) * CX, :] = value

    zero, one = jnp.zeros(shape, F32), jnp.ones(shape, F32)
    no_offset = [zero] * (CZ - 2)
    onehot, row_mask = panel_masks(cell_ref[...])
    from_first = expand(one, zero, to_first, to_next, no_offset)
    from_last = expand(zero, one, to_first, to_next, no_offset)
    panel_ref[0:1, :] = pick(jnp.concatenate(from_first, 0), onehot, row_mask)
    panel_ref[1:2, :] = pick(jnp.concatenate(from_last, 0), onehot, row_mask)


def pack_kernel(
    mat_ref, src_ref, pair_ref, other_ref, w_ref, panel_ref, cell_ref, sec_ref, geom_ref,
    send_ref, offset_ref, constant_ref, rows_ref,
):
    slab = lax.axis_index("slab")
    even = lax.rem(slab, 2) == 0
    shape = (CX, NY)
    rows = row_iota(shape)
    received, beyond = pair_ref[...], other_ref[...]
    from_left = jnp.where(even, beyond, received)
    from_right = jnp.where(even, received, beyond)
    source = []
    for z in range(CZ):
        halo = jnp.where(rows == 0, from_left[z : z + 1, :], 0.0) + jnp.where(
            rows == CX - 1, from_right[z : z + 1, :], 0.0
        )
        source.append(level(src_ref, z) + halo)
    to_first = [level(mat_ref, A_AT + j) for j in range(CZ - 2)]
    to_next = [level(mat_ref, B_AT + j) for j in range(CZ - 2)]
    inverse = [level(mat_ref, I_AT + j) for j in range(CZ - 2)]
    first, last, offsets = condense_source(source, to_first, to_next, inverse)
    for j, offset in enumerate(offsets):
        offset_ref[j * CX : (j + 1) * CX, :] = offset

    section = sec_ref[...] - (slab * SEC_DEV - REACH)
    cell = cell_ref[...]
    column = cell & (CX * NY - 1)
    panel_rows = [geom_ref[k : k + 1, :] for k in range(3)]
    panel_rows += [panel_ref[0:1, :], panel_ref[1:2, :]]
    panel_rows += [column.astype(F32), section.astype(F32)]
    rows_ref[...] = jnp.zeros_like(rows_ref)
    for at, row in enumerate(panel_rows):
        for half in range(2):
            rows_ref[1 + 2 * at + half : 2 + 2 * at + half, :] = row[
                :, half * LANES : (half + 1) * LANES
            ]
    for owner in range(COLS):
        send_ref[owner * SEND_ROWS + 8 : owner * SEND_ROWS + 24, :] = rows_ref[...]
    ports = [level(mat_ref, PORT_AT + j) for j in range(3)] + [first, last]
    ports += [level(mat_ref, PORT_AT + 3), level(mat_ref, PORT_AT + 4)]
    ports += [level(w_ref, 0), level(w_ref, CZ - 1)]
    for at, value in enumerate(ports):
        for half in range(2):
            send_ref[pl.ds(half * SEND_ROWS + at, CX, stride=2 * SEND_ROWS), :] = value[
                :, half * LANES : (half + 1) * LANES
            ]

    zero = jnp.zeros(shape, F32)
    constant = expand(zero, zero, to_first, to_next, offsets)
    onehot, row_mask = panel_masks(cell)
    at_panel = pick(jnp.concatenate(constant, 0), onehot, row_mask)
    in_section = row_iota((8, PANELS_DEV)) == section
    terms = [
        jnp.where(in_section, geom_ref[k : k + 1, :] * at_panel, 0.0) for k in range(3)
    ]
    constant_ref[...] = jnp.zeros_like(constant_ref)
    for k, row in enumerate(section_rows(terms)):
        constant_ref[k : k + 1, :] = row


def owner_kernel(recv_ref, constant_ref, back_ref, group_ref, ends_ref, parts_ref, picked_ref):
    def value(at, x):
        return recv_ref[pl.ds(x * SEND_ROWS + at, 4, stride=4 * SEND_ROWS), :]

    per = [[value(at, x) for x in range(4)] for at in range(9)]
    low_k, high_k, link, low_r, high_r, low_d, high_d, low_w, high_w = per
    join = [2.0 / (high_d[x] + low_d[x + 1]) for x in range(3)]
    for x in range(3):
        high_r[x] = high_r[x] - HALF_DIV * low_w[x + 1]
        low_r[x + 1] = low_r[x + 1] + HALF_DIV * high_w[x]
    ground, source, edges = [], [], []
    for x in range(4):
        ground += [low_k[x], high_k[x]]
        source += [low_r[x], high_r[x]]
        edges += [link[x]] + ([join[x]] if x < 3 else [])
    first, last, across, to_first, to_next, inverse = condense(ground, edges)
    first_r, last_r, offsets = condense_source(source, to_first, to_next, inverse)

    stored = [first, last, across, first_r, last_r, low_d[0], high_d[3], low_w[0], high_w[3]]
    for at, x in enumerate(stored):
        group_ref[at * 4 : (at + 1) * 4, :] = x
    per = [[group_ref[at * 4 + z : at * 4 + z + 1, :] for z in range(4)] for at in range(9)]
    low_k, high_k, link, low_r, high_r, low_d, high_d, low_w, high_w = per
    outer = [2.0 / (high_d[z] + low_d[z + 1]) for z in range(3)]
    for z in range(3):
        high_r[z] = high_r[z] - HALF_DIV * low_w[z + 1]
        low_r[z + 1] = low_r[z + 1] + HALF_DIV * high_w[z]
    ground, source, edges = [], [], []
    for z in range(4):
        ground += [low_k[z], high_k[z]]
        source += [low_r[z], high_r[z]]
        edges += [link[z]] + ([outer[z]] if z < 3 else [])
    k_a, k_b, f_ab, a_list, b_list, i_list = condense(ground, edges)
    r_a, r_b, o_list = condense_source(source, a_list, b_list, i_list)
    scale = 1.0 / (k_a * k_b + f_ab * (k_a + k_b))
    p_a = ((k_b + f_ab) * r_a + f_ab * r_b) * scale
    p_b = ((k_a + f_ab) * r_b + f_ab * r_a) * scale
    nodes = expand(p_a, p_b, a_list, b_list, o_list)
    zero_row = jnp.zeros((1, LANES), F32)
    flux = [outer[z] * (nodes[2 * z + 2] - nodes[2 * z + 1]) for z in range(3)]
    for z in range(4):
        ends_ref[z : z + 1, :] = nodes[2 * z]
        ends_ref[4 + z : 5 + z, :] = nodes[2 * z + 1]
        ends_ref[8 + z : 9 + z, :] = flux[z - 1] if z > 0 else zero_row
        ends_ref[12 + z : 13 + z, :] = flux[z] if z < 3 else zero_row

    nodes = expand(ends_ref[0:4, :], ends_ref[4:8, :], to_first, to_next, offsets)
    inner = [join[x] * (nodes[2 * x + 2] - nodes[2 * x + 1]) for x in range(3)]
    below = [ends_ref[8:12, :]] + inner
    above = inner + [ends_ref[12:16, :]]

    def put(ref, rows, at, x, what):
        ref[pl.ds(x * rows + at, 4, stride=4 * rows), :] = what

    for x in range(4):
        put(back_ref, BACK_ROWS, 0, x, nodes[2 * x])
        put(back_ref, BACK_ROWS, 1, x, nodes[2 * x + 1])
        put(back_ref, BACK_ROWS, 2, x, below[x])
        put(back_ref, BACK_ROWS, 3, x, above[x])
        for end in range(2):
            for at, part in enumerate(split_three(nodes[2 * x + end])):
                put(parts_ref, 8, 3 * end + at, x, part.astype(F32))
            put(parts_ref, 8, 6 + end, x, jnp.zeros((4, LANES), F32))

    mine = lax.axis_index("col") * LANES
    want = (row_iota((LANES, LANES)) + mine).astype(F32)
    for block in range(COLS):
        ends = parts_ref[block * 8 : (block + 1) * 8, :].astype(jnp.bfloat16)
        at = block * SEND_ROWS + 9 + 10
        for half in range(2):
            column = recv_ref[at + half : at + half + 1, :]
            onehot = jnp.where(want == column, 1.0, 0.0).astype(jnp.bfloat16)
            got = jnp.dot(ends, onehot, preferred_element_type=F32)
            picked_ref[(half * COLS + block) * 8 : (half * COLS + block + 1) * 8, :] = got
    sums = [[None] * 8 for _ in range(3)]
    for half in range(2):

        def panel(at):
            return recv_ref[pl.ds(9 + 2 * at + half, COLS, stride=SEND_ROWS), :]

        def got(at):
            return picked_ref[pl.ds(half * COLS * 8 + at, COLS, stride=8), :]

        low = got(0) + got(1) + got(2)
        high = got(3) + got(4) + got(5)
        at_panel = panel(3) * low + panel(4) * high
        section = panel(6)
        for k in range(3):
            term = panel(k) * at_panel
            for j in range(8):
                part = jnp.where(section == float(j), term, 0.0)
                part = part[0:8, :] + part[8:16, :]
                sums[k][j] = part if half == 0 else sums[k][j] + part
    terms = [
        jnp.concatenate([jnp.sum(x, axis=0, keepdims=True) for x in sums[k]], 0)
        for k in range(3)
    ]
    rows = section_rows(terms)
    for block in range(COLS):
        for k in range(3):
            at = block * BACK_ROWS + 4 + k
            back_ref[at : at + 1, :] = rows[k] + constant_ref[k : k + 1, :]
        back_ref[block * BACK_ROWS + 7 : block * BACK_ROWS + 8, :] = zero_row


def load_kernel(back_ref, load_ref):
    load_ref[...] = jnp.zeros_like(load_ref)
    for k in range(3):
        rows = back_ref[pl.ds(4 + k, COLS, stride=BACK_ROWS), :]
        load_ref[k : k + 1, :] = jnp.sum(rows, axis=0, keepdims=True)


def field_kernel(back_ref, mat_ref, offset_ref, w_ref, pressure_ref, velocity_ref):
    def end(at):
        halves = [
            back_ref[pl.ds(half * BACK_ROWS + at, CX, stride=2 * BACK_ROWS), :] for half in range(2)
        ]
        return jnp.concatenate(halves, axis=1)

    to_first = [level(mat_ref, A_AT + j) for j in range(CZ - 2)]
    to_next = [level(mat_ref, B_AT + j) for j in range(CZ - 2)]
    offsets = [level(offset_ref, j) for j in range(CZ - 2)]
    pressure = expand(end(0), end(1), to_first, to_next, offsets)
    flux = [end(2)]
    for z in range(CZ - 1):
        flux.append(level(mat_ref, FACE_AT + z) * (pressure[z + 1] - pressure[z]))
    flux.append(end(3))
    for z in range(CZ):
        pressure_ref[z * CX : (z + 1) * CX, :] = pressure[z]
        velocity_ref[z * CX : (z + 1) * CX, :] = level(w_ref, z) - 0.5 * (flux[z + 1] + flux[z])


def section_kernel(load_ref, pair_ref, other_ref, out_ref):
    even = lax.rem(lax.axis_index("slab"), 2) == 0
    received, beyond = pair_ref[...], other_ref[...]
    from_left = jnp.where(even, beyond, received)
    from_right = jnp.where(even, received, beyond)
    lanes = lane_iota((8, LANES))
    total = load_ref[...]
    total = total + jnp.where(lanes < 4, pltpu.roll(from_left, LANES - 4, 1), 0.0)
    total = total + jnp.where(lanes >= 4, pltpu.roll(from_right, 4, 1), 0.0)
    total = pltpu.roll(total, LANES - REACH, 1)
    out_ref[...] = total[0:3, 0:SEC_DEV]


def call(kernel, outs, scratch=(), flops=20000):
    shapes = [jax.ShapeDtypeStruct(shape, F32) for shape in outs]
    return pl.pallas_call(
        kernel,
        out_shape=shapes if len(shapes) > 1 else shapes[0],
        scratch_shapes=[pltpu.VMEM(shape, F32) for shape in scratch],
        compiler_params=pltpu.CompilerParams(vmem_limit_bytes=16 * 1024 * 1024),
        cost_estimate=pl.CostEstimate(flops=flops, bytes_accessed=500000, transcendentals=0),
    )


def per_device(p_star, u_star, v_star, w_star, flags, panel_cell, panel_section, panel_geom):
    flat = (CZ * CX, NY)
    p, u, v, w = (x.reshape(flat) for x in (p_star, u_star, v_star, w_star))
    flags = flags.reshape(flat)
    cell = panel_cell.reshape(1, PANELS_DEV)
    section = panel_section.reshape(1, PANELS_DEV)
    slabs = lax.axis_size("slab")
    pairs = [(i, i ^ 1) for i in range(slabs)]
    others = [(i, i + 1) for i in range(1, slabs - 1, 2)]
    others += [(j, i) for i, j in others]

    to_pair, to_other = call(edge_kernel, [(CZ, NY)] * 2)(p_star, u_star)
    from_pair = lax.ppermute(to_pair, "slab", pairs)
    from_other = lax.ppermute(to_other, "slab", others)
    mat, source, panel = call(
        matrix_kernel, [(MAT_LEVELS * CX, NY), flat, (2, PANELS_DEV)], flops=5000000
    )(p, u, v, w, flags, cell)
    send, offsets, constant = call(
        pack_kernel,
        [(COLS * SEND_ROWS, LANES), ((CZ - 2) * CX, NY), (8, LANES)],
        [(16, LANES)],
    )(mat, source, from_pair, from_other, w, panel, cell, section, panel_geom)
    recv = lax.all_to_all(send, "col", 0, 0, tiled=True)
    back = call(
        owner_kernel,
        [(COLS * BACK_ROWS, LANES)],
        [(40, LANES), (16, LANES), (COLS * 8, LANES), (2 * COLS * 8, LANES)],
    )(recv, constant)
    back = lax.all_to_all(back, "col", 0, 0, tiled=True)
    loads = call(load_kernel, [(8, LANES)])(back)
    loads_pair = lax.ppermute(loads, "slab", pairs)
    loads_other = lax.ppermute(loads, "slab", others)
    pressure, velocity = call(field_kernel, [flat, flat], flops=5000000)(back, mat, offsets, w)
    section_loads = call(section_kernel, [(3, SEC_DEV)])(loads, loads_pair, loads_other)
    return pressure.reshape(p_star.shape), velocity.reshape(p_star.shape), section_loads


def solution(mesh):
    in_specs = (
        P("col", "slab", None),
        P("col", "slab", None),
        P("col", "slab", None),
        P("col", "slab", None),
        P("col", "slab", None),
        P(("col", "slab")),
        P(("col", "slab")),
        P(None, ("col", "slab")),
    )
    out_specs = (P("col", "slab", None), P("col", "slab", None), P(None, "slab"))
    return jax.shard_map(
        per_device, mesh=mesh, in_specs=in_specs, out_specs=out_specs, check_vma=False
    )
```

time: 333 us -> 59.7 us (0.18)
  blocking collectives: 190 us -> 22.6 us
  waiting for transfers between devices: 83.9 us -> 3.98 us
  local copies, waits for them, and re-layouts: 17.7 us -> 3.89 us
  between operations: 14.4 us -> 0.74 us
  starting transfers between devices: 16.8 us -> 25 us
  other arithmetic: 6.28 us -> 0 us
    psum x1 -> x0, blocking collectives: 124 us -> none  [per_device(): totals = lax.psum(partial_loads, ('col', 'slab'))]
    all_gather x1 -> x0, waiting for transfers between devices: 76.9 us -> none  [carried_in(): everything = jax.tree.map(lambda part: lax.all_gather(part, axis), x)]
    all_gather x2 -> x0, blocking collectives: 66 us -> none  [carried_in(): everything = jax.tree.map(lambda part: lax.all_gather(part, axis), x)]
    all_to_all x0 -> x2, blocking collectives: none -> 22.6 us  [the longest x1 12.8 us: per_device(): recv = lax.all_to_all(send, 'col', 0, 0, tiled=True)]
    mul x32 -> x0, local copies, waits for them, and re-layouts: 14.5 us -> none  [the longest x16 14.3 us: matmul_three(): return jnp.sum(left_side[:, :, None] * right_side[None, :, :], axis=1)]
    ppermute x4, starting transfers between devices: 16.8 us -> 25 us  [the longest x1 11 us: per_device(): loads_other = lax.ppermute(loads, 'slab', others)]
  transfers between devices with their start and end apart: 5 -> 4, of which waited for: 2 -> 2; matrix products, arithmetic and copies ran while one was open for 1% -> 0% of each run, Pallas kernels for 0% -> 2%
where the time goes in v1:
time: 59.7 us; the launch traced here: 59.2 us
  starting transfers between devices  25 us (42%)
  blocking collectives  22.6 us (38%)
  waiting for transfers between devices  3.98 us (7%)
  local copies, waits for them, and re-layouts  3.89 us (7%)
  Pallas kernels  2.99 us (5%)
  between operations  0.74 us (1%)
    all_to_all x1, blocking collectives, per_device(): recv = lax.all_to_all(send, 'col', 0, 0, tiled=True)  12.8 us
    ppermute x1, starting transfers between devices, per_device(): loads_other = lax.ppermute(loads, 'slab', others)  11 us
    all_to_all x1, blocking collectives, per_device(): back = lax.all_to_all(back, 'col', 0, 0, tiled=True)  9.83 us
    ppermute x1, starting transfers between devices, per_device(): from_pair = lax.ppermute(to_pair, 'slab', pairs)  8.79 us
    unnamed x16, local copies, waits for them, and re-layouts  3.89 us
    ppermute x1, waiting for transfers between devices, per_device(): from_other = lax.ppermute(to_other, 'slab', others)  3.53 us
    ppermute x1, starting transfers between devices, per_device(): from_other = lax.ppermute(to_other, 'slab', others)  3.34 us
    ppermute x1, starting transfers between devices, per_device(): loads_pair = lax.ppermute(loads, 'slab', pairs)  1.92 us
  transfers between devices with their start and end apart: 4, of which 2 were waited for; matrix products, arithmetic and copies ran while one was open for 0% of the time, Pallas kernels for 2%

profile of v1, /device:TPU:1, one launch (start us, length us, event | category | flops | bytes accessed | tf_op | source)
XLA Modules:
  0.0 59.2 jit_solution(1017748014419916257)
XLA Ops:
  0.6 0.0 copy-start
  0.6 0.0 copy-start.1
  0.7 0.9 %copy-done.1 = f32[8,8,256]{2,1,0:T(8,128)S(1)} copy-done((f32[8,8,256]{2,1,0:T(8,128)S(1)}, f32[8,8,256]{2,1,0:T(8,128)}, u32[]{:S(2)}) %copy-start.1) | copy-done | bytes 65560
  1.5 0.0 copy-start.2
  1.5 0.8 %copy-done.2 = f32[8,8,256]{2,1,0:T(8,128)S(1)} copy-done((f32[8,8,256]{2,1,0:T(8,128)S(1)}, f32[8,8,256]{2,1,0:T(8,128)}, u32[]{:S(2)}) %copy-start.2) | copy-done | bytes 65560
  2.4 0.0 copy-start.3
  2.4 8.8 %collective-permute-start = (f32[8,256]{1,0:T(8,128)S(1)}, f32[8,256]{1,0:T(8,128)S(1)}, u32[]{:S(2)}, u32[]{:S(2)}) collective-permute-start(f32[8,256]{1,0:T(8,128)S(1)} %get-tuple-element.15), channel_id=1, source_target_pairs={{0,1},{1,0},{2,3},{3,2},{4,5},{5,4},{6,7},{7,6},{8,9},{9,8},{10,11... | collective-permute-start | bytes 24584 | tf_op jit(solution)/shard_map/ppermute | solution.py:411
  11.2 3.3 %collective-permute-start.1 = (f32[8,256]{1,0:T(8,128)S(1)}, f32[8,256]{1,0:T(8,128)S(1)}, u32[]{:S(2)}, u32[]{:S(2)}) collective-permute-start(f32[8,256]{1,0:T(8,128)S(1)} %get-tuple-element.16), channel_id=1, source_target_pairs={{1,2},{3,4},{5,6},{7,8},{9,10},{11,12},{13,14},{15,16},{17,18},{19... | collective-permute-start | bytes 24584 | tf_op jit(solution)/shard_map/ppermute | solution.py:412
  14.5 0.0 copy-start.6
  14.5 0.0 copy-done
  14.6 0.0 copy-done.3
  14.6 0.7 %copy-done.6 = s32[256]{0:T(256)S(1)} copy-done((s32[256]{0:T(256)S(1)}, s32[256]{0:T(256)}, u32[]{:S(2)}) %copy-start.6) | copy-done | bytes 1048
  15.2 0.0 copy-start.4
  15.2 0.8 %copy-done.4 = s32[8,8,256]{2,1,0:T(8,128)S(1)} copy-done((s32[8,8,256]{2,1,0:T(8,128)S(1)}, s32[8,8,256]{2,1,0:T(8,128)}, u32[]{:S(2)}) %copy-start.4) | copy-done | bytes 65560
  16.1 0.4 shard_map.103
  16.5 0.0 copy-start.5
  16.5 0.0 collective-permute-done.pair_ref
  16.5 3.5 %collective-permute-done.1.other_ref = f32[8,256]{1,0:T(8,128)S(1)} collective-permute-done((f32[8,256]{1,0:T(8,128)S(1)}, f32[8,256]{1,0:T(8,128)S(1)}, u32[]{:S(2)}, u32[]{:S(2)}) %collective-permute-start.1) | collective-permute-done | bytes 8224 | tf_op jit(solution)/shard_map/ppermute | solution.py:412
  20.1 0.0 copy-start.7
  20.1 0.0 copy-done.5
  20.1 0.7 %copy-done.7 = s32[256]{0:T(256)S(1)} copy-done((s32[256]{0:T(256)S(1)}, s32[256]{0:T(256)}, u32[]{:S(2)}) %copy-start.7) | copy-done | bytes 1048
  20.7 0.3 shard_map.105
  21.1 12.8 %all_to_all.22 = f32[16,24,128]{2,1,0:T(8,128)S(1)} all-to-all(f32[16,24,128]{2,1,0:T(8,128)S(1)} %bitcast.22), channel_id=1, replica_groups=mesh['col'=16,'slab'=32] {'col'}, dimensions={0} | all-to-all | bytes 393216 | tf_op jit(solution)/shard_map/all_to_all | solution.py:421
  33.8 0.8 %shard_map.106 = f32[128,128]{1,0:T(8,128)S(1)} custom-call(f32[384,128]{1,0:T(8,128)S(1)} %bitcast.13, f32[8,128]{1,0:T(8,128)S(1)} %get-tuple-element.19.constant_ref), custom_call_target="tpu_custom_call" | custom-call | flops 20000 | bytes 500000 | tf_op jit(solution)/shard_map/pallas_call | solution.py:422
  34.6 9.8 %all_to_all.23 = f32[16,8,128]{2,1,0:T(8,128)S(1)} all-to-all(f32[16,8,128]{2,1,0:T(8,128)S(1)} %bitcast.21), channel_id=1, replica_groups=mesh['col'=16,'slab'=32] {'col'}, dimensions={0} | all-to-all | bytes 131072 | tf_op jit(solution)/shard_map/all_to_all | solution.py:427
  44.5 11.0 %collective-permute-start.3 = (f32[8,128]{1,0:T(8,128)S(1)}, f32[8,128]{1,0:T(8,128)S(1)}, u32[]{:S(2)}, u32[]{:S(2)}) collective-permute-start(f32[8,128]{1,0:T(8,128)S(1)} %shard_map.108.load_ref), channel_id=1, source_target_pairs={{1,2},{3,4},{5,6},{7,8},{9,10},{11,12},{13,14},{15,16},{17,18},{19... | collective-permute-start | bytes 12296 | tf_op jit(solution)/shard_map/ppermute | solution.py:430
  55.4 1.9 %collective-permute-start.2 = (f32[8,128]{1,0:T(8,128)S(1)}, f32[8,128]{1,0:T(8,128)S(1)}, u32[]{:S(2)}, u32[]{:S(2)}) collective-permute-start(f32[8,128]{1,0:T(8,128)S(1)} %shard_map.108.load_ref), channel_id=1, source_target_pairs={{0,1},{1,0},{2,3},{3,2},{4,5},{5,4},{6,7},{7,6},{8,9},{9,8},{10,11... | collective-permute-start | bytes 12296 | tf_op jit(solution)/shard_map/ppermute | solution.py:429
  57.3 0.7 %shard_map.107 = (f32[64,256]{1,0:T(8,128)}, f32[64,256]{1,0:T(8,128)}) custom-call(f32[128,128]{1,0:T(8,128)S(1)} %bitcast.18, f32[240,256]{1,0:T(8,128)S(1)} %get-tuple-element.13.mat_ref, f32[48,256]{1,0:T(8,128)S(1)} %get-tuple-element.20.offset_ref, f32[64,256]{1,0:T(8,128)S(1)} %bitcast.16), custom_call_target="tpu_custom_call" | custom-call | flops 5000000 | bytes 500000 | tf_op jit(solution)/shard_map/pallas_call | solution.py:431
  58.0 0.0 collective-permute-done.3.other_ref
  58.0 0.4 collective-permute-done.2.pair_ref
  58.5 0.7 %shard_map.109 = f32[3,4]{1,0:T(4,128)} custom-call(f32[8,128]{1,0:T(8,128)S(1)} %shard_map.108.load_ref, f32[8,128]{1,0:T(8,128)S(1)} %collective-permute-done.2.pair_ref, f32[8,128]{1,0:T(8,128)S(1)} %collective-permute-done.3.other_ref), custom_call_target="tpu_custom_call" | custom-call | flops 20000 | bytes 500000 | tf_op jit(solution)/shard_map/pallas_call | solution.py:432
  (2 shorter events, 0.0 us)
Async XLA Ops:
  0.6 13.9 %copy-start = (f32[8,8,256]{2,1,0:T(8,128)S(1)}, f32[8,8,256]{2,1,0:T(8,128)}, u32[]{:S(2)}) copy-start(f32[8,8,256]{2,1,0:T(8,128)} %param.11) | copy-start | bytes 196612
  0.6 0.9 %copy-start.1 = (f32[8,8,256]{2,1,0:T(8,128)S(1)}, f32[8,8,256]{2,1,0:T(8,128)}, u32[]{:S(2)}) copy-start(f32[8,8,256]{2,1,0:T(8,128)} %p_ref.1) | copy-start | bytes 196612
  1.5 0.8 %copy-start.2 = (f32[8,8,256]{2,1,0:T(8,128)S(1)}, f32[8,8,256]{2,1,0:T(8,128)}, u32[]{:S(2)}) copy-start(f32[8,8,256]{2,1,0:T(8,128)} %u_ref.1) | copy-start | bytes 196612
  2.4 12.2 %copy-start.3 = (f32[8,8,256]{2,1,0:T(8,128)S(1)}, f32[8,8,256]{2,1,0:T(8,128)}, u32[]{:S(2)}) copy-start(f32[8,8,256]{2,1,0:T(8,128)} %param.10) | copy-start | bytes 196612
  2.4 14.1 %collective-permute-start = (f32[8,256]{1,0:T(8,128)S(1)}, f32[8,256]{1,0:T(8,128)S(1)}, u32[]{:S(2)}, u32[]{:S(2)}) collective-permute-start(f32[8,256]{1,0:T(8,128)S(1)} %get-tuple-element.15), channel_id=1, source_target_pairs={{0,1},{1,0},{2,3},{3,2},{4,5},{5,4},{6,7},{7,6},{8,9},{9,8},{10,11... | collective-permute-start | bytes 24584 | tf_op jit(solution)/shard_map/ppermute | solution.py:411
  11.2 8.9 %collective-permute-start.1 = (f32[8,256]{1,0:T(8,128)S(1)}, f32[8,256]{1,0:T(8,128)S(1)}, u32[]{:S(2)}, u32[]{:S(2)}) collective-permute-start(f32[8,256]{1,0:T(8,128)S(1)} %get-tuple-element.16), channel_id=1, source_target_pairs={{1,2},{3,4},{5,6},{7,8},{9,10},{11,12},{13,14},{15,16},{17,18},{19... | collective-permute-start | bytes 24584 | tf_op jit(solution)/shard_map/ppermute | solution.py:412
  14.5 0.7 %copy-start.6 = (s32[256]{0:T(256)S(1)}, s32[256]{0:T(256)}, u32[]{:S(2)}) copy-start(s32[256]{0:T(256)} %param.13) | copy-start | bytes 3076
  15.2 0.8 %copy-start.4 = (s32[8,8,256]{2,1,0:T(8,128)S(1)}, s32[8,8,256]{2,1,0:T(8,128)}, u32[]{:S(2)}) copy-start(s32[8,8,256]{2,1,0:T(8,128)} %param.12) | copy-start | bytes 196612
  16.5 3.6 %copy-start.5 = (f32[3,256]{1,0:T(4,128)S(1)}, f32[3,256]{1,0:T(4,128)}, u32[]{:S(2)}) copy-start(f32[3,256]{1,0:T(4,128)} %geom_ref.1) | copy-start | bytes 9220
  20.1 0.7 %copy-start.7 = (s32[256]{0:T(256)S(1)}, s32[256]{0:T(256)}, u32[]{:S(2)}) copy-start(s32[256]{0:T(256)} %param.14) | copy-start | bytes 3076
  44.5 13.6 %collective-permute-start.3 = (f32[8,128]{1,0:T(8,128)S(1)}, f32[8,128]{1,0:T(8,128)S(1)}, u32[]{:S(2)}, u32[]{:S(2)}) collective-permute-start(f32[8,128]{1,0:T(8,128)S(1)} %shard_map.108.load_ref), channel_id=1, source_target_pairs={{1,2},{3,4},{5,6},{7,8},{9,10},{11,12},{13,14},{15,16},{17,18},{19... | collective-permute-start | bytes 12296 | tf_op jit(solution)/shard_map/ppermute | solution.py:430
  55.4 3.1 %collective-permute-start.2 = (f32[8,128]{1,0:T(8,128)S(1)}, f32[8,128]{1,0:T(8,128)S(1)}, u32[]{:S(2)}, u32[]{:S(2)}) collective-permute-start(f32[8,128]{1,0:T(8,128)S(1)} %shard_map.108.load_ref), channel_id=1, source_target_pairs={{0,1},{1,0},{2,3},{3,2},{4,5},{5,4},{6,7},{7,6},{8,9},{9,8},{10,11... | collective-permute-start | bytes 12296 | tf_op jit(solution)/shard_map/ppermute | solution.py:429

commit v2 on v1

--- a/solution.py
+++ b/solution.py
@@ -106,23 +106,14 @@
     return rows
 
 
-def edge_kernel(p_ref, u_ref, pair_ref, other_ref):
-    even = lax.rem(lax.axis_index("slab"), 2) == 0
-
-    def plane(ref, x):
-        return ref[:, x, :]
-
-    leading = GAMMA_HORIZ * plane(p_ref, 0) - HALF_DIV * plane(u_ref, 0)
-    trailing = GAMMA_HORIZ * plane(p_ref, CX - 1) + HALF_DIV * plane(u_ref, CX - 1)
-    pair_ref[...] = jnp.where(even, trailing, leading)
-    other_ref[...] = jnp.where(even, leading, trailing)
-
-
 A_AT, B_AT, I_AT, FACE_AT, PORT_AT = 0, 6, 12, 18, 25
 MAT_LEVELS = 30
 
 
-def matrix_kernel(p_ref, u_ref, v_ref, w_ref, flags_ref, cell_ref, mat_ref, src_ref, panel_ref):
+def matrix_kernel(
+    p_ref, u_ref, v_ref, w_ref, flags_ref, cell_ref, sec_ref, geom_ref,
+    mat_ref, src_ref, panel_ref,
+):
     shape = (CX, NY)
     rows, lanes = row_iota(shape), lane_iota(shape)
     densities, kappas = [], []
@@ -176,16 +167,25 @@
     onehot, row_mask = panel_masks(cell_ref[...])
     from_first = expand(one, zero, to_first, to_next, no_offset)
     from_last = expand(zero, one, to_first, to_next, no_offset)
-    panel_ref[0:1, :] = pick(jnp.concatenate(from_first, 0), onehot, row_mask)
-    panel_ref[1:2, :] = pick(jnp.concatenate(from_last, 0), onehot, row_mask)
+    section = sec_ref[...] - (lax.axis_index("slab") * SEC_DEV - REACH)
+    column = cell_ref[...] & (CX * NY - 1)
+    panel_rows = [geom_ref[k : k + 1, :] for k in range(3)]
+    panel_rows.append(pick(jnp.concatenate(from_first, 0), onehot, row_mask))
+    panel_rows.append(pick(jnp.concatenate(from_last, 0), onehot, row_mask))
+    panel_rows += [column.astype(F32), section.astype(F32)]
+    panel_ref[...] = jnp.zeros_like(panel_ref)
+    for at, row in enumerate(panel_rows):
+        for half in range(2):
+            panel_ref[1 + 2 * at + half : 2 + 2 * at + half, :] = row[
+                :, half * LANES : (half + 1) * LANES
+            ]
 
 
 def pack_kernel(
-    mat_ref, src_ref, pair_ref, other_ref, w_ref, panel_ref, cell_ref, sec_ref, geom_ref,
-    send_ref, offset_ref, constant_ref, rows_ref,
+    mat_ref, src_ref, pair_ref, other_ref, w_ref, panel_ref, cell_ref,
+    send_ref, offset_ref, constant_ref,
 ):
-    slab = lax.axis_index("slab")
-    even = lax.rem(slab, 2) == 0
+    even = lax.rem(lax.axis_index("slab"), 2) == 0
     shape = (CX, NY)
     rows = row_iota(shape)
     received, beyond = pair_ref[...], other_ref[...]
@@ -204,20 +204,8 @@
     for j, offset in enumerate(offsets):
         offset_ref[j * CX : (j + 1) * CX, :] = offset
 
-    section = sec_ref[...] - (slab * SEC_DEV - REACH)
-    cell = cell_ref[...]
-    column = cell & (CX * NY - 1)
-    panel_rows = [geom_ref[k : k + 1, :] for k in range(3)]
-    panel_rows += [panel_ref[0:1, :], panel_ref[1:2, :]]
-    panel_rows += [column.astype(F32), section.astype(F32)]
-    rows_ref[...] = jnp.zeros_like(rows_ref)
-    for at, row in enumerate(panel_rows):
-        for half in range(2):
-            rows_ref[1 + 2 * at + half : 2 + 2 * at + half, :] = row[
-                :, half * LANES : (half + 1) * LANES
-            ]
     for owner in range(COLS):
-        send_ref[owner * SEND_ROWS + 8 : owner * SEND_ROWS + 24, :] = rows_ref[...]
+        send_ref[owner * SEND_ROWS + 8 : owner * SEND_ROWS + 24, :] = panel_ref[...]
     ports = [level(mat_ref, PORT_AT + j) for j in range(3)] + [first, last]
     ports += [level(mat_ref, PORT_AT + 3), level(mat_ref, PORT_AT + 4)]
     ports += [level(w_ref, 0), level(w_ref, CZ - 1)]
@@ -229,12 +217,15 @@
 
     zero = jnp.zeros(shape, F32)
     constant = expand(zero, zero, to_first, to_next, offsets)
-    onehot, row_mask = panel_masks(cell)
+    onehot, row_mask = panel_masks(cell_ref[...])
     at_panel = pick(jnp.concatenate(constant, 0), onehot, row_mask)
-    in_section = row_iota((8, PANELS_DEV)) == section
-    terms = [
-        jnp.where(in_section, geom_ref[k : k + 1, :] * at_panel, 0.0) for k in range(3)
-    ]
+    terms = [0.0, 0.0, 0.0]
+    for half in range(2):
+        lanes = slice(half * LANES, (half + 1) * LANES)
+        in_section = row_iota((8, LANES)).astype(F32) == panel_ref[13 + half : 14 + half, :]
+        for k in range(3):
+            row = panel_ref[1 + 2 * k + half : 2 + 2 * k + half, :] * at_panel[:, lanes]
+            terms[k] = terms[k] + jnp.where(in_section, row, 0.0)
     constant_ref[...] = jnp.zeros_like(constant_ref)
     for k, row in enumerate(section_rows(terms)):
         constant_ref[k : k + 1, :] = row
@@ -407,17 +398,20 @@
     others = [(i, i + 1) for i in range(1, slabs - 1, 2)]
     others += [(j, i) for i, j in others]
 
-    to_pair, to_other = call(edge_kernel, [(CZ, NY)] * 2)(p_star, u_star)
+    even = lax.rem(lax.axis_index("slab"), 2) == 0
+    leading = GAMMA_HORIZ * p_star[:, 0, :] - HALF_DIV * u_star[:, 0, :]
+    trailing = GAMMA_HORIZ * p_star[:, CX - 1, :] + HALF_DIV * u_star[:, CX - 1, :]
+    to_pair = jnp.where(even, trailing, leading)
+    to_other = jnp.where(even, leading, trailing)
+    from_other = lax.ppermute(to_other, "slab", others)
     from_pair = lax.ppermute(to_pair, "slab", pairs)
-    from_other = lax.ppermute(to_other, "slab", others)
     mat, source, panel = call(
-        matrix_kernel, [(MAT_LEVELS * CX, NY), flat, (2, PANELS_DEV)], flops=5000000
-    )(p, u, v, w, flags, cell)
+        matrix_kernel, [(MAT_LEVELS * CX, NY), flat, (16, LANES)], flops=5000000
+    )(p, u, v, w, flags, cell, section, panel_geom)
     send, offsets, constant = call(
         pack_kernel,
         [(COLS * SEND_ROWS, LANES), ((CZ - 2) * CX, NY), (8, LANES)],
-        [(16, LANES)],
-    )(mat, source, from_pair, from_other, w, panel, cell, section, panel_geom)
+    )(mat, source, from_pair, from_other, w, panel, cell)
     recv = lax.all_to_all(send, "col", 0, 0, tiled=True)
     back = call(
         owner_kernel,

time: 59.7 us -> 59.2 us (level)
  blocking collectives: 22.6 us -> 27.8 us
  waiting for transfers between devices: 3.98 us -> 0.45 us
  starting transfers between devices: 25 us -> 22.4 us
    ppermute x1, starting transfers between devices: 3.34 us -> 10.2 us  [per_device(): from_other = lax.ppermute(to_other, 'slab', others)]
    ppermute x1, starting transfers between devices: 8.79 us -> 1.92 us  [per_device(): from_pair = lax.ppermute(to_pair, 'slab', pairs)]
    all_to_all x1, blocking collectives: 12.8 us -> 16.6 us  [per_device(): recv = lax.all_to_all(send, 'col', 0, 0, tiled=True)]
    ppermute x1, waiting for transfers between devices: 3.53 us -> 0.01 us  [per_device(): from_other = lax.ppermute(to_other, 'slab', others)]
    ppermute x1, starting transfers between devices: 11 us -> 8.39 us  [per_device(): loads_other = lax.ppermute(loads, 'slab', others)]
    all_to_all x1, blocking collectives: 9.83 us -> 11.2 us  [per_device(): back = lax.all_to_all(back, 'col', 0, 0, tiled=True)]
    slice x0 -> x1, local copies, waits for them, and re-layouts: none -> 1 us  [per_device(): leading = GAMMA_HORIZ * p_star[:, 0, :] - HALF_DIV * u_star[:, 0, :]]
    unnamed x16, local copies, waits for them, and re-layouts: 3.89 us -> 3.19 us
  transfers between devices with their start and end apart: 4 -> 4, of which waited for: 2 -> 1; matrix products, arithmetic and copies ran while one was open for 0% -> 0% of each run, Pallas kernels for 2% -> 2%
where the time goes in v2:
time: 59.2 us; the launch traced here: 58.7 us
  blocking collectives  27.8 us (47%)
  starting transfers between devices  22.4 us (38%)
  local copies, waits for them, and re-layouts  4.19 us (7%)
  Pallas kernels  2.96 us (5%)
  between operations  0.77 us (1%)
    all_to_all x1, blocking collectives, per_device(): recv = lax.all_to_all(send, 'col', 0, 0, tiled=True)  16.6 us
    all_to_all x1, blocking collectives, per_device(): back = lax.all_to_all(back, 'col', 0, 0, tiled=True)  11.2 us
    ppermute x1, starting transfers between devices, per_device(): from_other = lax.ppermute(to_other, 'slab', others)  10.2 us
    ppermute x1, starting transfers between devices, per_device(): loads_other = lax.ppermute(loads, 'slab', others)  8.39 us
    unnamed x16, local copies, waits for them, and re-layouts  3.19 us
    ppermute x1, starting transfers between devices, per_device(): from_pair = lax.ppermute(to_pair, 'slab', pairs)  1.92 us
    ppermute x1, starting transfers between devices, per_device(): loads_pair = lax.ppermute(loads, 'slab', pairs)  1.92 us
  transfers between devices with their start and end apart: 4, of which 1 were waited for; matrix products, arithmetic and copies ran while one was open for 0% of the time, Pallas kernels for 2%

profile of v2, /device:TPU:1, one launch (start us, length us, event | category | flops | bytes accessed | tf_op | source)
XLA Modules:
  0.0 58.7 jit_solution(2683676807491488265)
XLA Ops:
  0.6 0.0 copy-start
  0.6 0.0 copy-start.1
  0.7 1.0 %fusion.2 = (f32[8,1,256]{2,1,0:T(1,128)S(1)}, f32[8,1,256]{2,1,0:T(1,128)S(1)}, f32[8,1,256]{2,1,0:T(1,128)S(1)}, f32[8,1,256]{2,1,0:T(1,128)S(1)}) fusion(f32[8,8,256]{2,1,0:T(8,128)} %param.8, f32[8,8,256]{2,1,0:T(8,128)} %param.9), kind=kLoop, calls=%fused_computation.8 | loop fusion | bytes 65536 | tf_op jit(solution)/shard_map/slice | solution.py:402
  1.7 10.2 %collective-permute-start.1 = (f32[8,256]{1,0:T(8,128)S(1)}, f32[8,256]{1,0:T(8,128)S(1)}, u32[]{:S(2)}, u32[]{:S(2)}) collective-permute-start(f32[8,256]{1,0:T(8,128)S(1)} %get-tuple-element.23), channel_id=1, source_target_pairs={{1,2},{3,4},{5,6},{7,8},{9,10},{11,12},{13,14},{15,16},{17,18},{19... | collective-permute-start | bytes 24584 | tf_op jit(solution)/shard_map/ppermute | solution.py:406
  11.9 1.9 %collective-permute-start = (f32[8,256]{1,0:T(8,128)S(1)}, f32[8,256]{1,0:T(8,128)S(1)}, u32[]{:S(2)}, u32[]{:S(2)}) collective-permute-start(f32[8,256]{1,0:T(8,128)S(1)} %get-tuple-element.24), channel_id=1, source_target_pairs={{0,1},{1,0},{2,3},{3,2},{4,5},{5,4},{6,7},{7,6},{8,9},{9,8},{10,11... | collective-permute-start | bytes 24584 | tf_op jit(solution)/shard_map/ppermute | solution.py:407
  13.8 0.0 copy-start.6
  13.8 0.0 copy-start.7
  13.8 0.0 copy-start.5
  13.9 0.0 copy-done
  13.9 0.0 copy-done.1
  13.9 0.6 %copy-done.6 = f32[3,256]{1,0:T(4,128)S(1)} copy-done((f32[3,256]{1,0:T(4,128)S(1)}, f32[3,256]{1,0:T(4,128)}, u32[]{:S(2)}) %copy-start.6) | copy-done | bytes 3096
  14.5 0.0 copy-done.7
  14.5 0.0 copy-done.5
  14.5 0.0 copy-start.2
  14.5 0.8 %copy-done.2 = f32[8,8,256]{2,1,0:T(8,128)S(1)} copy-done((f32[8,8,256]{2,1,0:T(8,128)S(1)}, f32[8,8,256]{2,1,0:T(8,128)}, u32[]{:S(2)}) %copy-start.2) | copy-done | bytes 65560
  15.4 0.0 copy-start.3
  15.4 0.8 %copy-done.3 = f32[8,8,256]{2,1,0:T(8,128)S(1)} copy-done((f32[8,8,256]{2,1,0:T(8,128)S(1)}, f32[8,8,256]{2,1,0:T(8,128)}, u32[]{:S(2)}) %copy-start.3) | copy-done | bytes 65560
  16.2 0.0 copy-start.4
  16.2 0.8 %copy-done.4 = s32[8,8,256]{2,1,0:T(8,128)S(1)} copy-done((s32[8,8,256]{2,1,0:T(8,128)S(1)}, s32[8,8,256]{2,1,0:T(8,128)}, u32[]{:S(2)}) %copy-start.4) | copy-done | bytes 65560
  17.1 0.4 shard_map.103
  17.5 0.0 collective-permute-done.1.other_ref
  17.5 0.0 collective-permute-done.pair_ref
  17.5 0.3 shard_map.104
  17.9 16.6 %all_to_all.22 = f32[16,24,128]{2,1,0:T(8,128)S(1)} all-to-all(f32[16,24,128]{2,1,0:T(8,128)S(1)} %bitcast.24), channel_id=1, replica_groups=mesh['col'=16,'slab'=32] {'col'}, dimensions={0} | all-to-all | bytes 393216 | tf_op jit(solution)/shard_map/all_to_all | solution.py:415
  34.5 0.8 %shard_map.105 = f32[128,128]{1,0:T(8,128)S(1)} custom-call(f32[384,128]{1,0:T(8,128)S(1)} %bitcast.17, f32[8,128]{1,0:T(8,128)S(1)} %get-tuple-element.15.constant_ref), custom_call_target="tpu_custom_call" | custom-call | flops 20000 | bytes 500000 | tf_op jit(solution)/shard_map/pallas_call | solution.py:416
  35.2 11.2 %all_to_all.23 = f32[16,8,128]{2,1,0:T(8,128)S(1)} all-to-all(f32[16,8,128]{2,1,0:T(8,128)S(1)} %bitcast.23), channel_id=1, replica_groups=mesh['col'=16,'slab'=32] {'col'}, dimensions={0} | all-to-all | bytes 131072 | tf_op jit(solution)/shard_map/all_to_all | solution.py:421
  46.5 8.4 %collective-permute-start.3 = (f32[8,128]{1,0:T(8,128)S(1)}, f32[8,128]{1,0:T(8,128)S(1)}, u32[]{:S(2)}, u32[]{:S(2)}) collective-permute-start(f32[8,128]{1,0:T(8,128)S(1)} %shard_map.107.load_ref), channel_id=1, source_target_pairs={{1,2},{3,4},{5,6},{7,8},{9,10},{11,12},{13,14},{15,16},{17,18},{19... | collective-permute-start | bytes 12296 | tf_op jit(solution)/shard_map/ppermute | solution.py:424
  54.9 1.9 %collective-permute-start.2 = (f32[8,128]{1,0:T(8,128)S(1)}, f32[8,128]{1,0:T(8,128)S(1)}, u32[]{:S(2)}, u32[]{:S(2)}) collective-permute-start(f32[8,128]{1,0:T(8,128)S(1)} %shard_map.107.load_ref), channel_id=1, source_target_pairs={{0,1},{1,0},{2,3},{3,2},{4,5},{5,4},{6,7},{7,6},{8,9},{9,8},{10,11... | collective-permute-start | bytes 12296 | tf_op jit(solution)/shard_map/ppermute | solution.py:423
  56.8 0.7 %shard_map.106 = (f32[64,256]{1,0:T(8,128)}, f32[64,256]{1,0:T(8,128)}) custom-call(f32[128,128]{1,0:T(8,128)S(1)} %bitcast.22, f32[240,256]{1,0:T(8,128)S(1)} %get-tuple-element.11.mat_ref, f32[48,256]{1,0:T(8,128)S(1)} %get-tuple-element.16.offset_ref, f32[64,256]{1,0:T(8,128)S(1)} %bitcast.20), custom_call_target="tpu_custom_call" | custom-call | flops 5000000 | bytes 500000 | tf_op jit(solution)/shard_map/pallas_call | solution.py:425
  57.5 0.0 collective-permute-done.3.other_ref
  57.5 0.4 collective-permute-done.2.pair_ref
  57.9 0.7 %shard_map.108 = f32[3,4]{1,0:T(4,128)} custom-call(f32[8,128]{1,0:T(8,128)S(1)} %shard_map.107.load_ref, f32[8,128]{1,0:T(8,128)S(1)} %collective-permute-done.2.pair_ref, f32[8,128]{1,0:T(8,128)S(1)} %collective-permute-done.3.other_ref), custom_call_target="tpu_custom_call" | custom-call | flops 20000 | bytes 500000 | tf_op jit(solution)/shard_map/pallas_call | solution.py:426
  (2 shorter events, 0.0 us)
Async XLA Ops:
  0.6 13.2 %copy-start = (f32[8,8,256]{2,1,0:T(8,128)S(1)}, f32[8,8,256]{2,1,0:T(8,128)}, u32[]{:S(2)}) copy-start(f32[8,8,256]{2,1,0:T(8,128)} %param.11) | copy-start | bytes 196612
  0.6 13.2 %copy-start.1 = (f32[8,8,256]{2,1,0:T(8,128)S(1)}, f32[8,8,256]{2,1,0:T(8,128)}, u32[]{:S(2)}) copy-start(f32[8,8,256]{2,1,0:T(8,128)} %param.8) | copy-start | bytes 196612
  1.7 15.8 %collective-permute-start.1 = (f32[8,256]{1,0:T(8,128)S(1)}, f32[8,256]{1,0:T(8,128)S(1)}, u32[]{:S(2)}, u32[]{:S(2)}) collective-permute-start(f32[8,256]{1,0:T(8,128)S(1)} %get-tuple-element.23), channel_id=1, source_target_pairs={{1,2},{3,4},{5,6},{7,8},{9,10},{11,12},{13,14},{15,16},{17,18},{19... | collective-permute-start | bytes 24584 | tf_op jit(solution)/shard_map/ppermute | solution.py:406
  11.9 5.6 %collective-permute-start = (f32[8,256]{1,0:T(8,128)S(1)}, f32[8,256]{1,0:T(8,128)S(1)}, u32[]{:S(2)}, u32[]{:S(2)}) collective-permute-start(f32[8,256]{1,0:T(8,128)S(1)} %get-tuple-element.24), channel_id=1, source_target_pairs={{0,1},{1,0},{2,3},{3,2},{4,5},{5,4},{6,7},{7,6},{8,9},{9,8},{10,11... | collective-permute-start | bytes 24584 | tf_op jit(solution)/shard_map/ppermute | solution.py:407
  13.8 0.7 %copy-start.6 = (f32[3,256]{1,0:T(4,128)S(1)}, f32[3,256]{1,0:T(4,128)}, u32[]{:S(2)}) copy-start(f32[3,256]{1,0:T(4,128)} %geom_ref.1) | copy-start | bytes 9220
  13.8 0.7 %copy-start.7 = (s32[256]{0:T(256)S(1)}, s32[256]{0:T(256)}, u32[]{:S(2)}) copy-start(s32[256]{0:T(256)} %param.14) | copy-start | bytes 3076
  13.8 0.7 %copy-start.5 = (s32[256]{0:T(256)S(1)}, s32[256]{0:T(256)}, u32[]{:S(2)}) copy-start(s32[256]{0:T(256)} %param.13) | copy-start | bytes 3076
  14.5 0.8 %copy-start.2 = (f32[8,8,256]{2,1,0:T(8,128)S(1)}, f32[8,8,256]{2,1,0:T(8,128)}, u32[]{:S(2)}) copy-start(f32[8,8,256]{2,1,0:T(8,128)} %param.9) | copy-start | bytes 196612
  15.4 0.8 %copy-start.3 = (f32[8,8,256]{2,1,0:T(8,128)S(1)}, f32[8,8,256]{2,1,0:T(8,128)}, u32[]{:S(2)}) copy-start(f32[8,8,256]{2,1,0:T(8,128)} %param.10) | copy-start | bytes 196612
  16.2 0.8 %copy-start.4 = (s32[8,8,256]{2,1,0:T(8,128)S(1)}, s32[8,8,256]{2,1,0:T(8,128)}, u32[]{:S(2)}) copy-start(s32[8,8,256]{2,1,0:T(8,128)} %param.12) | copy-start | bytes 196612
  46.5 11.0 %collective-permute-start.3 = (f32[8,128]{1,0:T(8,128)S(1)}, f32[8,128]{1,0:T(8,128)S(1)}, u32[]{:S(2)}, u32[]{:S(2)}) collective-permute-start(f32[8,128]{1,0:T(8,128)S(1)} %shard_map.107.load_ref), channel_id=1, source_target_pairs={{1,2},{3,4},{5,6},{7,8},{9,10},{11,12},{13,14},{15,16},{17,18},{19... | collective-permute-start | bytes 12296 | tf_op jit(solution)/shard_map/ppermute | solution.py:424
  54.9 3.1 %collective-permute-start.2 = (f32[8,128]{1,0:T(8,128)S(1)}, f32[8,128]{1,0:T(8,128)S(1)}, u32[]{:S(2)}, u32[]{:S(2)}) collective-permute-start(f32[8,128]{1,0:T(8,128)S(1)} %shard_map.107.load_ref), channel_id=1, source_target_pairs={{0,1},{1,0},{2,3},{3,2},{4,5},{5,4},{6,7},{7,6},{8,9},{9,8},{10,11... | collective-permute-start | bytes 12296 | tf_op jit(solution)/shard_map/ppermute | solution.py:423

commit v3 on v2

--- a/solution.py
+++ b/solution.py
@@ -106,14 +106,28 @@
     return rows
 
 
+def choose_kernel(leading_ref, trailing_ref, plane_ref):
+    even = lax.rem(lax.axis_index("slab"), 2) == 0
+    for z in range(CZ):
+        plane_ref[z : z + 1, :] = jnp.where(even, leading_ref[z], trailing_ref[z])
+
+
 A_AT, B_AT, I_AT, FACE_AT, PORT_AT = 0, 6, 12, 18, 25
 MAT_LEVELS = 30
 
 
 def matrix_kernel(
     p_ref, u_ref, v_ref, w_ref, flags_ref, cell_ref, sec_ref, geom_ref,
-    mat_ref, src_ref, panel_ref,
+    mat_ref, src_ref, panel_ref, plane_ref,
 ):
+    even = lax.rem(lax.axis_index("slab"), 2) == 0
+    for z in range(CZ):
+        p, u = level(p_ref, z), level(u_ref, z)
+        plane_ref[z : z + 1, :] = jnp.where(
+            even,
+            GAMMA_HORIZ * p[CX - 1 :, :] + HALF_DIV * u[CX - 1 :, :],
+            GAMMA_HORIZ * p[:1, :] - HALF_DIV * u[:1, :],
+        )
     shape = (CX, NY)
     rows, lanes = row_iota(shape), lane_iota(shape)
     densities, kappas = [], []
@@ -398,16 +412,14 @@
     others = [(i, i + 1) for i in range(1, slabs - 1, 2)]
     others += [(j, i) for i, j in others]
 
-    even = lax.rem(lax.axis_index("slab"), 2) == 0
-    leading = GAMMA_HORIZ * p_star[:, 0, :] - HALF_DIV * u_star[:, 0, :]
-    trailing = GAMMA_HORIZ * p_star[:, CX - 1, :] + HALF_DIV * u_star[:, CX - 1, :]
-    to_pair = jnp.where(even, trailing, leading)
-    to_other = jnp.where(even, leading, trailing)
+    leading = GAMMA_HORIZ * p_star[:, :1, :] - HALF_DIV * u_star[:, :1, :]
+    trailing = GAMMA_HORIZ * p_star[:, CX - 1 :, :] + HALF_DIV * u_star[:, CX - 1 :, :]
+    to_other = call(choose_kernel, [(CZ, NY)], flops=2000000000)(leading, trailing)
     from_other = lax.ppermute(to_other, "slab", others)
-    from_pair = lax.ppermute(to_pair, "slab", pairs)
-    mat, source, panel = call(
-        matrix_kernel, [(MAT_LEVELS * CX, NY), flat, (16, LANES)], flops=5000000
+    mat, source, panel, plane = call(
+        matrix_kernel, [(MAT_LEVELS * CX, NY), flat, (16, LANES), (CZ, NY)], flops=5000000
     )(p, u, v, w, flags, cell, section, panel_geom)
+    from_pair = lax.ppermute(plane, "slab", pairs)
     send, offsets, constant = call(
         pack_kernel,
         [(COLS * SEND_ROWS, LANES), ((CZ - 2) * CX, NY), (8, LANES)],
@@ -420,8 +432,8 @@
     )(recv, constant)
     back = lax.all_to_all(back, "col", 0, 0, tiled=True)
     loads = call(load_kernel, [(8, LANES)])(back)
+    loads_other = lax.ppermute(loads, "slab", others)
     loads_pair = lax.ppermute(loads, "slab", pairs)
-    loads_other = lax.ppermute(loads, "slab", others)
     pressure, velocity = call(field_kernel, [flat, flat], flops=5000000)(back, mat, offsets, w)
     section_loads = call(section_kernel, [(3, SEC_DEV)])(loads, loads_pair, loads_other)
     return pressure.reshape(p_star.shape), velocity.reshape(p_star.shape), section_loads

time: 59.2 us -> 57.8 us (0.976)
  local copies, waits for them, and re-layouts: 4.19 us -> 0.66 us
  waiting for transfers between devices: 0.45 us -> 1.58 us
  other arithmetic: 0.01 us -> 0.97 us
    unnamed x16, local copies, waits for them, and re-layouts: 3.19 us -> 0.66 us
    ppermute x1, waiting for transfers between devices: 0.01 us -> 1.13 us  [per_device(): from_pair = lax.ppermute(plane, 'slab', pairs)]
    slice x1 -> x0, local copies, waits for them, and re-layouts: 1 us -> none  [per_device(): leading = GAMMA_HORIZ * p_star[:, 0, :] - HALF_DIV * u_star[:, 0, :]]
    add x0 -> x1, other arithmetic: none -> 0.97 us  [per_device(): GAMMA_HORIZ * p_star[:, CX - 1:, :] + HALF_DIV * u_star[:, CX - 1:, :]]
  transfers between devices with their start and end apart: 4 -> 4, of which waited for: 1 -> 2; matrix products, arithmetic and copies ran while one was open for 0% -> 0% of each run, Pallas kernels for 2% -> 2%
where the time goes in v3:
time: 57.8 us; the launch traced here: 57.4 us
  blocking collectives  27.9 us (48%)
  starting transfers between devices  22.5 us (39%)
  Pallas kernels  2.97 us (5%)
  waiting for transfers between devices  1.58 us (3%)
  other arithmetic  0.97 us (2%)
  between operations  0.81 us (1%)
  local copies, waits for them, and re-layouts  0.66 us (1%)
    all_to_all x1, blocking collectives, per_device(): recv = lax.all_to_all(send, 'col', 0, 0, tiled=True)  17 us
    all_to_all x1, blocking collectives, per_device(): back = lax.all_to_all(back, 'col', 0, 0, tiled=True)  10.9 us
    ppermute x1, starting transfers between devices, per_device(): from_other = lax.ppermute(to_other, 'slab', others)  10.3 us
    ppermute x1, starting transfers between devices, per_device(): loads_other = lax.ppermute(loads, 'slab', others)  8.33 us
    ppermute x1, starting transfers between devices, per_device(): from_pair = lax.ppermute(plane, 'slab', pairs)  1.92 us
    ppermute x1, starting transfers between devices, per_device(): loads_pair = lax.ppermute(loads, 'slab', pairs)  1.92 us
  transfers between devices with their start and end apart: 4, of which 2 were waited for; matrix products, arithmetic and copies ran while one was open for 0% of the time, Pallas kernels for 2%

profile of v3, /device:TPU:1, one launch (start us, length us, event | category | flops | bytes accessed | tf_op | source)
XLA Modules:
  0.0 57.4 jit_solution(2710962633402465324)
XLA Ops:
  0.6 1.0 %multiply_add_fusion = (f32[8,1,256]{2,1,0:T(1,128)S(1)}, f32[8,1,256]{2,1,0:T(1,128)S(1)}) fusion(f32[8,8,256]{2,1,0:T(8,128)} %param.9, f32[8,8,256]{2,1,0:T(8,128)} %param.8), kind=kLoop, calls=%fused_computation | loop fusion | flops 12288 | bytes 49152 | tf_op jit(solution)/shard_map/add | solution.py:416
  1.6 0.0 copy-start
  1.6 0.0 copy-start.1
  1.6 0.0 copy-start.2
  1.6 0.0 copy-start.3
  1.6 0.0 copy-start.4
  1.7 0.0 copy-start.7
  1.7 10.3 %collective-permute-start.1 = (f32[8,256]{1,0:T(8,128)S(1)}, f32[8,256]{1,0:T(8,128)S(1)}, u32[]{:S(2)}, u32[]{:S(2)}) collective-permute-start(f32[8,256]{1,0:T(8,128)S(1)} %shard_map.104), channel_id=1, source_target_pairs={{1,2},{3,4},{5,6},{7,8},{9,10},{11,12},{13,14},{15,16},{17,18},{19... | collective-permute-start | bytes 24584 | tf_op jit(solution)/shard_map/ppermute | solution.py:418
  12.0 0.0 copy-start.6
  12.1 0.0 copy-start.5
  12.1 0.0 copy-done
  12.1 0.0 copy-done.1
  12.1 0.0 copy-done.2
  12.1 0.0 copy-done.3
  12.1 0.0 copy-done.4
  12.1 0.0 copy-done.7
  12.1 0.6 %copy-done.6 = f32[3,256]{1,0:T(4,128)S(1)} copy-done((f32[3,256]{1,0:T(4,128)S(1)}, f32[3,256]{1,0:T(4,128)}, u32[]{:S(2)}) %copy-start.6) | copy-done | bytes 3096
  12.7 0.0 copy-done.5
  12.7 0.4 shard_map.103
  13.2 1.9 %collective-permute-start = (f32[8,256]{1,0:T(8,128)S(1)}, f32[8,256]{1,0:T(8,128)S(1)}, u32[]{:S(2)}, u32[]{:S(2)}) collective-permute-start(f32[8,256]{1,0:T(8,128)S(1)} %get-tuple-element.14), channel_id=1, source_target_pairs={{0,1},{1,0},{2,3},{3,2},{4,5},{5,4},{6,7},{7,6},{8,9},{9,8},{10,11... | collective-permute-start | bytes 24584 | tf_op jit(solution)/shard_map/ppermute | solution.py:422
  15.1 0.0 collective-permute-done.1.other_ref
  15.1 1.1 %collective-permute-done.pair_ref = f32[8,256]{1,0:T(8,128)S(1)} collective-permute-done((f32[8,256]{1,0:T(8,128)S(1)}, f32[8,256]{1,0:T(8,128)S(1)}, u32[]{:S(2)}, u32[]{:S(2)}) %collective-permute-start) | collective-permute-done | bytes 8224 | tf_op jit(solution)/shard_map/ppermute | solution.py:422
  16.3 0.3 shard_map.105
  16.6 17.0 %all_to_all.22 = f32[16,24,128]{2,1,0:T(8,128)S(1)} all-to-all(f32[16,24,128]{2,1,0:T(8,128)S(1)} %bitcast.20), channel_id=1, replica_groups=mesh['col'=16,'slab'=32] {'col'}, dimensions={0} | all-to-all | bytes 393216 | tf_op jit(solution)/shard_map/all_to_all | solution.py:427
  33.6 0.8 %shard_map.106 = f32[128,128]{1,0:T(8,128)S(1)} custom-call(f32[384,128]{1,0:T(8,128)S(1)} %bitcast.13, f32[8,128]{1,0:T(8,128)S(1)} %get-tuple-element.17.constant_ref), custom_call_target="tpu_custom_call" | custom-call | flops 20000 | bytes 500000 | tf_op jit(solution)/shard_map/pallas_call | solution.py:428
  34.3 10.9 %all_to_all.23 = f32[16,8,128]{2,1,0:T(8,128)S(1)} all-to-all(f32[16,8,128]{2,1,0:T(8,128)S(1)} %bitcast.19), channel_id=1, replica_groups=mesh['col'=16,'slab'=32] {'col'}, dimensions={0} | all-to-all | bytes 131072 | tf_op jit(solution)/shard_map/all_to_all | solution.py:433
  45.3 8.3 %collective-permute-start.3 = (f32[8,128]{1,0:T(8,128)S(1)}, f32[8,128]{1,0:T(8,128)S(1)}, u32[]{:S(2)}, u32[]{:S(2)}) collective-permute-start(f32[8,128]{1,0:T(8,128)S(1)} %shard_map.108.load_ref), channel_id=1, source_target_pairs={{1,2},{3,4},{5,6},{7,8},{9,10},{11,12},{13,14},{15,16},{17,18},{19... | collective-permute-start | bytes 12296 | tf_op jit(solution)/shard_map/ppermute | solution.py:435
  53.6 1.9 %collective-permute-start.2 = (f32[8,128]{1,0:T(8,128)S(1)}, f32[8,128]{1,0:T(8,128)S(1)}, u32[]{:S(2)}, u32[]{:S(2)}) collective-permute-start(f32[8,128]{1,0:T(8,128)S(1)} %shard_map.108.load_ref), channel_id=1, source_target_pairs={{0,1},{1,0},{2,3},{3,2},{4,5},{5,4},{6,7},{7,6},{8,9},{9,8},{10,11... | collective-permute-start | bytes 12296 | tf_op jit(solution)/shard_map/ppermute | solution.py:436
  55.5 0.7 %shard_map.107 = (f32[64,256]{1,0:T(8,128)}, f32[64,256]{1,0:T(8,128)}) custom-call(f32[128,128]{1,0:T(8,128)S(1)} %bitcast.18, f32[240,256]{1,0:T(8,128)S(1)} %get-tuple-element.12.mat_ref, f32[48,256]{1,0:T(8,128)S(1)} %get-tuple-element.18.offset_ref, f32[64,256]{1,0:T(8,128)S(1)} %bitcast.16), custom_call_target="tpu_custom_call" | custom-call | flops 5000000 | bytes 500000 | tf_op jit(solution)/shard_map/pallas_call | solution.py:437
  56.2 0.0 collective-permute-done.3.other_ref
  56.2 0.4 collective-permute-done.2.pair_ref
  56.7 0.7 %shard_map.109 = f32[3,4]{1,0:T(4,128)} custom-call(f32[8,128]{1,0:T(8,128)S(1)} %shard_map.108.load_ref, f32[8,128]{1,0:T(8,128)S(1)} %collective-permute-done.2.pair_ref, f32[8,128]{1,0:T(8,128)S(1)} %collective-permute-done.3.other_ref), custom_call_target="tpu_custom_call" | custom-call | flops 20000 | bytes 500000 | tf_op jit(solution)/shard_map/pallas_call | solution.py:438
  (2 shorter events, 0.0 us)
Async XLA Ops:
  1.6 10.5 %copy-start = (f32[8,8,256]{2,1,0:T(8,128)S(1)}, f32[8,8,256]{2,1,0:T(8,128)}, u32[]{:S(2)}) copy-start(f32[8,8,256]{2,1,0:T(8,128)} %param.11) | copy-start | bytes 196612
  1.6 10.5 %copy-start.1 = (f32[8,8,256]{2,1,0:T(8,128)S(1)}, f32[8,8,256]{2,1,0:T(8,128)}, u32[]{:S(2)}) copy-start(f32[8,8,256]{2,1,0:T(8,128)} %param.8) | copy-start | bytes 196612
  1.6 10.5 %copy-start.2 = (f32[8,8,256]{2,1,0:T(8,128)S(1)}, f32[8,8,256]{2,1,0:T(8,128)}, u32[]{:S(2)}) copy-start(f32[8,8,256]{2,1,0:T(8,128)} %param.9) | copy-start | bytes 196612
  1.6 10.5 %copy-start.3 = (f32[8,8,256]{2,1,0:T(8,128)S(1)}, f32[8,8,256]{2,1,0:T(8,128)}, u32[]{:S(2)}) copy-start(f32[8,8,256]{2,1,0:T(8,128)} %param.10) | copy-start | bytes 196612
  1.6 10.5 %copy-start.4 = (s32[8,8,256]{2,1,0:T(8,128)S(1)}, s32[8,8,256]{2,1,0:T(8,128)}, u32[]{:S(2)}) copy-start(s32[8,8,256]{2,1,0:T(8,128)} %param.12) | copy-start | bytes 196612
  1.7 10.5 %copy-start.7 = (s32[256]{0:T(256)S(1)}, s32[256]{0:T(256)}, u32[]{:S(2)}) copy-start(s32[256]{0:T(256)} %param.14) | copy-start | bytes 3076
  1.7 13.4 %collective-permute-start.1 = (f32[8,256]{1,0:T(8,128)S(1)}, f32[8,256]{1,0:T(8,128)S(1)}, u32[]{:S(2)}, u32[]{:S(2)}) collective-permute-start(f32[8,256]{1,0:T(8,128)S(1)} %shard_map.104), channel_id=1, source_target_pairs={{1,2},{3,4},{5,6},{7,8},{9,10},{11,12},{13,14},{15,16},{17,18},{19... | collective-permute-start | bytes 24584 | tf_op jit(solution)/shard_map/ppermute | solution.py:418
  12.0 0.7 %copy-start.6 = (f32[3,256]{1,0:T(4,128)S(1)}, f32[3,256]{1,0:T(4,128)}, u32[]{:S(2)}) copy-start(f32[3,256]{1,0:T(4,128)} %geom_ref.1) | copy-start | bytes 9220
  12.1 0.7 %copy-start.5 = (s32[256]{0:T(256)S(1)}, s32[256]{0:T(256)}, u32[]{:S(2)}) copy-start(s32[256]{0:T(256)} %param.13) | copy-start | bytes 3076
  13.2 3.1 %collective-permute-start = (f32[8,256]{1,0:T(8,128)S(1)}, f32[8,256]{1,0:T(8,128)S(1)}, u32[]{:S(2)}, u32[]{:S(2)}) collective-permute-start(f32[8,256]{1,0:T(8,128)S(1)} %get-tuple-element.14), channel_id=1, source_target_pairs={{0,1},{1,0},{2,3},{3,2},{4,5},{5,4},{6,7},{7,6},{8,9},{9,8},{10,11... | collective-permute-start | bytes 24584 | tf_op jit(solution)/shard_map/ppermute | solution.py:422
  45.3 11.0 %collective-permute-start.3 = (f32[8,128]{1,0:T(8,128)S(1)}, f32[8,128]{1,0:T(8,128)S(1)}, u32[]{:S(2)}, u32[]{:S(2)}) collective-permute-start(f32[8,128]{1,0:T(8,128)S(1)} %shard_map.108.load_ref), channel_id=1, source_target_pairs={{1,2},{3,4},{5,6},{7,8},{9,10},{11,12},{13,14},{15,16},{17,18},{19... | collective-permute-start | bytes 12296 | tf_op jit(solution)/shard_map/ppermute | solution.py:435
  53.6 3.1 %collective-permute-start.2 = (f32[8,128]{1,0:T(8,128)S(1)}, f32[8,128]{1,0:T(8,128)S(1)}, u32[]{:S(2)}, u32[]{:S(2)}) collective-permute-start(f32[8,128]{1,0:T(8,128)S(1)} %shard_map.108.load_ref), channel_id=1, source_target_pairs={{0,1},{1,0},{2,3},{3,2},{4,5},{5,4},{6,7},{7,6},{8,9},{9,8},{10,11... | collective-permute-start | bytes 12296 | tf_op jit(solution)/shard_map/ppermute | solution.py:436

commit v4 on v3

--- a/solution.py
+++ b/solution.py
@@ -22,8 +22,10 @@
 COLS = 16
 PANELS_DEV = 256
 REACH = 2
-SEND_ROWS = 24
-BACK_ROWS = 8
+OWNERS = 8
+SEND_ROWS = 32
+BACK_ROWS = 16
+GEOM_ROW, FIRST_ROW, LAST_ROW, COLUMN_ROW, META_ROW = 18, 24, 26, 28, 30
 
 F32 = jnp.float32
 
@@ -97,13 +99,28 @@
     return values[::-1]
 
 
+def to_row(column):
+    on_diagonal = row_iota((8, LANES)) == lane_iota((8, LANES))
+    return jnp.sum(jnp.where(on_diagonal, column, 0.0), axis=0, keepdims=True)
+
+
 def section_rows(terms):
-    rows = []
-    for term in terms:
-        sums = jnp.sum(term, axis=1, keepdims=True)
-        on_diagonal = row_iota((8, LANES)) == lane_iota((8, LANES))
-        rows.append(jnp.sum(jnp.where(on_diagonal, sums, 0.0), axis=0, keepdims=True))
-    return rows
+    return [to_row(jnp.sum(term, axis=1, keepdims=True)) for term in terms]
+
+
+def sort_panels(section, rows):
+    square = (PANELS_DEV, PANELS_DEV)
+    key = section * PANELS_DEV + lane_iota((1, PANELS_DEV))
+    key = key.astype(F32)
+    on_diagonal = row_iota(square) == lane_iota(square)
+    key_column = jnp.sum(jnp.where(on_diagonal, key, 0.0), axis=1, keepdims=True)
+    rank = jnp.sum(jnp.where(key < key_column, 1.0, 0.0), axis=1, keepdims=True)
+    order = jnp.where(lane_iota(square).astype(F32) == rank, 1.0, 0.0).astype(jnp.bfloat16)
+    total = None
+    for part in split_three(rows):
+        term = jnp.dot(part, order, preferred_element_type=F32)
+        total = term if total is None else total + term
+    return total
 
 
 def choose_kernel(leading_ref, trailing_ref, plane_ref):
@@ -118,7 +135,7 @@
 
 def matrix_kernel(
     p_ref, u_ref, v_ref, w_ref, flags_ref, cell_ref, sec_ref, geom_ref,
-    mat_ref, src_ref, panel_ref, plane_ref,
+    mat_ref, src_ref, panel_ref, bound_ref, sorted_ref, plane_ref,
 ):
     even = lax.rem(lax.axis_index("slab"), 2) == 0
     for z in range(CZ):
@@ -178,26 +195,36 @@
 
     zero, one = jnp.zeros(shape, F32), jnp.ones(shape, F32)
     no_offset = [zero] * (CZ - 2)
-    onehot, row_mask = panel_masks(cell_ref[...])
+    section = sec_ref[...] - (lax.axis_index("slab") * SEC_DEV - REACH)
+    rows = [geom_ref[k : k + 1, :] for k in range(3)] + [cell_ref[...].astype(F32)]
+    rows = sort_panels(section, jnp.concatenate(rows + [jnp.zeros((4, PANELS_DEV), F32)], 0))
+    sorted_ref[...] = rows
+    at_section = row_iota((8, PANELS_DEV))
+    starts = jnp.sum(jnp.where(section < at_section, 1.0, 0.0), axis=1, keepdims=True)
+    stops = jnp.sum(jnp.where(section <= at_section, 1.0, 0.0), axis=1, keepdims=True)
+    bound_ref[0:8, :] = jnp.broadcast_to(starts, (8, LANES))
+    bound_ref[8:16, :] = jnp.broadcast_to(stops, (8, LANES))
+
+    cell = rows[3:4, :].astype(jnp.int32)
+    onehot, row_mask = panel_masks(cell)
     from_first = expand(one, zero, to_first, to_next, no_offset)
     from_last = expand(zero, one, to_first, to_next, no_offset)
-    section = sec_ref[...] - (lax.axis_index("slab") * SEC_DEV - REACH)
-    column = cell_ref[...] & (CX * NY - 1)
-    panel_rows = [geom_ref[k : k + 1, :] for k in range(3)]
+    panel_rows = [rows[k : k + 1, :] for k in range(3)]
     panel_rows.append(pick(jnp.concatenate(from_first, 0), onehot, row_mask))
     panel_rows.append(pick(jnp.concatenate(from_last, 0), onehot, row_mask))
-    panel_rows += [column.astype(F32), section.astype(F32)]
+    panel_rows.append((cell & (CX * NY - 1)).astype(F32))
     panel_ref[...] = jnp.zeros_like(panel_ref)
     for at, row in enumerate(panel_rows):
         for half in range(2):
-            panel_ref[1 + 2 * at + half : 2 + 2 * at + half, :] = row[
+            panel_ref[2 + 2 * at + half : 3 + 2 * at + half, :] = row[
                 :, half * LANES : (half + 1) * LANES
             ]
+    panel_ref[META_ROW - 16 : META_ROW - 15, :] = to_row(starts)
 
 
 def pack_kernel(
-    mat_ref, src_ref, pair_ref, other_ref, w_ref, panel_ref, cell_ref,
-    send_ref, offset_ref, constant_ref,
+    mat_ref, src_ref, pair_ref, other_ref, w_ref, panel_ref, bound_ref, sorted_ref,
+    send_ref, offset_ref,
 ):
     even = lax.rem(lax.axis_index("slab"), 2) == 0
     shape = (CX, NY)
@@ -218,36 +245,43 @@
     for j, offset in enumerate(offsets):
         offset_ref[j * CX : (j + 1) * CX, :] = offset
 
-    for owner in range(COLS):
-        send_ref[owner * SEND_ROWS + 8 : owner * SEND_ROWS + 24, :] = panel_ref[...]
+    zero = jnp.zeros(shape, F32)
+    constant = expand(zero, zero, to_first, to_next, offsets)
+    onehot, row_mask = panel_masks(sorted_ref[3:4, :].astype(jnp.int32))
+    at_panel = pick(jnp.concatenate(constant, 0), onehot, row_mask)
+    terms = [0.0, 0.0, 0.0]
+    for half in range(2):
+        lanes = slice(half * LANES, (half + 1) * LANES)
+        place = (lane_iota((8, LANES)) + half * LANES).astype(F32)
+        in_section = (place >= bound_ref[0:8, :]) & (place < bound_ref[8:16, :])
+        for k in range(3):
+            row = sorted_ref[k : k + 1, lanes] * at_panel[:, lanes]
+            terms[k] = terms[k] + jnp.where(in_section, row, 0.0)
+    meta = panel_ref[META_ROW - 16 : META_ROW - 15, :]
+    for k, row in enumerate(section_rows(terms)):
+        meta = meta + pltpu.roll(row, 8 * (k + 1), 1)
+
+    for device in range(COLS):
+        send_ref[device * SEND_ROWS + 16 : (device + 1) * SEND_ROWS, :] = panel_ref[...]
+    for device in range(COLS):
+        at = device * SEND_ROWS + META_ROW
+        send_ref[at : at + 1, :] = meta
     ports = [level(mat_ref, PORT_AT + j) for j in range(3)] + [first, last]
     ports += [level(mat_ref, PORT_AT + 3), level(mat_ref, PORT_AT + 4)]
     ports += [level(w_ref, 0), level(w_ref, CZ - 1)]
     for at, value in enumerate(ports):
         for half in range(2):
-            send_ref[pl.ds(half * SEND_ROWS + at, CX, stride=2 * SEND_ROWS), :] = value[
-                :, half * LANES : (half + 1) * LANES
-            ]
-
-    zero = jnp.zeros(shape, F32)
-    constant = expand(zero, zero, to_first, to_next, offsets)
-    onehot, row_mask = panel_masks(cell_ref[...])
-    at_panel = pick(jnp.concatenate(constant, 0), onehot, row_mask)
-    terms = [0.0, 0.0, 0.0]
-    for half in range(2):
-        lanes = slice(half * LANES, (half + 1) * LANES)
-        in_section = row_iota((8, LANES)).astype(F32) == panel_ref[13 + half : 14 + half, :]
-        for k in range(3):
-            row = panel_ref[1 + 2 * k + half : 2 + 2 * k + half, :] * at_panel[:, lanes]
-            terms[k] = terms[k] + jnp.where(in_section, row, 0.0)
-    constant_ref[...] = jnp.zeros_like(constant_ref)
-    for k, row in enumerate(section_rows(terms)):
-        constant_ref[k : k + 1, :] = row
-
-
-def owner_kernel(recv_ref, constant_ref, back_ref, group_ref, ends_ref, parts_ref, picked_ref):
+            row = half * 8 + at if at < 8 else 16 + half
+            for group in range(0, COLS, OWNERS):
+                send_ref[pl.ds(group * SEND_ROWS + row, OWNERS, stride=SEND_ROWS), :] = value[
+                    :, half * LANES : (half + 1) * LANES
+                ]
+
+
+def solve_columns(half, recv_ref, group_ref, ends_ref, all_ref, parts_ref):
     def value(at, x):
-        return recv_ref[pl.ds(x * SEND_ROWS + at, 4, stride=4 * SEND_ROWS), :]
+        row = half * 8 + at if at < 8 else 16 + half
+        return recv_ref[pl.ds(x * SEND_ROWS + row, 4, stride=4 * SEND_ROWS), :]
 
     per = [[value(at, x) for x in range(4)] for at in range(9)]
     low_k, high_k, link, low_r, high_r, low_d, high_d, low_w, high_w = per
@@ -265,8 +299,8 @@
 
     stored = [first, last, across, first_r, last_r, low_d[0], high_d[3], low_w[0], high_w[3]]
     for at, x in enumerate(stored):
-        group_ref[at * 4 : (at + 1) * 4, :] = x
-    per = [[group_ref[at * 4 + z : at * 4 + z + 1, :] for z in range(4)] for at in range(9)]
+        group_ref[half, at * 4 : (at + 1) * 4, :] = x
+    per = [[group_ref[half, at * 4 + z : at * 4 + z + 1, :] for z in range(4)] for at in range(9)]
     low_k, high_k, link, low_r, high_r, low_d, high_d, low_w, high_w = per
     outer = [2.0 / (high_d[z] + low_d[z + 1]) for z in range(3)]
     for z in range(3):
@@ -286,82 +320,107 @@
     zero_row = jnp.zeros((1, LANES), F32)
     flux = [outer[z] * (nodes[2 * z + 2] - nodes[2 * z + 1]) for z in range(3)]
     for z in range(4):
-        ends_ref[z : z + 1, :] = nodes[2 * z]
-        ends_ref[4 + z : 5 + z, :] = nodes[2 * z + 1]
-        ends_ref[8 + z : 9 + z, :] = flux[z - 1] if z > 0 else zero_row
-        ends_ref[12 + z : 13 + z, :] = flux[z] if z < 3 else zero_row
-
-    nodes = expand(ends_ref[0:4, :], ends_ref[4:8, :], to_first, to_next, offsets)
+        ends_ref[half, z : z + 1, :] = nodes[2 * z]
+        ends_ref[half, 4 + z : 5 + z, :] = nodes[2 * z + 1]
+        ends_ref[half, 8 + z : 9 + z, :] = flux[z - 1] if z > 0 else zero_row
+        ends_ref[half, 12 + z : 13 + z, :] = flux[z] if z < 3 else zero_row
+
+    nodes = expand(ends_ref[half, 0:4, :], ends_ref[half, 4:8, :], to_first, to_next, offsets)
     inner = [join[x] * (nodes[2 * x + 2] - nodes[2 * x + 1]) for x in range(3)]
-    below = [ends_ref[8:12, :]] + inner
-    above = inner + [ends_ref[12:16, :]]
+    below = [ends_ref[half, 8:12, :]] + inner
+    above = inner + [ends_ref[half, 12:16, :]]
 
     def put(ref, rows, at, x, what):
         ref[pl.ds(x * rows + at, 4, stride=4 * rows), :] = what
 
     for x in range(4):
-        put(back_ref, BACK_ROWS, 0, x, nodes[2 * x])
-        put(back_ref, BACK_ROWS, 1, x, nodes[2 * x + 1])
-        put(back_ref, BACK_ROWS, 2, x, below[x])
-        put(back_ref, BACK_ROWS, 3, x, above[x])
+        for at, what in enumerate([nodes[2 * x], nodes[2 * x + 1], below[x], above[x]]):
+            put(all_ref, BACK_ROWS, half * 4 + at, x, what)
         for end in range(2):
             for at, part in enumerate(split_three(nodes[2 * x + end])):
-                put(parts_ref, 8, 3 * end + at, x, part.astype(F32))
-            put(parts_ref, 8, 6 + end, x, jnp.zeros((4, LANES), F32))
-
-    mine = lax.axis_index("col") * LANES
-    want = (row_iota((LANES, LANES)) + mine).astype(F32)
+                put(parts_ref, 16, half * 8 + 3 * end + at, x, part.astype(F32))
+            put(parts_ref, 16, half * 8 + 6 + end, x, jnp.zeros((4, LANES), F32))
+
+
+def owner_kernel(
+    recv_ref, back_ref, group_ref, ends_ref, all_ref, parts_ref, place_ref, picked_ref
+):
+    for half in range(2):
+        solve_columns(half, recv_ref, group_ref, ends_ref, all_ref, parts_ref)
+
+    column_device = lax.axis_index("col")
+    mine = lax.rem(column_device, OWNERS) * NY
+
+    def panel(row):
+        return recv_ref[pl.ds(row, COLS, stride=SEND_ROWS), :]
+
+    inside, upper = [], []
+    for half in range(2):
+        place = panel(COLUMN_ROW + half).astype(jnp.int32) - mine
+        inside.append((place >= 0) & (place < NY))
+        upper.append(place >= LANES)
+        place_ref[half * COLS : (half + 1) * COLS, :] = (place & (LANES - 1)).astype(F32)
+    want = row_iota((LANES, LANES)).astype(F32)
     for block in range(COLS):
-        ends = parts_ref[block * 8 : (block + 1) * 8, :].astype(jnp.bfloat16)
-        at = block * SEND_ROWS + 9 + 10
+        ends = parts_ref[block * 16 : (block + 1) * 16, :].astype(jnp.bfloat16)
         for half in range(2):
-            column = recv_ref[at + half : at + half + 1, :]
-            onehot = jnp.where(want == column, 1.0, 0.0).astype(jnp.bfloat16)
+            at = half * COLS + block
+            onehot = jnp.where(want == place_ref[at : at + 1, :], 1.0, 0.0).astype(jnp.bfloat16)
             got = jnp.dot(ends, onehot, preferred_element_type=F32)
-            picked_ref[(half * COLS + block) * 8 : (half * COLS + block + 1) * 8, :] = got
+            picked_ref[at * 16 : (at + 1) * 16, :] = got
+    meta = panel(META_ROW)
+    starts = [meta[:, j : j + 1] for j in range(8)] + [float(PANELS_DEV)]
     sums = [[None] * 8 for _ in range(3)]
     for half in range(2):
 
-        def panel(at):
-            return recv_ref[pl.ds(9 + 2 * at + half, COLS, stride=SEND_ROWS), :]
-
         def got(at):
-            return picked_ref[pl.ds(half * COLS * 8 + at, COLS, stride=8), :]
-
-        low = got(0) + got(1) + got(2)
-        high = got(3) + got(4) + got(5)
-        at_panel = panel(3) * low + panel(4) * high
-        section = panel(6)
-        for k in range(3):
-            term = panel(k) * at_panel
-            for j in range(8):
-                part = jnp.where(section == float(j), term, 0.0)
+            return picked_ref[pl.ds(half * COLS * 16 + at, COLS, stride=16), :]
+
+        low = [got(8 * h) + got(8 * h + 1) + got(8 * h + 2) for h in range(2)]
+        high = [got(8 * h + 3) + got(8 * h + 4) + got(8 * h + 5) for h in range(2)]
+        low = jnp.where(upper[half], low[1], low[0])
+        high = jnp.where(upper[half], high[1], high[0])
+        at_panel = panel(FIRST_ROW + half) * low + panel(LAST_ROW + half) * high
+        at_panel = jnp.where(inside[half], at_panel, 0.0)
+        place = (lane_iota((COLS, LANES)) + half * LANES).astype(F32)
+        reached = [place >= start for start in starts]
+        terms = [panel(GEOM_ROW + 2 * k + half) * at_panel for k in range(3)]
+        for j in range(8):
+            in_section = reached[j] & jnp.logical_not(reached[j + 1])
+            for k in range(3):
+                part = jnp.where(in_section, terms[k], 0.0)
                 part = part[0:8, :] + part[8:16, :]
                 sums[k][j] = part if half == 0 else sums[k][j] + part
     terms = [
         jnp.concatenate([jnp.sum(x, axis=0, keepdims=True) for x in sums[k]], 0)
         for k in range(3)
     ]
+    constant = jnp.sum(meta, axis=0, keepdims=True)
+    lanes = lane_iota((1, LANES))
+    own = lax.rem(column_device, OWNERS) == 0
     rows = section_rows(terms)
+    for k in range(3):
+        moved = pltpu.roll(constant, LANES - 8 * (k + 1), 1)
+        rows[k] = rows[k] + jnp.where((lanes < 8) & own, moved, 0.0)
     for block in range(COLS):
+        at = block * BACK_ROWS + 8
         for k in range(3):
-            at = block * BACK_ROWS + 4 + k
-            back_ref[at : at + 1, :] = rows[k] + constant_ref[k : k + 1, :]
-        back_ref[block * BACK_ROWS + 7 : block * BACK_ROWS + 8, :] = zero_row
+            all_ref[at + k : at + k + 1, :] = rows[k]
+        all_ref[at + 3 : at + 8, :] = jnp.zeros((5, LANES), F32)
+    mine = pl.multiple_of((column_device // OWNERS) * (OWNERS * BACK_ROWS), OWNERS * BACK_ROWS)
+    back_ref[...] = all_ref[pl.ds(mine, OWNERS * BACK_ROWS), :]
 
 
 def load_kernel(back_ref, load_ref):
     load_ref[...] = jnp.zeros_like(load_ref)
     for k in range(3):
-        rows = back_ref[pl.ds(4 + k, COLS, stride=BACK_ROWS), :]
+        rows = back_ref[pl.ds(8 + k, OWNERS, stride=BACK_ROWS), :]
         load_ref[k : k + 1, :] = jnp.sum(rows, axis=0, keepdims=True)
 
 
 def field_kernel(back_ref, mat_ref, offset_ref, w_ref, pressure_ref, velocity_ref):
     def end(at):
-        halves = [
-            back_ref[pl.ds(half * BACK_ROWS + at, CX, stride=2 * BACK_ROWS), :] for half in range(2)
-        ]
+        halves = [back_ref[pl.ds(half * 4 + at, CX, stride=BACK_ROWS), :] for half in range(2)]
         return jnp.concatenate(halves, axis=1)
 
     to_first = [level(mat_ref, A_AT + j) for j in range(CZ - 2)]
@@ -416,21 +475,30 @@
     trailing = GAMMA_HORIZ * p_star[:, CX - 1 :, :] + HALF_DIV * u_star[:, CX - 1 :, :]
     to_other = call(choose_kernel, [(CZ, NY)], flops=2000000000)(leading, trailing)
     from_other = lax.ppermute(to_other, "slab", others)
-    mat, source, panel, plane = call(
-        matrix_kernel, [(MAT_LEVELS * CX, NY), flat, (16, LANES), (CZ, NY)], flops=5000000
+    mat, source, panel, bounds, ordered, plane = call(
+        matrix_kernel,
+        [(MAT_LEVELS * CX, NY), flat, (16, LANES), (16, LANES), (8, PANELS_DEV), (CZ, NY)],
+        flops=5000000,
     )(p, u, v, w, flags, cell, section, panel_geom)
     from_pair = lax.ppermute(plane, "slab", pairs)
-    send, offsets, constant = call(
-        pack_kernel,
-        [(COLS * SEND_ROWS, LANES), ((CZ - 2) * CX, NY), (8, LANES)],
-    )(mat, source, from_pair, from_other, w, panel, cell)
+    send, offsets = call(pack_kernel, [(COLS * SEND_ROWS, LANES), ((CZ - 2) * CX, NY)])(
+        mat, source, from_pair, from_other, w, panel, bounds, ordered
+    )
     recv = lax.all_to_all(send, "col", 0, 0, tiled=True)
     back = call(
         owner_kernel,
-        [(COLS * BACK_ROWS, LANES)],
-        [(40, LANES), (16, LANES), (COLS * 8, LANES), (2 * COLS * 8, LANES)],
-    )(recv, constant)
-    back = lax.all_to_all(back, "col", 0, 0, tiled=True)
+        [(OWNERS * BACK_ROWS, LANES)],
+        [
+            (2, 40, LANES),
+            (2, 16, LANES),
+            (COLS * BACK_ROWS, LANES),
+            (COLS * 16, LANES),
+            (2 * COLS, LANES),
+            (2 * COLS * 16, LANES),
+        ],
+    )(recv)
+    sets = [list(range(at, at + OWNERS)) for at in range(0, COLS, OWNERS)]
+    back = lax.all_to_all(back, "col", 0, 0, axis_index_groups=sets, tiled=True)
     loads = call(load_kernel, [(8, LANES)])(back)
     loads_other = lax.ppermute(loads, "slab", others)
     loads_pair = lax.ppermute(loads, "slab", pairs)

time: 57.8 us -> 56.7 us (0.981)
  blocking collectives: 27.9 us -> 25.6 us
  starting transfers between devices: 22.5 us -> 23.2 us
    all_to_all x1, blocking collectives: 10.9 us -> 7.58 us  [per_device(): back = lax.all_to_all(back, 'col', 0, 0, axis_index_groups=sets, tiled=True)]
    all_to_all x1, blocking collectives: 17 us -> 18.1 us  [per_device(): recv = lax.all_to_all(send, 'col', 0, 0, tiled=True)]
    ppermute x1, starting transfers between devices: 8.33 us -> 9.06 us  [per_device(): loads_other = lax.ppermute(loads, 'slab', others)]
where the time goes in v4:
time: 56.7 us; the launch traced here: 56.3 us
  blocking collectives  25.6 us (45%)
  starting transfers between devices  23.2 us (41%)
  Pallas kernels  3.44 us (6%)
  waiting for transfers between devices  1.58 us (3%)
  other arithmetic  0.97 us (2%)
  between operations  0.81 us (1%)
  local copies, waits for them, and re-layouts  0.66 us (1%)
    all_to_all x1, blocking collectives, per_device(): recv = lax.all_to_all(send, 'col', 0, 0, tiled=True)  18.1 us
    ppermute x1, starting transfers between devices, per_device(): from_other = lax.ppermute(to_other, 'slab', others)  10.3 us
    ppermute x1, starting transfers between devices, per_device(): loads_other = lax.ppermute(loads, 'slab', others)  9.06 us
    all_to_all x1, blocking collectives, per_device(): back = lax.all_to_all(back, 'col', 0, 0, axis_index_groups=sets, tiled=True)  7.58 us
    ppermute x1, starting transfers between devices, per_device(): from_pair = lax.ppermute(plane, 'slab', pairs)  1.92 us
    ppermute x1, starting transfers between devices, per_device(): loads_pair = lax.ppermute(loads, 'slab', pairs)  1.92 us
  transfers between devices with their start and end apart: 4, of which 2 were waited for; matrix products, arithmetic and copies ran while one was open for 0% of the time, Pallas kernels for 2%

profile of v4, /device:TPU:1, one launch (start us, length us, event | category | flops | bytes accessed | tf_op | source)
XLA Modules:
  0.0 56.3 jit_solution(6164713375190675981)
XLA Ops:
  0.6 1.0 %multiply_add_fusion = (f32[8,1,256]{2,1,0:T(1,128)S(1)}, f32[8,1,256]{2,1,0:T(1,128)S(1)}) fusion(f32[8,8,256]{2,1,0:T(8,128)} %param.9, f32[8,8,256]{2,1,0:T(8,128)} %param.8), kind=kLoop, calls=%fused_computation | loop fusion | flops 12288 | bytes 49152 | tf_op jit(solution)/shard_map/add | solution.py:475
  1.6 0.0 copy-start
  1.6 0.0 copy-start.1
  1.6 0.0 copy-start.2
  1.6 0.0 copy-start.3
  1.6 0.0 copy-start.4
  1.7 0.0 copy-start.7
  1.7 10.3 %collective-permute-start.1 = (f32[8,256]{1,0:T(8,128)S(1)}, f32[8,256]{1,0:T(8,128)S(1)}, u32[]{:S(2)}, u32[]{:S(2)}) collective-permute-start(f32[8,256]{1,0:T(8,128)S(1)} %shard_map.104), channel_id=1, source_target_pairs={{1,2},{3,4},{5,6},{7,8},{9,10},{11,12},{13,14},{15,16},{17,18},{19... | collective-permute-start | bytes 24584 | tf_op jit(solution)/shard_map/ppermute | solution.py:477
  12.0 0.0 copy-start.5
  12.1 0.0 copy-start.6
  12.1 0.0 copy-done
  12.1 0.0 copy-done.1
  12.1 0.0 copy-done.2
  12.1 0.0 copy-done.3
  12.1 0.0 copy-done.4
  12.1 0.0 copy-done.7
  12.1 0.6 %copy-done.5 = f32[3,256]{1,0:T(4,128)S(1)} copy-done((f32[3,256]{1,0:T(4,128)S(1)}, f32[3,256]{1,0:T(4,128)}, u32[]{:S(2)}) %copy-start.5) | copy-done | bytes 3096
  12.7 0.0 copy-done.6
  12.7 0.7 %shard_map.103 = (f32[240,256]{1,0:T(8,128)S(1)}, f32[64,256]{1,0:T(8,128)S(1)}, f32[16,128]{1,0:T(8,128)S(1)}, f32[16,128]{1,0:T(8,128)S(1)}, f32[8,256]{1,0:T(8,128)S(1)}, /*index=5*/f32[8,256]{1,0:T(8,128)S(1)}) custom-call(f32[64,256]{1,0:T(8,128)S(1)} %bitcast.21, f32[64,256]{1,0:T(8,128)S(1)} %bitcast.22, f32[64,256]{1,0:T(8,128)S(1)} %bitcast.23, ...), custom_call_target="tpu_custom_call" | custom-call | flops 5000000 | bytes 500000 | tf_op jit(solution)/shard_map/pallas_call | solution.py:478
  13.4 1.9 %collective-permute-start = (f32[8,256]{1,0:T(8,128)S(1)}, f32[8,256]{1,0:T(8,128)S(1)}, u32[]{:S(2)}, u32[]{:S(2)}) collective-permute-start(f32[8,256]{1,0:T(8,128)S(1)} %get-tuple-element.15), channel_id=1, source_target_pairs={{0,1},{1,0},{2,3},{3,2},{4,5},{5,4},{6,7},{7,6},{8,9},{9,8},{10,11... | collective-permute-start | bytes 24584 | tf_op jit(solution)/shard_map/ppermute | solution.py:483
  15.4 0.0 collective-permute-done.1.other_ref
  15.4 1.1 %collective-permute-done.pair_ref = f32[8,256]{1,0:T(8,128)S(1)} collective-permute-done((f32[8,256]{1,0:T(8,128)S(1)}, f32[8,256]{1,0:T(8,128)S(1)}, u32[]{:S(2)}, u32[]{:S(2)}) %collective-permute-start) | collective-permute-done | bytes 8224 | tf_op jit(solution)/shard_map/ppermute | solution.py:483
  16.5 0.4 shard_map.105
  16.9 18.1 %all_to_all.22 = f32[16,32,128]{2,1,0:T(8,128)S(1)} all-to-all(f32[16,32,128]{2,1,0:T(8,128)S(1)} %bitcast.20), channel_id=1, replica_groups=mesh['col'=16,'slab'=32] {'col'}, dimensions={0} | all-to-all | bytes 524288 | tf_op jit(solution)/shard_map/all_to_all | solution.py:487
  35.0 0.9 %shard_map.106 = f32[128,128]{1,0:T(8,128)S(1)} custom-call(f32[512,128]{1,0:T(8,128)S(1)} %bitcast.13), custom_call_target="tpu_custom_call" | custom-call | flops 20000 | bytes 500000 | tf_op jit(solution)/shard_map/pallas_call | solution.py:488
  35.9 7.6 %all_to_all.23 = f32[8,16,128]{2,1,0:T(8,128)S(1)} all-to-all(f32[8,16,128]{2,1,0:T(8,128)S(1)} %bitcast.19), channel_id=1, replica_groups={{0,32,64,96,128,160,192,224},{256,288,320,352,384,416,448,480},{1,33,65..., dimensions={0} | all-to-all | bytes 131072 | tf_op jit(solution)/shard_map/all_to_all | solution.py:501
  43.5 9.1 %collective-permute-start.3 = (f32[8,128]{1,0:T(8,128)S(1)}, f32[8,128]{1,0:T(8,128)S(1)}, u32[]{:S(2)}, u32[]{:S(2)}) collective-permute-start(f32[8,128]{1,0:T(8,128)S(1)} %shard_map.108.load_ref), channel_id=1, source_target_pairs={{1,2},{3,4},{5,6},{7,8},{9,10},{11,12},{13,14},{15,16},{17,18},{19... | collective-permute-start | bytes 12296 | tf_op jit(solution)/shard_map/ppermute | solution.py:503
  52.6 1.9 %collective-permute-start.2 = (f32[8,128]{1,0:T(8,128)S(1)}, f32[8,128]{1,0:T(8,128)S(1)}, u32[]{:S(2)}, u32[]{:S(2)}) collective-permute-start(f32[8,128]{1,0:T(8,128)S(1)} %shard_map.108.load_ref), channel_id=1, source_target_pairs={{0,1},{1,0},{2,3},{3,2},{4,5},{5,4},{6,7},{7,6},{8,9},{9,8},{10,11... | collective-permute-start | bytes 12296 | tf_op jit(solution)/shard_map/ppermute | solution.py:504
  54.5 0.7 %shard_map.107 = (f32[64,256]{1,0:T(8,128)}, f32[64,256]{1,0:T(8,128)}) custom-call(f32[128,128]{1,0:T(8,128)S(1)} %bitcast.18, f32[240,256]{1,0:T(8,128)S(1)} %get-tuple-element.13.mat_ref, f32[48,256]{1,0:T(8,128)S(1)} %get-tuple-element.20.offset_ref, f32[64,256]{1,0:T(8,128)S(1)} %bitcast.16), custom_call_target="tpu_custom_call" | custom-call | flops 5000000 | bytes 500000 | tf_op jit(solution)/shard_map/pallas_call | solution.py:505
  55.2 0.0 collective-permute-done.3.other_ref
  55.2 0.4 collective-permute-done.2.pair_ref
  55.6 0.7 %shard_map.109 = f32[3,4]{1,0:T(4,128)} custom-call(f32[8,128]{1,0:T(8,128)S(1)} %shard_map.108.load_ref, f32[8,128]{1,0:T(8,128)S(1)} %collective-permute-done.2.pair_ref, f32[8,128]{1,0:T(8,128)S(1)} %collective-permute-done.3.other_ref), custom_call_target="tpu_custom_call" | custom-call | flops 20000 | bytes 500000 | tf_op jit(solution)/shard_map/pallas_call | solution.py:506
  (2 shorter events, 0.0 us)
Async XLA Ops:
  1.6 10.5 %copy-start = (f32[8,8,256]{2,1,0:T(8,128)S(1)}, f32[8,8,256]{2,1,0:T(8,128)}, u32[]{:S(2)}) copy-start(f32[8,8,256]{2,1,0:T(8,128)} %param.11) | copy-start | bytes 196612
  1.6 10.5 %copy-start.1 = (f32[8,8,256]{2,1,0:T(8,128)S(1)}, f32[8,8,256]{2,1,0:T(8,128)}, u32[]{:S(2)}) copy-start(f32[8,8,256]{2,1,0:T(8,128)} %param.8) | copy-start | bytes 196612
  1.6 10.5 %copy-start.2 = (f32[8,8,256]{2,1,0:T(8,128)S(1)}, f32[8,8,256]{2,1,0:T(8,128)}, u32[]{:S(2)}) copy-start(f32[8,8,256]{2,1,0:T(8,128)} %param.9) | copy-start | bytes 196612
  1.6 10.5 %copy-start.3 = (f32[8,8,256]{2,1,0:T(8,128)S(1)}, f32[8,8,256]{2,1,0:T(8,128)}, u32[]{:S(2)}) copy-start(f32[8,8,256]{2,1,0:T(8,128)} %param.10) | copy-start | bytes 196612
  1.6 10.5 %copy-start.4 = (s32[8,8,256]{2,1,0:T(8,128)S(1)}, s32[8,8,256]{2,1,0:T(8,128)}, u32[]{:S(2)}) copy-start(s32[8,8,256]{2,1,0:T(8,128)} %param.12) | copy-start | bytes 196612
  1.7 10.5 %copy-start.7 = (s32[256]{0:T(256)S(1)}, s32[256]{0:T(256)}, u32[]{:S(2)}) copy-start(s32[256]{0:T(256)} %param.14) | copy-start | bytes 3076
  1.7 13.7 %collective-permute-start.1 = (f32[8,256]{1,0:T(8,128)S(1)}, f32[8,256]{1,0:T(8,128)S(1)}, u32[]{:S(2)}, u32[]{:S(2)}) collective-permute-start(f32[8,256]{1,0:T(8,128)S(1)} %shard_map.104), channel_id=1, source_target_pairs={{1,2},{3,4},{5,6},{7,8},{9,10},{11,12},{13,14},{15,16},{17,18},{19... | collective-permute-start | bytes 24584 | tf_op jit(solution)/shard_map/ppermute | solution.py:477
  12.0 0.7 %copy-start.5 = (f32[3,256]{1,0:T(4,128)S(1)}, f32[3,256]{1,0:T(4,128)}, u32[]{:S(2)}) copy-start(f32[3,256]{1,0:T(4,128)} %geom_ref.1) | copy-start | bytes 9220
  12.1 0.7 %copy-start.6 = (s32[256]{0:T(256)S(1)}, s32[256]{0:T(256)}, u32[]{:S(2)}) copy-start(s32[256]{0:T(256)} %param.13) | copy-start | bytes 3076
  13.4 3.1 %collective-permute-start = (f32[8,256]{1,0:T(8,128)S(1)}, f32[8,256]{1,0:T(8,128)S(1)}, u32[]{:S(2)}, u32[]{:S(2)}) collective-permute-start(f32[8,256]{1,0:T(8,128)S(1)} %get-tuple-element.15), channel_id=1, source_target_pairs={{0,1},{1,0},{2,3},{3,2},{4,5},{5,4},{6,7},{7,6},{8,9},{9,8},{10,11... | collective-permute-start | bytes 24584 | tf_op jit(solution)/shard_map/ppermute | solution.py:483
  43.5 11.7 %collective-permute-start.3 = (f32[8,128]{1,0:T(8,128)S(1)}, f32[8,128]{1,0:T(8,128)S(1)}, u32[]{:S(2)}, u32[]{:S(2)}) collective-permute-start(f32[8,128]{1,0:T(8,128)S(1)} %shard_map.108.load_ref), channel_id=1, source_target_pairs={{1,2},{3,4},{5,6},{7,8},{9,10},{11,12},{13,14},{15,16},{17,18},{19... | collective-permute-start | bytes 12296 | tf_op jit(solution)/shard_map/ppermute | solution.py:503
  52.6 3.1 %collective-permute-start.2 = (f32[8,128]{1,0:T(8,128)S(1)}, f32[8,128]{1,0:T(8,128)S(1)}, u32[]{:S(2)}, u32[]{:S(2)}) collective-permute-start(f32[8,128]{1,0:T(8,128)S(1)} %shard_map.108.load_ref), channel_id=1, source_target_pairs={{0,1},{1,0},{2,3},{3,2},{4,5},{5,4},{6,7},{7,6},{8,9},{9,8},{10,11... | collective-permute-start | bytes 12296 | tf_op jit(solution)/shard_map/ppermute | solution.py:504

commit v5 on v4

--- a/solution.py
+++ b/solution.py
@@ -50,11 +50,15 @@
     return high, middle, low
 
 
+def exact_dot(x, onehot):
+    rows = x.shape[0]
+    parts = jnp.concatenate(split_three(x), 0)
+    got = jnp.dot(parts, onehot, preferred_element_type=F32)
+    return got[:rows] + got[rows : 2 * rows] + got[2 * rows :]
+
+
 def pick(fields, onehot, row_mask):
-    total = None
-    for part in split_three(fields):
-        term = jnp.dot(part, onehot, preferred_element_type=F32)
-        total = term if total is None else total + term
+    total = exact_dot(fields, onehot)
     return jnp.sum(jnp.where(row_mask, total, 0.0), axis=0, keepdims=True)
 
 
@@ -64,39 +68,45 @@
     return onehot.astype(jnp.bfloat16), row_mask
 
 
+def halving(count):
+    nodes, order = list(range(count)), []
+    while len(nodes) > 2:
+        gone = range(1, len(nodes) - 1, 2)
+        order += [(nodes[i], nodes[i - 1], nodes[i + 1]) for i in gone]
+        nodes = [node for i, node in enumerate(nodes) if i not in gone]
+    return order
+
+
 def condense(ground, edges):
-    first, here, link = ground[0], ground[1], edges[0]
-    to_first, to_next, inverse = [], [], []
-    for j in range(1, len(ground) - 1):
-        edge = edges[j]
-        inv = 1.0 / (here + link + edge)
-        a, b = link * inv, edge * inv
-        first = first + a * here
-        here = ground[j + 1] + b * here
-        link = link * b
-        to_first.append(a)
-        to_next.append(b)
-        inverse.append(inv)
-    return first, here, link, to_first, to_next, inverse
-
-
-def condense_source(source, to_first, to_next, inverse):
-    first, here = source[0], source[1]
-    offsets = []
-    for j in range(1, len(source) - 1):
-        a, b = to_first[j - 1], to_next[j - 1]
-        offsets.append(here * inverse[j - 1])
-        first = first + a * here
-        here = source[j + 1] + b * here
-    return first, here, offsets
-
-
-def expand(first, last, to_first, to_next, offsets):
-    values = [last]
-    for a, b, offset in zip(reversed(to_first), reversed(to_next), reversed(offsets)):
-        values.append(offset + a * first + b * values[-1])
-    values.append(first)
-    return values[::-1]
+    count = len(ground)
+    ground = list(ground)
+    edges = {(i, i + 1): edge for i, edge in enumerate(edges)}
+    to_low, to_high, inverse = ([None] * (count - 2) for _ in range(3))
+    for node, low, high in halving(count):
+        inv = 1.0 / (ground[node] + edges[low, node] + edges[node, high])
+        a, b = edges[low, node] * inv, edges[node, high] * inv
+        to_low[node - 1], to_high[node - 1], inverse[node - 1] = a, b, inv
+        ground[low] = ground[low] + a * ground[node]
+        ground[high] = ground[high] + b * ground[node]
+        edges[low, high] = edges[low, node] * b
+    return ground[0], ground[-1], edges[0, count - 1], to_low, to_high, inverse
+
+
+def condense_source(source, to_low, to_high, inverse):
+    source = list(source)
+    for node, low, high in halving(len(source)):
+        source[low] = source[low] + to_low[node - 1] * source[node]
+        source[high] = source[high] + to_high[node - 1] * source[node]
+    offsets = [x * inv for x, inv in zip(source[1:-1], inverse)]
+    return source[0], source[-1], offsets
+
+
+def expand(first, last, to_low, to_high, offsets):
+    values = [first] + [None] * len(offsets) + [last]
+    for node, low, high in reversed(halving(len(values))):
+        inflow = to_low[node - 1] * values[low] + to_high[node - 1] * values[high]
+        values[node] = inflow if offsets[node - 1] is None else offsets[node - 1] + inflow
+    return values
 
 
 def to_row(column):
@@ -116,17 +126,27 @@
     key_column = jnp.sum(jnp.where(on_diagonal, key, 0.0), axis=1, keepdims=True)
     rank = jnp.sum(jnp.where(key < key_column, 1.0, 0.0), axis=1, keepdims=True)
     order = jnp.where(lane_iota(square).astype(F32) == rank, 1.0, 0.0).astype(jnp.bfloat16)
-    total = None
-    for part in split_three(rows):
-        term = jnp.dot(part, order, preferred_element_type=F32)
-        total = term if total is None else total + term
-    return total
-
-
-def choose_kernel(leading_ref, trailing_ref, plane_ref):
+    return exact_dot(rows, order)
+
+
+def fetch_kernel(*refs):
+    sources, targets, other_ref, pair_ref, sems = refs[:8], refs[8:16], *refs[16:]
+    fetches = [
+        pltpu.make_async_copy(source, target, sems.at[i])
+        for i, (source, target) in enumerate(zip(sources, targets))
+    ]
+    for fetch in fetches:
+        fetch.start()
+    p_ref, u_ref = targets[:2]
     even = lax.rem(lax.axis_index("slab"), 2) == 0
+    for fetch in fetches:
+        fetch.wait()
     for z in range(CZ):
-        plane_ref[z : z + 1, :] = jnp.where(even, leading_ref[z], trailing_ref[z])
+        first, last = z * CX, (z + 1) * CX - 1
+        leading = GAMMA_HORIZ * p_ref[first : first + 1, :] - HALF_DIV * u_ref[first : first + 1, :]
+        trailing = GAMMA_HORIZ * p_ref[last : last + 1, :] + HALF_DIV * u_ref[last : last + 1, :]
+        other_ref[z : z + 1, :] = jnp.where(even, leading, trailing)
+        pair_ref[z : z + 1, :] = jnp.where(even, trailing, leading)
 
 
 A_AT, B_AT, I_AT, FACE_AT, PORT_AT = 0, 6, 12, 18, 25
@@ -135,16 +155,8 @@
 
 def matrix_kernel(
     p_ref, u_ref, v_ref, w_ref, flags_ref, cell_ref, sec_ref, geom_ref,
-    mat_ref, src_ref, panel_ref, bound_ref, sorted_ref, plane_ref,
+    mat_ref, src_ref, panel_ref, bound_ref, sorted_ref,
 ):
-    even = lax.rem(lax.axis_index("slab"), 2) == 0
-    for z in range(CZ):
-        p, u = level(p_ref, z), level(u_ref, z)
-        plane_ref[z : z + 1, :] = jnp.where(
-            even,
-            GAMMA_HORIZ * p[CX - 1 :, :] + HALF_DIV * u[CX - 1 :, :],
-            GAMMA_HORIZ * p[:1, :] - HALF_DIV * u[:1, :],
-        )
     shape = (CX, NY)
     rows, lanes = row_iota(shape), lane_iota(shape)
     densities, kappas = [], []
@@ -188,13 +200,13 @@
             kappa * p + GAMMA_HORIZ * laplacian - DIVERGENCE_SCALE * divergence
         )
     faces = [2.0 / (densities[z] + densities[z + 1]) for z in range(CZ - 1)]
-    first, last, link, to_first, to_next, inverse = condense(kappas, faces)
-    stored = to_first + to_next + inverse + faces + [first, last, link, densities[0], densities[-1]]
+    first, last, link, to_low, to_high, inverse = condense(kappas, faces)
+    stored = to_low + to_high + inverse + faces + [first, last, link, densities[0], densities[-1]]
     for at, value in enumerate(stored):
         mat_ref[at * CX : (at + 1) * CX, :] = value
 
     zero, one = jnp.zeros(shape, F32), jnp.ones(shape, F32)
-    no_offset = [zero] * (CZ - 2)
+    no_offset = [None] * (CZ - 2)
     section = sec_ref[...] - (lax.axis_index("slab") * SEC_DEV - REACH)
     rows = [geom_ref[k : k + 1, :] for k in range(3)] + [cell_ref[...].astype(F32)]
     rows = sort_panels(section, jnp.concatenate(rows + [jnp.zeros((4, PANELS_DEV), F32)], 0))
@@ -207,8 +219,8 @@
 
     cell = rows[3:4, :].astype(jnp.int32)
     onehot, row_mask = panel_masks(cell)
-    from_first = expand(one, zero, to_first, to_next, no_offset)
-    from_last = expand(zero, one, to_first, to_next, no_offset)
+    from_first = expand(one, zero, to_low, to_high, no_offset)
+    from_last = expand(zero, one, to_low, to_high, no_offset)
     panel_rows = [rows[k : k + 1, :] for k in range(3)]
     panel_rows.append(pick(jnp.concatenate(from_first, 0), onehot, row_mask))
     panel_rows.append(pick(jnp.concatenate(from_last, 0), onehot, row_mask))
@@ -223,7 +235,7 @@
 
 
 def pack_kernel(
-    mat_ref, src_ref, pair_ref, other_ref, w_ref, panel_ref, bound_ref, sorted_ref,
+    mat_ref, src_ref, other_ref, pair_ref, w_ref, panel_ref, bound_ref, sorted_ref,
     send_ref, offset_ref,
 ):
     even = lax.rem(lax.axis_index("slab"), 2) == 0
@@ -238,15 +250,15 @@
             rows == CX - 1, from_right[z : z + 1, :], 0.0
         )
         source.append(level(src_ref, z) + halo)
-    to_first = [level(mat_ref, A_AT + j) for j in range(CZ - 2)]
-    to_next = [level(mat_ref, B_AT + j) for j in range(CZ - 2)]
+    to_low = [level(mat_ref, A_AT + j) for j in range(CZ - 2)]
+    to_high = [level(mat_ref, B_AT + j) for j in range(CZ - 2)]
     inverse = [level(mat_ref, I_AT + j) for j in range(CZ - 2)]
-    first, last, offsets = condense_source(source, to_first, to_next, inverse)
+    first, last, offsets = condense_source(source, to_low, to_high, inverse)
     for j, offset in enumerate(offsets):
         offset_ref[j * CX : (j + 1) * CX, :] = offset
 
     zero = jnp.zeros(shape, F32)
-    constant = expand(zero, zero, to_first, to_next, offsets)
+    constant = expand(zero, zero, to_low, to_high, offsets)
     onehot, row_mask = panel_masks(sorted_ref[3:4, :].astype(jnp.int32))
     at_panel = pick(jnp.concatenate(constant, 0), onehot, row_mask)
     terms = [0.0, 0.0, 0.0]
@@ -294,8 +306,8 @@
         ground += [low_k[x], high_k[x]]
         source += [low_r[x], high_r[x]]
         edges += [link[x]] + ([join[x]] if x < 3 else [])
-    first, last, across, to_first, to_next, inverse = condense(ground, edges)
-    first_r, last_r, offsets = condense_source(source, to_first, to_next, inverse)
+    first, last, across, to_low, to_high, inverse = condense(ground, edges)
+    first_r, last_r, offsets = condense_source(source, to_low, to_high, inverse)
 
     stored = [first, last, across, first_r, last_r, low_d[0], high_d[3], low_w[0], high_w[3]]
     for at, x in enumerate(stored):
@@ -311,12 +323,12 @@
         ground += [low_k[z], high_k[z]]
         source += [low_r[z], high_r[z]]
         edges += [link[z]] + ([outer[z]] if z < 3 else [])
-    k_a, k_b, f_ab, a_list, b_list, i_list = condense(ground, edges)
-    r_a, r_b, o_list = condense_source(source, a_list, b_list, i_list)
+    k_a, k_b, f_ab, *factors = condense(ground, edges)
+    r_a, r_b, outer_offsets = condense_source(source, *factors)
     scale = 1.0 / (k_a * k_b + f_ab * (k_a + k_b))
     p_a = ((k_b + f_ab) * r_a + f_ab * r_b) * scale
     p_b = ((k_a + f_ab) * r_b + f_ab * r_a) * scale
-    nodes = expand(p_a, p_b, a_list, b_list, o_list)
+    nodes = expand(p_a, p_b, *factors[:2], outer_offsets)
     zero_row = jnp.zeros((1, LANES), F32)
     flux = [outer[z] * (nodes[2 * z + 2] - nodes[2 * z + 1]) for z in range(3)]
     for z in range(4):
@@ -325,7 +337,7 @@
         ends_ref[half, 8 + z : 9 + z, :] = flux[z - 1] if z > 0 else zero_row
         ends_ref[half, 12 + z : 13 + z, :] = flux[z] if z < 3 else zero_row
 
-    nodes = expand(ends_ref[half, 0:4, :], ends_ref[half, 4:8, :], to_first, to_next, offsets)
+    nodes = expand(ends_ref[half, 0:4, :], ends_ref[half, 4:8, :], to_low, to_high, offsets)
     inner = [join[x] * (nodes[2 * x + 2] - nodes[2 * x + 1]) for x in range(3)]
     below = [ends_ref[half, 8:12, :]] + inner
     above = inner + [ends_ref[half, 12:16, :]]
@@ -360,14 +372,18 @@
         inside.append((place >= 0) & (place < NY))
         upper.append(place >= LANES)
         place_ref[half * COLS : (half + 1) * COLS, :] = (place & (LANES - 1)).astype(F32)
-    want = row_iota((LANES, LANES)).astype(F32)
+    want = row_iota((LANES, LANES)).astype(F32).astype(jnp.bfloat16)
     for block in range(COLS):
         ends = parts_ref[block * 16 : (block + 1) * 16, :].astype(jnp.bfloat16)
+        onehots = []
         for half in range(2):
             at = half * COLS + block
-            onehot = jnp.where(want == place_ref[at : at + 1, :], 1.0, 0.0).astype(jnp.bfloat16)
-            got = jnp.dot(ends, onehot, preferred_element_type=F32)
-            picked_ref[at * 16 : (at + 1) * 16, :] = got
+            place = place_ref[at : at + 1, :].astype(jnp.bfloat16)
+            onehots.append(jnp.where(want == place, jnp.bfloat16(1.0), jnp.bfloat16(0.0)))
+        got = jnp.dot(ends, jnp.concatenate(onehots, 1), preferred_element_type=F32)
+        for half in range(2):
+            at = half * COLS + block
+            picked_ref[at * 16 : (at + 1) * 16, :] = got[:, half * LANES : (half + 1) * LANES]
     meta = panel(META_ROW)
     starts = [meta[:, j : j + 1] for j in range(8)] + [float(PANELS_DEV)]
     sums = [[None] * 8 for _ in range(3)]
@@ -423,10 +439,10 @@
         halves = [back_ref[pl.ds(half * 4 + at, CX, stride=BACK_ROWS), :] for half in range(2)]
         return jnp.concatenate(halves, axis=1)
 
-    to_first = [level(mat_ref, A_AT + j) for j in range(CZ - 2)]
-    to_next = [level(mat_ref, B_AT + j) for j in range(CZ - 2)]
+    to_low = [level(mat_ref, A_AT + j) for j in range(CZ - 2)]
+    to_high = [level(mat_ref, B_AT + j) for j in range(CZ - 2)]
     offsets = [level(offset_ref, j) for j in range(CZ - 2)]
-    pressure = expand(end(0), end(1), to_first, to_next, offsets)
+    pressure = expand(end(0), end(1), to_low, to_high, offsets)
     flux = [end(2)]
     for z in range(CZ - 1):
         flux.append(level(mat_ref, FACE_AT + z) * (pressure[z + 1] - pressure[z]))
@@ -471,18 +487,26 @@
     others = [(i, i + 1) for i in range(1, slabs - 1, 2)]
     others += [(j, i) for i, j in others]
 
-    leading = GAMMA_HORIZ * p_star[:, :1, :] - HALF_DIV * u_star[:, :1, :]
-    trailing = GAMMA_HORIZ * p_star[:, CX - 1 :, :] + HALF_DIV * u_star[:, CX - 1 :, :]
-    to_other = call(choose_kernel, [(CZ, NY)], flops=2000000000)(leading, trailing)
+    inputs = [p, u, v, w, flags, cell, section, panel_geom]
+    *inputs, to_other, to_pair = pl.pallas_call(
+        fetch_kernel,
+        out_shape=[jax.ShapeDtypeStruct(x.shape, x.dtype) for x in inputs]
+        + [jax.ShapeDtypeStruct((CZ, NY), F32)] * 2,
+        in_specs=[pl.BlockSpec(memory_space=pltpu.HBM)] * 8,
+        scratch_shapes=[pltpu.SemaphoreType.DMA((8,))],
+        compiler_params=pltpu.CompilerParams(vmem_limit_bytes=16 * 1024 * 1024),
+        cost_estimate=pl.CostEstimate(flops=20000, bytes_accessed=500000, transcendentals=0),
+    )(*[pltpu.with_memory_space_constraint(x, pltpu.HBM) for x in inputs])
+    p, u, v, w, flags, cell, section, panel_geom = inputs
     from_other = lax.ppermute(to_other, "slab", others)
-    mat, source, panel, bounds, ordered, plane = call(
+    from_pair = lax.ppermute(to_pair, "slab", pairs)
+    mat, source, panel, bounds, ordered = call(
         matrix_kernel,
-        [(MAT_LEVELS * CX, NY), flat, (16, LANES), (16, LANES), (8, PANELS_DEV), (CZ, NY)],
+        [(MAT_LEVELS * CX, NY), flat, (16, LANES), (16, LANES), (8, PANELS_DEV)],
         flops=5000000,
     )(p, u, v, w, flags, cell, section, panel_geom)
-    from_pair = lax.ppermute(plane, "slab", pairs)
     send, offsets = call(pack_kernel, [(COLS * SEND_ROWS, LANES), ((CZ - 2) * CX, NY)])(
-        mat, source, from_pair, from_other, w, panel, bounds, ordered
+        mat, source, from_other, from_pair, w, panel, bounds, ordered
     )
     recv = lax.all_to_all(send, "col", 0, 0, tiled=True)
     back = call(

time: 56.7 us -> 55 us (0.970)
  other arithmetic: 0.97 us -> 0 us
  Pallas kernels: 3.44 us -> 4.24 us
  local copies, waits for them, and re-layouts: 0.66 us -> 0 us
  waiting for transfers between devices: 1.58 us -> 0.95 us
    pallas_call x1, Pallas kernels: 0.02 us -> 1.07 us  [per_device(): pl.pallas_call(fetch_kernel, out_shape=[jax.ShapeDtypeStruct(x.shape, x.d...]
    add x1 -> x0, other arithmetic: 0.97 us -> none  [per_device(): GAMMA_HORIZ * p_star[:, CX - 1:, :] + HALF_DIV * u_star[:, CX - 1:, :]]
    unnamed x16 -> x0, local copies, waits for them, and re-layouts: 0.66 us -> none
    ppermute x1, waiting for transfers between devices: 1.13 us -> 0.49 us  [per_device(): from_pair = lax.ppermute(to_pair, 'slab', pairs)]
where the time goes in v5:
time: 55 us; the launch traced here: 54.6 us
  blocking collectives  25.7 us (47%)
  starting transfers between devices  23.1 us (42%)
  Pallas kernels  4.24 us (8%)
  waiting for transfers between devices  0.95 us (2%)
  between operations  0.7 us (1%)
    all_to_all x1, blocking collectives, per_device(): recv = lax.all_to_all(send, 'col', 0, 0, tiled=True)  18.1 us
    ppermute x1, starting transfers between devices, per_device(): from_other = lax.ppermute(to_other, 'slab', others)  10.2 us
    ppermute x1, starting transfers between devices, per_device(): loads_other = lax.ppermute(loads, 'slab', others)  9.06 us
    all_to_all x1, blocking collectives, per_device(): back = lax.all_to_all(back, 'col', 0, 0, axis_index_groups=sets, tiled=True)  7.58 us
    ppermute x1, starting transfers between devices, per_device(): loads_pair = lax.ppermute(loads, 'slab', pairs)  1.92 us
    ppermute x1, starting transfers between devices, per_device(): from_pair = lax.ppermute(to_pair, 'slab', pairs)  1.92 us
  transfers between devices with their start and end apart: 4, of which 2 were waited for; matrix products, arithmetic and copies ran while one was open for 0% of the time, Pallas kernels for 2%

profile of v5, /device:TPU:1, one launch (start us, length us, event | category | flops | bytes accessed | tf_op | source)
XLA Modules:
  0.0 54.6 jit_solution(2835040846188426128)
XLA Ops:
  0.6 1.1 %shard_map.103 = (f32[64,256]{1,0:T(8,128)S(1)}, f32[64,256]{1,0:T(8,128)S(1)}, f32[64,256]{1,0:T(8,128)S(1)}, f32[64,256]{1,0:T(8,128)S(1)}, s32[64,256]{1,0:T(...) custom-call(f32[64,256]{1,0:T(8,128)} %bitcast.18, ...), custom_call_target="tpu_custom_call" | custom-call | flops 20000 | bytes 500000 | tf_op jit(solution)/shard_map/pallas_call | solution.py:491
  1.7 10.2 %collective-permute-start = (f32[8,256]{1,0:T(8,128)S(1)}, f32[8,256]{1,0:T(8,128)S(1)}, u32[]{:S(2)}, u32[]{:S(2)}) collective-permute-start(f32[8,256]{1,0:T(8,128)S(1)} %get-tuple-element.32), channel_id=1, source_target_pairs={{1,2},{3,4},{5,6},{7,8},{9,10},{11,12},{13,14},{15,16},{17,18},{19... | collective-permute-start | bytes 24584 | tf_op jit(solution)/shard_map/ppermute | solution.py:501
  11.9 1.9 %collective-permute-start.1 = (f32[8,256]{1,0:T(8,128)S(1)}, f32[8,256]{1,0:T(8,128)S(1)}, u32[]{:S(2)}, u32[]{:S(2)}) collective-permute-start(f32[8,256]{1,0:T(8,128)S(1)} %get-tuple-element.33), channel_id=1, source_target_pairs={{0,1},{1,0},{2,3},{3,2},{4,5},{5,4},{6,7},{7,6},{8,9},{9,8},{10,11... | collective-permute-start | bytes 24584 | tf_op jit(solution)/shard_map/ppermute | solution.py:502
  13.9 0.6 %shard_map.104 = (f32[240,256]{1,0:T(8,128)S(1)}, f32[64,256]{1,0:T(8,128)S(1)}, f32[16,128]{1,0:T(8,128)S(1)}, f32[16,128]{1,0:T(8,128)S(1)}, f32[8,256]{1,0:T(8,128)S(1)}) custom-call(f32[64,256]{1,0:T(8,128)S(1)} %get-tuple-element.22.p_ref, f32[64,256]{1,0:T(8,128)S(1)} %get-tuple-element.23.u_ref, f32[64,256]{1,0:T(8,128)S(1)} %get-tuple-element.24.v_ref, ...), custom_call_target="tpu_custom_call" | custom-call | flops 5000000 | bytes 500000 | tf_op jit(solution)/shard_map/pallas_call | solution.py:503
  14.5 0.0 collective-permute-done.other_ref
  14.5 0.5 collective-permute-done.1.pair_ref
  15.0 0.4 shard_map.105
  15.4 18.1 %all_to_all.22 = f32[16,32,128]{2,1,0:T(8,128)S(1)} all-to-all(f32[16,32,128]{2,1,0:T(8,128)S(1)} %bitcast.17), channel_id=1, replica_groups=mesh['col'=16,'slab'=32] {'col'}, dimensions={0} | all-to-all | bytes 524288 | tf_op jit(solution)/shard_map/all_to_all | solution.py:511
  33.5 0.7 %shard_map.106 = f32[128,128]{1,0:T(8,128)S(1)} custom-call(f32[512,128]{1,0:T(8,128)S(1)} %bitcast.13), custom_call_target="tpu_custom_call" | custom-call | flops 20000 | bytes 500000 | tf_op jit(solution)/shard_map/pallas_call | solution.py:512
  34.2 7.6 %all_to_all.23 = f32[8,16,128]{2,1,0:T(8,128)S(1)} all-to-all(f32[8,16,128]{2,1,0:T(8,128)S(1)} %bitcast.16), channel_id=1, replica_groups={{0,32,64,96,128,160,192,224},{256,288,320,352,384,416,448,480},{1,33,65..., dimensions={0} | all-to-all | bytes 131072 | tf_op jit(solution)/shard_map/all_to_all | solution.py:525
  41.8 9.1 %collective-permute-start.3 = (f32[8,128]{1,0:T(8,128)S(1)}, f32[8,128]{1,0:T(8,128)S(1)}, u32[]{:S(2)}, u32[]{:S(2)}) collective-permute-start(f32[8,128]{1,0:T(8,128)S(1)} %shard_map.108.load_ref), channel_id=1, source_target_pairs={{1,2},{3,4},{5,6},{7,8},{9,10},{11,12},{13,14},{15,16},{17,18},{19... | collective-permute-start | bytes 12296 | tf_op jit(solution)/shard_map/ppermute | solution.py:527
  50.9 1.9 %collective-permute-start.2 = (f32[8,128]{1,0:T(8,128)S(1)}, f32[8,128]{1,0:T(8,128)S(1)}, u32[]{:S(2)}, u32[]{:S(2)}) collective-permute-start(f32[8,128]{1,0:T(8,128)S(1)} %shard_map.108.load_ref), channel_id=1, source_target_pairs={{0,1},{1,0},{2,3},{3,2},{4,5},{5,4},{6,7},{7,6},{8,9},{9,8},{10,11... | collective-permute-start | bytes 12296 | tf_op jit(solution)/shard_map/ppermute | solution.py:528
  52.8 0.7 %shard_map.107 = (f32[64,256]{1,0:T(8,128)}, f32[64,256]{1,0:T(8,128)}) custom-call(f32[128,128]{1,0:T(8,128)S(1)} %bitcast.15, f32[240,256]{1,0:T(8,128)S(1)} %get-tuple-element.30.mat_ref, f32[48,256]{1,0:T(8,128)S(1)} %get-tuple-element.38.offset_ref, f32[64,256]{1,0:T(8,128)S(1)} %get-tuple-element.25.w_ref), custom_call_target="tpu_custom_call" | custom-call | flops 5000000 | bytes 500000 | tf_op jit(solution)/shard_map/pallas_call | solution.py:529
  53.5 0.0 collective-permute-done.3.other_ref
  53.5 0.4 collective-permute-done.2.pair_ref
  53.9 0.7 %shard_map.109 = f32[3,4]{1,0:T(4,128)} custom-call(f32[8,128]{1,0:T(8,128)S(1)} %shard_map.108.load_ref, f32[8,128]{1,0:T(8,128)S(1)} %collective-permute-done.2.pair_ref, f32[8,128]{1,0:T(8,128)S(1)} %collective-permute-done.3.other_ref), custom_call_target="tpu_custom_call" | custom-call | flops 20000 | bytes 500000 | tf_op jit(solution)/shard_map/pallas_call | solution.py:530
  (1 shorter events, 0.0 us)
Async XLA Ops:
  1.7 12.8 %collective-permute-start = (f32[8,256]{1,0:T(8,128)S(1)}, f32[8,256]{1,0:T(8,128)S(1)}, u32[]{:S(2)}, u32[]{:S(2)}) collective-permute-start(f32[8,256]{1,0:T(8,128)S(1)} %get-tuple-element.32), channel_id=1, source_target_pairs={{1,2},{3,4},{5,6},{7,8},{9,10},{11,12},{13,14},{15,16},{17,18},{19... | collective-permute-start | bytes 24584 | tf_op jit(solution)/shard_map/ppermute | solution.py:501
  11.9 3.1 %collective-permute-start.1 = (f32[8,256]{1,0:T(8,128)S(1)}, f32[8,256]{1,0:T(8,128)S(1)}, u32[]{:S(2)}, u32[]{:S(2)}) collective-permute-start(f32[8,256]{1,0:T(8,128)S(1)} %get-tuple-element.33), channel_id=1, source_target_pairs={{0,1},{1,0},{2,3},{3,2},{4,5},{5,4},{6,7},{7,6},{8,9},{9,8},{10,11... | collective-permute-start | bytes 24584 | tf_op jit(solution)/shard_map/ppermute | solution.py:502
  41.8 11.7 %collective-permute-start.3 = (f32[8,128]{1,0:T(8,128)S(1)}, f32[8,128]{1,0:T(8,128)S(1)}, u32[]{:S(2)}, u32[]{:S(2)}) collective-permute-start(f32[8,128]{1,0:T(8,128)S(1)} %shard_map.108.load_ref), channel_id=1, source_target_pairs={{1,2},{3,4},{5,6},{7,8},{9,10},{11,12},{13,14},{15,16},{17,18},{19... | collective-permute-start | bytes 12296 | tf_op jit(solution)/shard_map/ppermute | solution.py:527
  50.9 3.1 %collective-permute-start.2 = (f32[8,128]{1,0:T(8,128)S(1)}, f32[8,128]{1,0:T(8,128)S(1)}, u32[]{:S(2)}, u32[]{:S(2)}) collective-permute-start(f32[8,128]{1,0:T(8,128)S(1)} %shard_map.108.load_ref), channel_id=1, source_target_pairs={{0,1},{1,0},{2,3},{3,2},{4,5},{5,4},{6,7},{7,6},{8,9},{9,8},{10,11... | collective-permute-start | bytes 12296 | tf_op jit(solution)/shard_map/ppermute | solution.py:528

commit v6 on v5

--- a/solution.py
+++ b/solution.py
@@ -238,10 +238,11 @@
     mat_ref, src_ref, other_ref, pair_ref, w_ref, panel_ref, bound_ref, sorted_ref,
     send_ref, offset_ref,
 ):
-    even = lax.rem(lax.axis_index("slab"), 2) == 0
+    core = lax.rem(lax.axis_index("slab"), 2)
+    even = core == 0
     shape = (CX, NY)
     rows = row_iota(shape)
-    received, beyond = pair_ref[...], other_ref[...]
+    received, beyond = pair_ref[1 - core], other_ref[...]
     from_left = jnp.where(even, beyond, received)
     from_right = jnp.where(even, received, beyond)
     source = []
@@ -453,8 +454,9 @@
 
 
 def section_kernel(load_ref, pair_ref, other_ref, out_ref):
-    even = lax.rem(lax.axis_index("slab"), 2) == 0
-    received, beyond = pair_ref[...], other_ref[...]
+    core = lax.rem(lax.axis_index("slab"), 2)
+    even = core == 0
+    received, beyond = pair_ref[1 - core], other_ref[...]
     from_left = jnp.where(even, beyond, received)
     from_right = jnp.where(even, received, beyond)
     lanes = lane_iota((8, LANES))
@@ -483,7 +485,7 @@
     cell = panel_cell.reshape(1, PANELS_DEV)
     section = panel_section.reshape(1, PANELS_DEV)
     slabs = lax.axis_size("slab")
-    pairs = [(i, i ^ 1) for i in range(slabs)]
+    cores = [[i, i + 1] for i in range(0, slabs, 2)]
     others = [(i, i + 1) for i in range(1, slabs - 1, 2)]
     others += [(j, i) for i, j in others]
 
@@ -499,7 +501,7 @@
     )(*[pltpu.with_memory_space_constraint(x, pltpu.HBM) for x in inputs])
     p, u, v, w, flags, cell, section, panel_geom = inputs
     from_other = lax.ppermute(to_other, "slab", others)
-    from_pair = lax.ppermute(to_pair, "slab", pairs)
+    from_pair = lax.all_gather(to_pair, "slab", axis_index_groups=cores)
     mat, source, panel, bounds, ordered = call(
         matrix_kernel,
         [(MAT_LEVELS * CX, NY), flat, (16, LANES), (16, LANES), (8, PANELS_DEV)],
@@ -525,7 +527,7 @@
     back = lax.all_to_all(back, "col", 0, 0, axis_index_groups=sets, tiled=True)
     loads = call(load_kernel, [(8, LANES)])(back)
     loads_other = lax.ppermute(loads, "slab", others)
-    loads_pair = lax.ppermute(loads, "slab", pairs)
+    loads_pair = lax.all_gather(loads, "slab", axis_index_groups=cores)
     pressure, velocity = call(field_kernel, [flat, flat], flops=5000000)(back, mat, offsets, w)
     section_loads = call(section_kernel, [(3, SEC_DEV)])(loads, loads_pair, loads_other)
     return pressure.reshape(p_star.shape), velocity.reshape(p_star.shape), section_loads

time: 55 us -> 54.1 us (0.984)
  starting transfers between devices: 23.1 us -> 19.3 us
  blocking collectives: 25.7 us -> 29.2 us
  waiting for transfers between devices: 0.95 us -> 0.01 us
    ppermute x2 -> x0, starting transfers between devices: 3.84 us -> none  [the longest x1 1.92 us: per_device(): loads_pair = lax.ppermute(loads, 'slab', pairs)]
    all_gather x0 -> x2, blocking collectives: none -> 3.6 us  [the longest x1 1.81 us: per_device(): from_pair = lax.all_gather(to_pair, 'slab', axis_index_groups=cores)]
    ppermute x2 -> x0, waiting for transfers between devices: 0.94 us -> none  [the longest x1 0.49 us: per_device(): from_pair = lax.ppermute(to_pair, 'slab', pairs)]
  transfers between devices with their start and end apart: 4 -> 2, of which waited for: 2 -> 0; matrix products, arithmetic and copies ran while one was open for 0% -> 0% of each run, Pallas kernels for 2% -> 2%
where the time goes in v6:
time: 54.1 us; the launch traced here: 53.5 us
  blocking collectives  29.2 us (54%)
  starting transfers between devices  19.3 us (36%)
  Pallas kernels  4.24 us (8%)
  between operations  0.68 us (1%)
    all_to_all x1, blocking collectives, per_device(): recv = lax.all_to_all(send, 'col', 0, 0, tiled=True)  18.1 us
    ppermute x1, starting transfers between devices, per_device(): from_other = lax.ppermute(to_other, 'slab', others)  10.2 us
    ppermute x1, starting transfers between devices, per_device(): loads_other = lax.ppermute(loads, 'slab', others)  9.1 us
    all_to_all x1, blocking collectives, per_device(): back = lax.all_to_all(back, 'col', 0, 0, axis_index_groups=sets, tiled=True)  7.58 us
    all_gather x1, blocking collectives, per_device(): from_pair = lax.all_gather(to_pair, 'slab', axis_index_groups=cores)  1.81 us
    all_gather x1, blocking collectives, per_device(): loads_pair = lax.all_gather(loads, 'slab', axis_index_groups=cores)  1.78 us
  transfers between devices with their start and end apart: 2, of which 0 were waited for; matrix products, arithmetic and copies ran while one was open for 0% of the time, Pallas kernels for 2%

profile of v6, /device:TPU:1, one launch (start us, length us, event | category | flops | bytes accessed | tf_op | source)
XLA Modules:
  0.0 53.5 jit_solution(9779083717641625568)
XLA Ops:
  0.6 1.1 %shard_map.103 = (f32[64,256]{1,0:T(8,128)S(1)}, f32[64,256]{1,0:T(8,128)S(1)}, f32[64,256]{1,0:T(8,128)S(1)}, f32[64,256]{1,0:T(8,128)S(1)}, s32[64,256]{1,0:T(...) custom-call(f32[64,256]{1,0:T(8,128)} %bitcast.22, ...), custom_call_target="tpu_custom_call" | custom-call | flops 20000 | bytes 500000 | tf_op jit(solution)/shard_map/pallas_call | solution.py:493
  1.7 10.2 %collective-permute-start = (f32[8,256]{1,0:T(8,128)S(1)}, f32[8,256]{1,0:T(8,128)S(1)}, u32[]{:S(2)}, u32[]{:S(2)}) collective-permute-start(f32[8,256]{1,0:T(8,128)S(1)} %get-tuple-element.32), channel_id=1, source_target_pairs={{1,2},{3,4},{5,6},{7,8},{9,10},{11,12},{13,14},{15,16},{17,18},{19... | collective-permute-start | bytes 24584 | tf_op jit(solution)/shard_map/ppermute | solution.py:503
  11.9 0.6 %shard_map.104 = (f32[240,256]{1,0:T(8,128)S(1)}, f32[64,256]{1,0:T(8,128)S(1)}, f32[16,128]{1,0:T(8,128)S(1)}, f32[16,128]{1,0:T(8,128)S(1)}, f32[8,256]{1,0:T(8,128)S(1)}) custom-call(f32[64,256]{1,0:T(8,128)S(1)} %get-tuple-element.22.p_ref, f32[64,256]{1,0:T(8,128)S(1)} %get-tuple-element.23.u_ref, f32[64,256]{1,0:T(8,128)S(1)} %get-tuple-element.24.v_ref, ...), custom_call_target="tpu_custom_call" | custom-call | flops 5000000 | bytes 500000 | tf_op jit(solution)/shard_map/pallas_call | solution.py:505
  12.6 1.8 %all-gather = f32[16,256]{1,0:T(8,128)S(1)} all-gather(f32[8,256]{1,0:T(8,128)S(1)} %get-tuple-element.33), channel_id=2, replica_groups={{0,1},{2,3},{4,5},{6,7},{8,9},{10,11},{12,13},{14,15},{16,17},{18,19},{..., dimensions={0}, use_global_device_ids=true | all-gather | bytes 24576 | tf_op jit(solution)/shard_map/all_gather | solution.py:504
  14.4 0.0 collective-permute-done.other_ref
  14.4 0.4 shard_map.105
  14.8 18.1 %all_to_all.22 = f32[16,32,128]{2,1,0:T(8,128)S(1)} all-to-all(f32[16,32,128]{2,1,0:T(8,128)S(1)} %bitcast.19), channel_id=1, replica_groups=mesh['col'=16,'slab'=32] {'col'}, dimensions={0} | all-to-all | bytes 524288 | tf_op jit(solution)/shard_map/all_to_all | solution.py:513
  32.8 0.7 %shard_map.106 = f32[128,128]{1,0:T(8,128)S(1)} custom-call(f32[512,128]{1,0:T(8,128)S(1)} %bitcast.15), custom_call_target="tpu_custom_call" | custom-call | flops 20000 | bytes 500000 | tf_op jit(solution)/shard_map/pallas_call | solution.py:514
  33.6 7.6 %all_to_all.23 = f32[8,16,128]{2,1,0:T(8,128)S(1)} all-to-all(f32[8,16,128]{2,1,0:T(8,128)S(1)} %bitcast.18), channel_id=1, replica_groups={{0,32,64,96,128,160,192,224},{256,288,320,352,384,416,448,480},{1,33,65..., dimensions={0} | all-to-all | bytes 131072 | tf_op jit(solution)/shard_map/all_to_all | solution.py:527
  41.2 9.1 %collective-permute-start.1 = (f32[8,128]{1,0:T(8,128)S(1)}, f32[8,128]{1,0:T(8,128)S(1)}, u32[]{:S(2)}, u32[]{:S(2)}) collective-permute-start(f32[8,128]{1,0:T(8,128)S(1)} %shard_map.108.load_ref), channel_id=1, source_target_pairs={{1,2},{3,4},{5,6},{7,8},{9,10},{11,12},{13,14},{15,16},{17,18},{19... | collective-permute-start | bytes 12296 | tf_op jit(solution)/shard_map/ppermute | solution.py:529
  50.3 0.7 %shard_map.107 = (f32[64,256]{1,0:T(8,128)}, f32[64,256]{1,0:T(8,128)}) custom-call(f32[128,128]{1,0:T(8,128)S(1)} %bitcast.17, f32[240,256]{1,0:T(8,128)S(1)} %get-tuple-element.30.mat_ref, f32[48,256]{1,0:T(8,128)S(1)} %get-tuple-element.38.offset_ref, f32[64,256]{1,0:T(8,128)S(1)} %get-tuple-element.25.w_ref), custom_call_target="tpu_custom_call" | custom-call | flops 5000000 | bytes 500000 | tf_op jit(solution)/shard_map/pallas_call | solution.py:531
  50.9 1.8 %all-gather.1 = f32[16,128]{1,0:T(8,128)S(1)} all-gather(f32[8,128]{1,0:T(8,128)S(1)} %shard_map.108.load_ref), channel_id=3, replica_groups={{0,1},{2,3},{4,5},{6,7},{8,9},{10,11},{12,13},{14,15},{16,17},{18,19},{..., dimensions={0}, use_global_device_ids=true | all-gather | bytes 12288 | tf_op jit(solution)/shard_map/all_gather | solution.py:530
  52.7 0.0 collective-permute-done.1.other_ref
  52.7 0.7 %shard_map.109 = f32[3,4]{1,0:T(4,128)} custom-call(f32[8,128]{1,0:T(8,128)S(1)} %shard_map.108.load_ref, f32[2,8,128]{2,1,0:T(8,128)S(1)} %bitcast.21, f32[8,128]{1,0:T(8,128)S(1)} %collective-permute-done.1.other_ref), custom_call_target="tpu_custom_call" | custom-call | flops 20000 | bytes 500000 | tf_op jit(solution)/shard_map/pallas_call | solution.py:532
  (1 shorter events, 0.0 us)
Async XLA Ops:
  1.7 12.7 %collective-permute-start = (f32[8,256]{1,0:T(8,128)S(1)}, f32[8,256]{1,0:T(8,128)S(1)}, u32[]{:S(2)}, u32[]{:S(2)}) collective-permute-start(f32[8,256]{1,0:T(8,128)S(1)} %get-tuple-element.32), channel_id=1, source_target_pairs={{1,2},{3,4},{5,6},{7,8},{9,10},{11,12},{13,14},{15,16},{17,18},{19... | collective-permute-start | bytes 24584 | tf_op jit(solution)/shard_map/ppermute | solution.py:503
  41.2 11.6 %collective-permute-start.1 = (f32[8,128]{1,0:T(8,128)S(1)}, f32[8,128]{1,0:T(8,128)S(1)}, u32[]{:S(2)}, u32[]{:S(2)}) collective-permute-start(f32[8,128]{1,0:T(8,128)S(1)} %shard_map.108.load_ref), channel_id=1, source_target_pairs={{1,2},{3,4},{5,6},{7,8},{9,10},{11,12},{13,14},{15,16},{17,18},{19... | collective-permute-start | bytes 12296 | tf_op jit(solution)/shard_map/ppermute | solution.py:529

commit v7 on v6

--- a/solution.py
+++ b/solution.py
@@ -23,9 +23,9 @@
 PANELS_DEV = 256
 REACH = 2
 OWNERS = 8
-SEND_ROWS = 32
-BACK_ROWS = 16
-GEOM_ROW, FIRST_ROW, LAST_ROW, COLUMN_ROW, META_ROW = 18, 24, 26, 28, 30
+SEND_ROWS = 29
+BACK_ROWS = 9
+GEOM_ROW, SHARE_ROW, COLUMN_ROW, META_ROW = 18, 24, 26, 28
 
 F32 = jnp.float32
 
@@ -130,16 +130,29 @@
 
 
 def fetch_kernel(*refs):
-    sources, targets, other_ref, pair_ref, sems = refs[:8], refs[8:16], *refs[16:]
+    sources, targets = refs[:8], refs[8:13] + refs[17:20]
+    other_ref, pair_ref, bound_ref, sorted_ref = refs[13:17]
+    p_ref, u_ref = targets[:2]
+    cell_ref, sec_ref, geom_ref = targets[5:]
     fetches = [
-        pltpu.make_async_copy(source, target, sems.at[i])
+        pltpu.make_async_copy(source, target, refs[20].at[i])
         for i, (source, target) in enumerate(zip(sources, targets))
     ]
-    for fetch in fetches:
+    for fetch in fetches[5:] + fetches[:5]:
         fetch.start()
-    p_ref, u_ref = targets[:2]
-    even = lax.rem(lax.axis_index("slab"), 2) == 0
-    for fetch in fetches:
+    slab = lax.axis_index("slab")
+    even = lax.rem(slab, 2) == 0
+    for fetch in fetches[5:]:
+        fetch.wait()
+    section = sec_ref[...] - (slab * SEC_DEV - REACH)
+    rows = [geom_ref[k : k + 1, :] for k in range(3)] + [cell_ref[...].astype(F32)]
+    rows = jnp.concatenate(rows + [jnp.zeros((4, PANELS_DEV), F32)], 0)
+    sorted_ref[...] = sort_panels(section, rows)
+    at_section = row_iota((8, PANELS_DEV))
+    for at, before in enumerate((section < at_section, section <= at_section)):
+        count = jnp.sum(jnp.where(before, 1.0, 0.0), axis=1, keepdims=True)
+        bound_ref[at * 8 : (at + 1) * 8, :] = jnp.broadcast_to(count, (8, LANES))
+    for fetch in fetches[:5]:
         fetch.wait()
     for z in range(CZ):
         first, last = z * CX, (z + 1) * CX - 1
@@ -154,8 +167,7 @@
 
 
 def matrix_kernel(
-    p_ref, u_ref, v_ref, w_ref, flags_ref, cell_ref, sec_ref, geom_ref,
-    mat_ref, src_ref, panel_ref, bound_ref, sorted_ref,
+    p_ref, u_ref, v_ref, w_ref, flags_ref, bound_ref, sorted_ref, mat_ref, src_ref, panel_ref
 ):
     shape = (CX, NY)
     rows, lanes = row_iota(shape), lane_iota(shape)
@@ -207,31 +219,23 @@
 
     zero, one = jnp.zeros(shape, F32), jnp.ones(shape, F32)
     no_offset = [None] * (CZ - 2)
-    section = sec_ref[...] - (lax.axis_index("slab") * SEC_DEV - REACH)
-    rows = [geom_ref[k : k + 1, :] for k in range(3)] + [cell_ref[...].astype(F32)]
-    rows = sort_panels(section, jnp.concatenate(rows + [jnp.zeros((4, PANELS_DEV), F32)], 0))
-    sorted_ref[...] = rows
-    at_section = row_iota((8, PANELS_DEV))
-    starts = jnp.sum(jnp.where(section < at_section, 1.0, 0.0), axis=1, keepdims=True)
-    stops = jnp.sum(jnp.where(section <= at_section, 1.0, 0.0), axis=1, keepdims=True)
-    bound_ref[0:8, :] = jnp.broadcast_to(starts, (8, LANES))
-    bound_ref[8:16, :] = jnp.broadcast_to(stops, (8, LANES))
-
+    rows = sorted_ref[...]
     cell = rows[3:4, :].astype(jnp.int32)
     onehot, row_mask = panel_masks(cell)
     from_first = expand(one, zero, to_low, to_high, no_offset)
     from_last = expand(zero, one, to_low, to_high, no_offset)
-    panel_rows = [rows[k : k + 1, :] for k in range(3)]
-    panel_rows.append(pick(jnp.concatenate(from_first, 0), onehot, row_mask))
-    panel_rows.append(pick(jnp.concatenate(from_last, 0), onehot, row_mask))
+    at_first = pick(jnp.concatenate(from_first, 0), onehot, row_mask)
+    at_last = pick(jnp.concatenate(from_last, 0), onehot, row_mask)
+    panel_rows = [rows[k : k + 1, :] * (at_first + at_last) for k in range(3)]
+    panel_rows.append(at_first / (at_first + at_last))
     panel_rows.append((cell & (CX * NY - 1)).astype(F32))
     panel_ref[...] = jnp.zeros_like(panel_ref)
     for at, row in enumerate(panel_rows):
         for half in range(2):
-            panel_ref[2 + 2 * at + half : 3 + 2 * at + half, :] = row[
+            panel_ref[2 * at + half : 2 * at + half + 1, :] = row[
                 :, half * LANES : (half + 1) * LANES
             ]
-    panel_ref[META_ROW - 16 : META_ROW - 15, :] = to_row(starts)
+    panel_ref[META_ROW - GEOM_ROW : META_ROW - GEOM_ROW + 1, :] = to_row(bound_ref[0:8, 0:1])
 
 
 def pack_kernel(
@@ -270,15 +274,13 @@
         for k in range(3):
             row = sorted_ref[k : k + 1, lanes] * at_panel[:, lanes]
             terms[k] = terms[k] + jnp.where(in_section, row, 0.0)
-    meta = panel_ref[META_ROW - 16 : META_ROW - 15, :]
+    meta = panel_ref[META_ROW - GEOM_ROW : META_ROW - GEOM_ROW + 1, :]
     for k, row in enumerate(section_rows(terms)):
         meta = meta + pltpu.roll(row, 8 * (k + 1), 1)
 
-    for device in range(COLS):
-        send_ref[device * SEND_ROWS + 16 : (device + 1) * SEND_ROWS, :] = panel_ref[...]
-    for device in range(COLS):
-        at = device * SEND_ROWS + META_ROW
-        send_ref[at : at + 1, :] = meta
+    for row in range(GEOM_ROW, SEND_ROWS):
+        value = meta if row == META_ROW else panel_ref[row - GEOM_ROW : row - GEOM_ROW + 1, :]
+        send_ref[pl.ds(row, COLS, stride=SEND_ROWS), :] = jnp.broadcast_to(value, (COLS, LANES))
     ports = [level(mat_ref, PORT_AT + j) for j in range(3)] + [first, last]
     ports += [level(mat_ref, PORT_AT + 3), level(mat_ref, PORT_AT + 4)]
     ports += [level(w_ref, 0), level(w_ref, CZ - 1)]
@@ -397,7 +399,7 @@
         high = [got(8 * h + 3) + got(8 * h + 4) + got(8 * h + 5) for h in range(2)]
         low = jnp.where(upper[half], low[1], low[0])
         high = jnp.where(upper[half], high[1], high[0])
-        at_panel = panel(FIRST_ROW + half) * low + panel(LAST_ROW + half) * high
+        at_panel = high + panel(SHARE_ROW + half) * (low - high)
         at_panel = jnp.where(inside[half], at_panel, 0.0)
         place = (lane_iota((COLS, LANES)) + half * LANES).astype(F32)
         reached = [place >= start for start in starts]
@@ -419,20 +421,17 @@
     for k in range(3):
         moved = pltpu.roll(constant, LANES - 8 * (k + 1), 1)
         rows[k] = rows[k] + jnp.where((lanes < 8) & own, moved, 0.0)
-    for block in range(COLS):
-        at = block * BACK_ROWS + 8
-        for k in range(3):
-            all_ref[at + k : at + k + 1, :] = rows[k]
-        all_ref[at + 3 : at + 8, :] = jnp.zeros((5, LANES), F32)
+    packed = sum(pltpu.roll(row, 8 * k, 1) for k, row in enumerate(rows))
+    all_ref[pl.ds(8, COLS, stride=BACK_ROWS), :] = jnp.broadcast_to(packed, (COLS, LANES))
     mine = pl.multiple_of((column_device // OWNERS) * (OWNERS * BACK_ROWS), OWNERS * BACK_ROWS)
     back_ref[...] = all_ref[pl.ds(mine, OWNERS * BACK_ROWS), :]
 
 
 def load_kernel(back_ref, load_ref):
-    load_ref[...] = jnp.zeros_like(load_ref)
-    for k in range(3):
-        rows = back_ref[pl.ds(8 + k, OWNERS, stride=BACK_ROWS), :]
-        load_ref[k : k + 1, :] = jnp.sum(rows, axis=0, keepdims=True)
+    packed = back_ref[pl.ds(8, OWNERS, stride=BACK_ROWS), :]
+    packed = jnp.sum(packed, axis=0, keepdims=True)
+    rows = [packed] + [pltpu.roll(packed, LANES - 8 * k, 1) for k in range(1, 3)]
+    load_ref[...] = jnp.concatenate(rows + [jnp.zeros((5, LANES), F32)], 0)
 
 
 def field_kernel(back_ref, mat_ref, offset_ref, w_ref, pressure_ref, velocity_ref):
@@ -478,6 +477,13 @@
     )
 
 
+def exchange(x, parts, groups=None):
+    rows, lanes = x.shape
+    x = x.reshape(parts, 1, rows // parts * lanes)
+    x = lax.all_to_all(x, "col", 0, 0, axis_index_groups=groups, tiled=True)
+    return x.reshape(rows, lanes)
+
+
 def per_device(p_star, u_star, v_star, w_star, flags, panel_cell, panel_section, panel_geom):
     flat = (CZ * CX, NY)
     p, u, v, w = (x.reshape(flat) for x in (p_star, u_star, v_star, w_star))
@@ -490,27 +496,26 @@
     others += [(j, i) for i, j in others]
 
     inputs = [p, u, v, w, flags, cell, section, panel_geom]
-    *inputs, to_other, to_pair = pl.pallas_call(
+    shapes = [(CZ, NY), (CZ, NY), (16, LANES), (8, PANELS_DEV)]
+    p, u, v, w, flags, to_other, to_pair, bounds, ordered = pl.pallas_call(
         fetch_kernel,
-        out_shape=[jax.ShapeDtypeStruct(x.shape, x.dtype) for x in inputs]
-        + [jax.ShapeDtypeStruct((CZ, NY), F32)] * 2,
+        out_shape=[jax.ShapeDtypeStruct(x.shape, x.dtype) for x in inputs[:5]]
+        + [jax.ShapeDtypeStruct(shape, F32) for shape in shapes],
         in_specs=[pl.BlockSpec(memory_space=pltpu.HBM)] * 8,
-        scratch_shapes=[pltpu.SemaphoreType.DMA((8,))],
+        scratch_shapes=[pltpu.VMEM(x.shape, x.dtype) for x in inputs[5:]]
+        + [pltpu.SemaphoreType.DMA((8,))],
         compiler_params=pltpu.CompilerParams(vmem_limit_bytes=16 * 1024 * 1024),
         cost_estimate=pl.CostEstimate(flops=20000, bytes_accessed=500000, transcendentals=0),
     )(*[pltpu.with_memory_space_constraint(x, pltpu.HBM) for x in inputs])
-    p, u, v, w, flags, cell, section, panel_geom = inputs
     from_other = lax.ppermute(to_other, "slab", others)
     from_pair = lax.all_gather(to_pair, "slab", axis_index_groups=cores)
-    mat, source, panel, bounds, ordered = call(
-        matrix_kernel,
-        [(MAT_LEVELS * CX, NY), flat, (16, LANES), (16, LANES), (8, PANELS_DEV)],
-        flops=5000000,
-    )(p, u, v, w, flags, cell, section, panel_geom)
+    mat, source, panel = call(
+        matrix_kernel, [(MAT_LEVELS * CX, NY), flat, (16, LANES)], flops=5000000
+    )(p, u, v, w, flags, bounds, ordered)
     send, offsets = call(pack_kernel, [(COLS * SEND_ROWS, LANES), ((CZ - 2) * CX, NY)])(
         mat, source, from_other, from_pair, w, panel, bounds, ordered
     )
-    recv = lax.all_to_all(send, "col", 0, 0, tiled=True)
+    recv = exchange(send, COLS)
     back = call(
         owner_kernel,
         [(OWNERS * BACK_ROWS, LANES)],
@@ -524,7 +529,7 @@
         ],
     )(recv)
     sets = [list(range(at, at + OWNERS)) for at in range(0, COLS, OWNERS)]
-    back = lax.all_to_all(back, "col", 0, 0, axis_index_groups=sets, tiled=True)
+    back = exchange(back, OWNERS, sets)
     loads = call(load_kernel, [(8, LANES)])(back)
     loads_other = lax.ppermute(loads, "slab", others)
     loads_pair = lax.all_gather(loads, "slab", axis_index_groups=cores)

time: 54.1 us -> 53.3 us (0.985)
  no operation moved by 1% of the time
where the time goes in v7:
time: 53.3 us; the launch traced here: 52.9 us
  blocking collectives  28.8 us (54%)
  starting transfers between devices  19.4 us (36%)
  Pallas kernels  4.03 us (8%)
  between operations  0.67 us (1%)
    all_to_all x2, blocking collectives, exchange(): x = lax.all_to_all(x, 'col', 0, 0, axis_index_groups=groups, tiled=True)  25.2 us
    ppermute x1, starting transfers between devices, per_device(): from_other = lax.ppermute(to_other, 'slab', others)  10.2 us
    ppermute x1, starting transfers between devices, per_device(): loads_other = lax.ppermute(loads, 'slab', others)  9.17 us
    all_gather x1, blocking collectives, per_device(): from_pair = lax.all_gather(to_pair, 'slab', axis_index_groups=cores)  1.81 us
    all_gather x1, blocking collectives, per_device(): loads_pair = lax.all_gather(loads, 'slab', axis_index_groups=cores)  1.78 us
    pallas_call x1, Pallas kernels, per_device(): pl.pallas_call(fetch_kernel, out_shape=[jax.ShapeDtypeStruct(x.shape, x.d...  1.14 us
  transfers between devices with their start and end apart: 2, of which 0 were waited for; matrix products, arithmetic and copies ran while one was open for 0% of the time, Pallas kernels for 2%

profile of v7, /device:TPU:1, one launch (start us, length us, event | category | flops | bytes accessed | tf_op | source)
XLA Modules:
  0.0 52.9 jit_solution(18222612261236351707)
XLA Ops:
  0.6 1.1 %shard_map.103 = (f32[64,256]{1,0:T(8,128)S(1)}, f32[64,256]{1,0:T(8,128)S(1)}, f32[64,256]{1,0:T(8,128)S(1)}, f32[64,256]{1,0:T(8,128)S(1)}, s32[64,256]{1,0:T(...) custom-call(f32[64,256]{1,0:T(8,128)} %bitcast.22, ...), custom_call_target="tpu_custom_call" | custom-call | flops 20000 | bytes 500000 | tf_op jit(solution)/shard_map/pallas_call | solution.py:500
  1.8 10.2 %collective-permute-start = (f32[8,256]{1,0:T(8,128)S(1)}, f32[8,256]{1,0:T(8,128)S(1)}, u32[]{:S(2)}, u32[]{:S(2)}) collective-permute-start(f32[8,256]{1,0:T(8,128)S(1)} %get-tuple-element.28), channel_id=1, source_target_pairs={{1,2},{3,4},{5,6},{7,8},{9,10},{11,12},{13,14},{15,16},{17,18},{19... | collective-permute-start | bytes 24584 | tf_op jit(solution)/shard_map/ppermute | solution.py:510
  12.0 0.4 shard_map.104
  12.4 1.8 %all-gather = f32[16,256]{1,0:T(8,128)S(1)} all-gather(f32[8,256]{1,0:T(8,128)S(1)} %get-tuple-element.29), channel_id=2, replica_groups={{0,1},{2,3},{4,5},{6,7},{8,9},{10,11},{12,13},{14,15},{16,17},{18,19},{..., dimensions={0}, use_global_device_ids=true | all-gather | bytes 24576 | tf_op jit(solution)/shard_map/all_gather | solution.py:511
  14.2 0.0 collective-permute-done.other_ref
  14.2 0.4 shard_map.105
  14.6 17.7 %all_to_all.10 = f32[16,1,3712]{2,1,0:T(1,128)S(1)} all-to-all(f32[16,1,3712]{2,1,0:T(1,128)S(1)} %bitcast.18), channel_id=1, replica_groups=mesh['col'=16,'slab'=32] {'col'}, dimensions={0} | all-to-all | bytes 475136 | tf_op jit(solution)/shard_map/all_to_all | solution.py:483
  32.3 0.7 %shard_map.106 = f32[72,128]{1,0:T(8,128)S(1)} custom-call(f32[464,128]{1,0:T(8,128)S(1)} %bitcast.15), custom_call_target="tpu_custom_call" | custom-call | flops 20000 | bytes 500000 | tf_op jit(solution)/shard_map/pallas_call | solution.py:519
  32.9 7.5 %all_to_all.11 = f32[8,1,1152]{2,1,0:T(1,128)S(1)} all-to-all(f32[8,1,1152]{2,1,0:T(1,128)S(1)} %bitcast.19), channel_id=1, replica_groups={{0,32,64,96,128,160,192,224},{256,288,320,352,384,416,448,480},{1,33,65..., dimensions={0} | all-to-all | bytes 73728 | tf_op jit(solution)/shard_map/all_to_all | solution.py:483
  40.4 0.1 shard_map.108.load_ref
  40.5 9.2 %collective-permute-start.1 = (f32[8,128]{1,0:T(8,128)S(1)}, f32[8,128]{1,0:T(8,128)S(1)}, u32[]{:S(2)}, u32[]{:S(2)}) collective-permute-start(f32[8,128]{1,0:T(8,128)S(1)} %shard_map.108.load_ref), channel_id=1, source_target_pairs={{1,2},{3,4},{5,6},{7,8},{9,10},{11,12},{13,14},{15,16},{17,18},{19... | collective-permute-start | bytes 12296 | tf_op jit(solution)/shard_map/ppermute | solution.py:534
  49.7 0.7 %shard_map.107 = (f32[64,256]{1,0:T(8,128)}, f32[64,256]{1,0:T(8,128)}) custom-call(f32[72,128]{1,0:T(8,128)S(1)} %bitcast.17, f32[240,256]{1,0:T(8,128)S(1)} %get-tuple-element.26.mat_ref, f32[48,256]{1,0:T(8,128)S(1)} %get-tuple-element.32.offset_ref, f32[64,256]{1,0:T(8,128)S(1)} %get-tuple-element.22.w_ref), custom_call_target="tpu_custom_call" | custom-call | flops 5000000 | bytes 500000 | tf_op jit(solution)/shard_map/pallas_call | solution.py:536
  50.4 1.8 %all-gather.1 = f32[16,128]{1,0:T(8,128)S(1)} all-gather(f32[8,128]{1,0:T(8,128)S(1)} %shard_map.108.load_ref), channel_id=3, replica_groups={{0,1},{2,3},{4,5},{6,7},{8,9},{10,11},{12,13},{14,15},{16,17},{18,19},{..., dimensions={0}, use_global_device_ids=true | all-gather | bytes 12288 | tf_op jit(solution)/shard_map/all_gather | solution.py:535
  52.1 0.0 collective-permute-done.1.other_ref
  52.2 0.7 %shard_map.109 = f32[3,4]{1,0:T(4,128)} custom-call(f32[8,128]{1,0:T(8,128)S(1)} %shard_map.108.load_ref, f32[2,8,128]{2,1,0:T(8,128)S(1)} %bitcast.21, f32[8,128]{1,0:T(8,128)S(1)} %collective-permute-done.1.other_ref), custom_call_target="tpu_custom_call" | custom-call | flops 20000 | bytes 500000 | tf_op jit(solution)/shard_map/pallas_call | solution.py:537
Async XLA Ops:
  1.8 12.4 %collective-permute-start = (f32[8,256]{1,0:T(8,128)S(1)}, f32[8,256]{1,0:T(8,128)S(1)}, u32[]{:S(2)}, u32[]{:S(2)}) collective-permute-start(f32[8,256]{1,0:T(8,128)S(1)} %get-tuple-element.28), channel_id=1, source_target_pairs={{1,2},{3,4},{5,6},{7,8},{9,10},{11,12},{13,14},{15,16},{17,18},{19... | collective-permute-start | bytes 24584 | tf_op jit(solution)/shard_map/ppermute | solution.py:510
  40.5 11.6 %collective-permute-start.1 = (f32[8,128]{1,0:T(8,128)S(1)}, f32[8,128]{1,0:T(8,128)S(1)}, u32[]{:S(2)}, u32[]{:S(2)}) collective-permute-start(f32[8,128]{1,0:T(8,128)S(1)} %shard_map.108.load_ref), channel_id=1, source_target_pairs={{1,2},{3,4},{5,6},{7,8},{9,10},{11,12},{13,14},{15,16},{17,18},{19... | collective-permute-start | bytes 12296 | tf_op jit(solution)/shard_map/ppermute | solution.py:534

commit v8 on v7

--- a/solution.py
+++ b/solution.py
@@ -52,7 +52,10 @@
 
 def exact_dot(x, onehot):
     rows = x.shape[0]
-    parts = jnp.concatenate(split_three(x), 0)
+    parts = split_three(x)
+    if rows % 16:
+        parts = [part.astype(F32) for part in parts]
+    parts = jnp.concatenate(parts, 0).astype(jnp.bfloat16)
     got = jnp.dot(parts, onehot, preferred_element_type=F32)
     return got[:rows] + got[rows : 2 * rows] + got[2 * rows :]
 

time: 53.3 us -> 53.3 us (level)
  no operation moved by 1% of the time
where the time goes in v8:
time: 53.3 us; the launch traced here: 52.9 us
  blocking collectives  28.8 us (54%)
  starting transfers between devices  19.4 us (36%)
  Pallas kernels  4.03 us (8%)
  between operations  0.67 us (1%)
    all_to_all x2, blocking collectives, exchange(): x = lax.all_to_all(x, 'col', 0, 0, axis_index_groups=groups, tiled=True)  25.2 us
    ppermute x1, starting transfers between devices, per_device(): from_other = lax.ppermute(to_other, 'slab', others)  10.2 us
    ppermute x1, starting transfers between devices, per_device(): loads_other = lax.ppermute(loads, 'slab', others)  9.17 us
    all_gather x1, blocking collectives, per_device(): from_pair = lax.all_gather(to_pair, 'slab', axis_index_groups=cores)  1.81 us
    all_gather x1, blocking collectives, per_device(): loads_pair = lax.all_gather(loads, 'slab', axis_index_groups=cores)  1.78 us
    pallas_call x1, Pallas kernels, per_device(): pl.pallas_call(fetch_kernel, out_shape=[jax.ShapeDtypeStruct(x.shape, x.d...  1.14 us
  transfers between devices with their start and end apart: 2, of which 0 were waited for; matrix products, arithmetic and copies ran while one was open for 0% of the time, Pallas kernels for 2%

profile of v8, /device:TPU:1, one launch (start us, length us, event | category | flops | bytes accessed | tf_op | source)
XLA Modules:
  0.0 52.9 jit_solution(9356627457602681550)
XLA Ops:
  0.6 1.1 %shard_map.103 = (f32[64,256]{1,0:T(8,128)S(1)}, f32[64,256]{1,0:T(8,128)S(1)}, f32[64,256]{1,0:T(8,128)S(1)}, f32[64,256]{1,0:T(8,128)S(1)}, s32[64,256]{1,0:T(...) custom-call(f32[64,256]{1,0:T(8,128)} %bitcast.22, ...), custom_call_target="tpu_custom_call" | custom-call | flops 20000 | bytes 500000 | tf_op jit(solution)/shard_map/pallas_call | solution.py:503
  1.8 10.2 %collective-permute-start = (f32[8,256]{1,0:T(8,128)S(1)}, f32[8,256]{1,0:T(8,128)S(1)}, u32[]{:S(2)}, u32[]{:S(2)}) collective-permute-start(f32[8,256]{1,0:T(8,128)S(1)} %get-tuple-element.28), channel_id=1, source_target_pairs={{1,2},{3,4},{5,6},{7,8},{9,10},{11,12},{13,14},{15,16},{17,18},{19... | collective-permute-start | bytes 24584 | tf_op jit(solution)/shard_map/ppermute | solution.py:513
  12.0 0.4 shard_map.104
  12.4 1.8 %all-gather = f32[16,256]{1,0:T(8,128)S(1)} all-gather(f32[8,256]{1,0:T(8,128)S(1)} %get-tuple-element.29), channel_id=2, replica_groups={{0,1},{2,3},{4,5},{6,7},{8,9},{10,11},{12,13},{14,15},{16,17},{18,19},{..., dimensions={0}, use_global_device_ids=true | all-gather | bytes 24576 | tf_op jit(solution)/shard_map/all_gather | solution.py:514
  14.2 0.0 collective-permute-done.other_ref
  14.2 0.4 shard_map.105
  14.6 17.7 %all_to_all.10 = f32[16,1,3712]{2,1,0:T(1,128)S(1)} all-to-all(f32[16,1,3712]{2,1,0:T(1,128)S(1)} %bitcast.18), channel_id=1, replica_groups=mesh['col'=16,'slab'=32] {'col'}, dimensions={0} | all-to-all | bytes 475136 | tf_op jit(solution)/shard_map/all_to_all | solution.py:486
  32.3 0.7 %shard_map.106 = f32[72,128]{1,0:T(8,128)S(1)} custom-call(f32[464,128]{1,0:T(8,128)S(1)} %bitcast.15), custom_call_target="tpu_custom_call" | custom-call | flops 20000 | bytes 500000 | tf_op jit(solution)/shard_map/pallas_call | solution.py:522
  32.9 7.5 %all_to_all.11 = f32[8,1,1152]{2,1,0:T(1,128)S(1)} all-to-all(f32[8,1,1152]{2,1,0:T(1,128)S(1)} %bitcast.19), channel_id=1, replica_groups={{0,32,64,96,128,160,192,224},{256,288,320,352,384,416,448,480},{1,33,65..., dimensions={0} | all-to-all | bytes 73728 | tf_op jit(solution)/shard_map/all_to_all | solution.py:486
  40.4 0.1 shard_map.108.load_ref
  40.5 9.2 %collective-permute-start.1 = (f32[8,128]{1,0:T(8,128)S(1)}, f32[8,128]{1,0:T(8,128)S(1)}, u32[]{:S(2)}, u32[]{:S(2)}) collective-permute-start(f32[8,128]{1,0:T(8,128)S(1)} %shard_map.108.load_ref), channel_id=1, source_target_pairs={{1,2},{3,4},{5,6},{7,8},{9,10},{11,12},{13,14},{15,16},{17,18},{19... | collective-permute-start | bytes 12296 | tf_op jit(solution)/shard_map/ppermute | solution.py:537
  49.7 0.7 %shard_map.107 = (f32[64,256]{1,0:T(8,128)}, f32[64,256]{1,0:T(8,128)}) custom-call(f32[72,128]{1,0:T(8,128)S(1)} %bitcast.17, f32[240,256]{1,0:T(8,128)S(1)} %get-tuple-element.26.mat_ref, f32[48,256]{1,0:T(8,128)S(1)} %get-tuple-element.32.offset_ref, f32[64,256]{1,0:T(8,128)S(1)} %get-tuple-element.22.w_ref), custom_call_target="tpu_custom_call" | custom-call | flops 5000000 | bytes 500000 | tf_op jit(solution)/shard_map/pallas_call | solution.py:539
  50.4 1.8 %all-gather.1 = f32[16,128]{1,0:T(8,128)S(1)} all-gather(f32[8,128]{1,0:T(8,128)S(1)} %shard_map.108.load_ref), channel_id=3, replica_groups={{0,1},{2,3},{4,5},{6,7},{8,9},{10,11},{12,13},{14,15},{16,17},{18,19},{..., dimensions={0}, use_global_device_ids=true | all-gather | bytes 12288 | tf_op jit(solution)/shard_map/all_gather | solution.py:538
  52.1 0.0 collective-permute-done.1.other_ref
  52.2 0.7 %shard_map.109 = f32[3,4]{1,0:T(4,128)} custom-call(f32[8,128]{1,0:T(8,128)S(1)} %shard_map.108.load_ref, f32[2,8,128]{2,1,0:T(8,128)S(1)} %bitcast.21, f32[8,128]{1,0:T(8,128)S(1)} %collective-permute-done.1.other_ref), custom_call_target="tpu_custom_call" | custom-call | flops 20000 | bytes 500000 | tf_op jit(solution)/shard_map/pallas_call | solution.py:540
Async XLA Ops:
  1.8 12.4 %collective-permute-start = (f32[8,256]{1,0:T(8,128)S(1)}, f32[8,256]{1,0:T(8,128)S(1)}, u32[]{:S(2)}, u32[]{:S(2)}) collective-permute-start(f32[8,256]{1,0:T(8,128)S(1)} %get-tuple-element.28), channel_id=1, source_target_pairs={{1,2},{3,4},{5,6},{7,8},{9,10},{11,12},{13,14},{15,16},{17,18},{19... | collective-permute-start | bytes 24584 | tf_op jit(solution)/shard_map/ppermute | solution.py:513
  40.5 11.6 %collective-permute-start.1 = (f32[8,128]{1,0:T(8,128)S(1)}, f32[8,128]{1,0:T(8,128)S(1)}, u32[]{:S(2)}, u32[]{:S(2)}) collective-permute-start(f32[8,128]{1,0:T(8,128)S(1)} %shard_map.108.load_ref), channel_id=1, source_target_pairs={{1,2},{3,4},{5,6},{7,8},{9,10},{11,12},{13,14},{15,16},{17,18},{19... | collective-permute-start | bytes 12296 | tf_op jit(solution)/shard_map/ppermute | solution.py:537

commit v9 on v8

--- a/solution.py
+++ b/solution.py
@@ -432,9 +432,7 @@
 
 def load_kernel(back_ref, load_ref):
     packed = back_ref[pl.ds(8, OWNERS, stride=BACK_ROWS), :]
-    packed = jnp.sum(packed, axis=0, keepdims=True)
-    rows = [packed] + [pltpu.roll(packed, LANES - 8 * k, 1) for k in range(1, 3)]
-    load_ref[...] = jnp.concatenate(rows + [jnp.zeros((5, LANES), F32)], 0)
+    load_ref[...] = jnp.sum(packed, axis=0, keepdims=True)
 
 
 def field_kernel(back_ref, mat_ref, offset_ref, w_ref, pressure_ref, velocity_ref):
@@ -461,12 +459,13 @@
     received, beyond = pair_ref[1 - core], other_ref[...]
     from_left = jnp.where(even, beyond, received)
     from_right = jnp.where(even, received, beyond)
-    lanes = lane_iota((8, LANES))
-    total = load_ref[...]
-    total = total + jnp.where(lanes < 4, pltpu.roll(from_left, LANES - 4, 1), 0.0)
-    total = total + jnp.where(lanes >= 4, pltpu.roll(from_right, 4, 1), 0.0)
-    total = pltpu.roll(total, LANES - REACH, 1)
-    out_ref[...] = total[0:3, 0:SEC_DEV]
+    lower = (lane_iota((1, LANES)) & 7) < 4
+    total = load_ref[...] + jnp.where(
+        lower, pltpu.roll(from_left, LANES - 4, 1), pltpu.roll(from_right, 4, 1)
+    )
+    for k in range(3):
+        moved = pltpu.roll(total, LANES - 8 * k - REACH, 1)
+        out_ref[k : k + 1, :] = moved[:, 0:SEC_DEV]
 
 
 def call(kernel, outs, scratch=(), flops=20000):
@@ -533,7 +532,7 @@
     )(recv)
     sets = [list(range(at, at + OWNERS)) for at in range(0, COLS, OWNERS)]
     back = exchange(back, OWNERS, sets)
-    loads = call(load_kernel, [(8, LANES)])(back)
+    loads = call(load_kernel, [(1, LANES)])(back)
     loads_other = lax.ppermute(loads, "slab", others)
     loads_pair = lax.all_gather(loads, "slab", axis_index_groups=cores)
     pressure, velocity = call(field_kernel, [flat, flat], flops=5000000)(back, mat, offsets, w)

time: 53.3 us -> 53.1 us (level)
  no operation moved by 1% of the time
where the time goes in v9:
time: 53.1 us; the launch traced here: 52.8 us
  blocking collectives  28.8 us (54%)
  starting transfers between devices  19.4 us (37%)
  Pallas kernels  3.96 us (7%)
  between operations  0.67 us (1%)
    all_to_all x2, blocking collectives, exchange(): x = lax.all_to_all(x, 'col', 0, 0, axis_index_groups=groups, tiled=True)  25.2 us
    ppermute x1, starting transfers between devices, per_device(): from_other = lax.ppermute(to_other, 'slab', others)  10.2 us
    ppermute x1, starting transfers between devices, per_device(): loads_other = lax.ppermute(loads, 'slab', others)  9.16 us
    all_gather x1, blocking collectives, per_device(): from_pair = lax.all_gather(to_pair, 'slab', axis_index_groups=cores)  1.81 us
    all_gather x1, blocking collectives, per_device(): loads_pair = lax.all_gather(loads, 'slab', axis_index_groups=cores)  1.77 us
    pallas_call x1, Pallas kernels, per_device(): pl.pallas_call(fetch_kernel, out_shape=[jax.ShapeDtypeStruct(x.shape, x.d...  1.14 us
  transfers between devices with their start and end apart: 2, of which 0 were waited for; matrix products, arithmetic and copies ran while one was open for 0% of the time, Pallas kernels for 2%

profile of v9, /device:TPU:1, one launch (start us, length us, event | category | flops | bytes accessed | tf_op | source)
XLA Modules:
  0.0 52.8 jit_solution(10387775869711577859)
XLA Ops:
  0.6 1.1 %shard_map.103 = (f32[64,256]{1,0:T(8,128)S(1)}, f32[64,256]{1,0:T(8,128)S(1)}, f32[64,256]{1,0:T(8,128)S(1)}, f32[64,256]{1,0:T(8,128)S(1)}, s32[64,256]{1,0:T(...) custom-call(f32[64,256]{1,0:T(8,128)} %bitcast.22, ...), custom_call_target="tpu_custom_call" | custom-call | flops 20000 | bytes 500000 | tf_op jit(solution)/shard_map/pallas_call | solution.py:502
  1.8 10.2 %collective-permute-start = (f32[8,256]{1,0:T(8,128)S(1)}, f32[8,256]{1,0:T(8,128)S(1)}, u32[]{:S(2)}, u32[]{:S(2)}) collective-permute-start(f32[8,256]{1,0:T(8,128)S(1)} %get-tuple-element.28), channel_id=1, source_target_pairs={{1,2},{3,4},{5,6},{7,8},{9,10},{11,12},{13,14},{15,16},{17,18},{19... | collective-permute-start | bytes 24584 | tf_op jit(solution)/shard_map/ppermute | solution.py:512
  12.0 0.4 shard_map.104
  12.4 1.8 %all-gather = f32[16,256]{1,0:T(8,128)S(1)} all-gather(f32[8,256]{1,0:T(8,128)S(1)} %get-tuple-element.29), channel_id=2, replica_groups={{0,1},{2,3},{4,5},{6,7},{8,9},{10,11},{12,13},{14,15},{16,17},{18,19},{..., dimensions={0}, use_global_device_ids=true | all-gather | bytes 24576 | tf_op jit(solution)/shard_map/all_gather | solution.py:513
  14.2 0.0 collective-permute-done.other_ref
  14.2 0.4 shard_map.105
  14.6 17.7 %all_to_all.10 = f32[16,1,3712]{2,1,0:T(1,128)S(1)} all-to-all(f32[16,1,3712]{2,1,0:T(1,128)S(1)} %bitcast.18), channel_id=1, replica_groups=mesh['col'=16,'slab'=32] {'col'}, dimensions={0} | all-to-all | bytes 475136 | tf_op jit(solution)/shard_map/all_to_all | solution.py:485
  32.3 0.7 %shard_map.106 = f32[72,128]{1,0:T(8,128)S(1)} custom-call(f32[464,128]{1,0:T(8,128)S(1)} %bitcast.15), custom_call_target="tpu_custom_call" | custom-call | flops 20000 | bytes 500000 | tf_op jit(solution)/shard_map/pallas_call | solution.py:521
  32.9 7.5 %all_to_all.11 = f32[8,1,1152]{2,1,0:T(1,128)S(1)} all-to-all(f32[8,1,1152]{2,1,0:T(1,128)S(1)} %bitcast.19), channel_id=1, replica_groups={{0,32,64,96,128,160,192,224},{256,288,320,352,384,416,448,480},{1,33,65..., dimensions={0} | all-to-all | bytes 73728 | tf_op jit(solution)/shard_map/all_to_all | solution.py:485
  40.4 9.2 %collective-permute-start.1 = (f32[1,128]{1,0:T(1,128)S(1)}, f32[1,128]{1,0:T(1,128)S(1)}, u32[]{:S(2)}, u32[]{:S(2)}) collective-permute-start(f32[1,128]{1,0:T(1,128)S(1)} %shard_map.108.load_ref), channel_id=1, source_target_pairs={{1,2},{3,4},{5,6},{7,8},{9,10},{11,12},{13,14},{15,16},{17,18},{19... | collective-permute-start | bytes 1544 | tf_op jit(solution)/shard_map/ppermute | solution.py:536
  49.6 1.8 %all-gather.2.pair_ref = f32[2,1,128]{2,1,0:T(1,128)S(1)} all-gather(f32[1,1,128]{2,1,0:T(1,128)S(1)} %bitcast.21), channel_id=3, replica_groups={{0,1},{2,3},{4,5},{6,7},{8,9},{10,11},{12,13},{14,15},{16,17},{18,19},{..., dimensions={0}, use_global_device_ids=true | all-gather | bytes 1536 | tf_op jit(solution)/shard_map/all_gather | solution.py:537
  51.4 0.7 %shard_map.107 = (f32[64,256]{1,0:T(8,128)}, f32[64,256]{1,0:T(8,128)}) custom-call(f32[72,128]{1,0:T(8,128)S(1)} %bitcast.17, f32[240,256]{1,0:T(8,128)S(1)} %get-tuple-element.26.mat_ref, f32[48,256]{1,0:T(8,128)S(1)} %get-tuple-element.32.offset_ref, f32[64,256]{1,0:T(8,128)S(1)} %get-tuple-element.22.w_ref), custom_call_target="tpu_custom_call" | custom-call | flops 5000000 | bytes 500000 | tf_op jit(solution)/shard_map/pallas_call | solution.py:538
  52.1 0.0 collective-permute-done.1.other_ref
  52.1 0.7 %shard_map.109 = f32[3,4]{1,0:T(4,128)} custom-call(f32[1,128]{1,0:T(1,128)S(1)} %shard_map.108.load_ref, f32[2,1,128]{2,1,0:T(1,128)S(1)} %all-gather.2.pair_ref, f32[1,128]{1,0:T(1,128)S(1)} %collective-permute-done.1.other_ref), custom_call_target="tpu_custom_call" | custom-call | flops 20000 | bytes 500000 | tf_op jit(solution)/shard_map/pallas_call | solution.py:539
  (1 shorter events, 0.0 us)
Async XLA Ops:
  1.8 12.4 %collective-permute-start = (f32[8,256]{1,0:T(8,128)S(1)}, f32[8,256]{1,0:T(8,128)S(1)}, u32[]{:S(2)}, u32[]{:S(2)}) collective-permute-start(f32[8,256]{1,0:T(8,128)S(1)} %get-tuple-element.28), channel_id=1, source_target_pairs={{1,2},{3,4},{5,6},{7,8},{9,10},{11,12},{13,14},{15,16},{17,18},{19... | collective-permute-start | bytes 24584 | tf_op jit(solution)/shard_map/ppermute | solution.py:512
  40.4 11.6 %collective-permute-start.1 = (f32[1,128]{1,0:T(1,128)S(1)}, f32[1,128]{1,0:T(1,128)S(1)}, u32[]{:S(2)}, u32[]{:S(2)}) collective-permute-start(f32[1,128]{1,0:T(1,128)S(1)} %shard_map.108.load_ref), channel_id=1, source_target_pairs={{1,2},{3,4},{5,6},{7,8},{9,10},{11,12},{13,14},{15,16},{17,18},{19... | collective-permute-start | bytes 1544 | tf_op jit(solution)/shard_map/ppermute | solution.py:536

commit v10 on v9

--- a/solution.py
+++ b/solution.py
@@ -435,7 +435,10 @@
     load_ref[...] = jnp.sum(packed, axis=0, keepdims=True)
 
 
-def field_kernel(back_ref, mat_ref, offset_ref, w_ref, pressure_ref, velocity_ref):
+def final_kernel(
+    back_ref, mat_ref, offset_ref, w_ref, load_ref, pair_ref, other_ref,
+    pressure_ref, velocity_ref, out_ref,
+):
     def end(at):
         halves = [back_ref[pl.ds(half * 4 + at, CX, stride=BACK_ROWS), :] for half in range(2)]
         return jnp.concatenate(halves, axis=1)
@@ -452,8 +455,6 @@
         pressure_ref[z * CX : (z + 1) * CX, :] = pressure[z]
         velocity_ref[z * CX : (z + 1) * CX, :] = level(w_ref, z) - 0.5 * (flux[z + 1] + flux[z])
 
-
-def section_kernel(load_ref, pair_ref, other_ref, out_ref):
     core = lax.rem(lax.axis_index("slab"), 2)
     even = core == 0
     received, beyond = pair_ref[1 - core], other_ref[...]
@@ -535,8 +536,9 @@
     loads = call(load_kernel, [(1, LANES)])(back)
     loads_other = lax.ppermute(loads, "slab", others)
     loads_pair = lax.all_gather(loads, "slab", axis_index_groups=cores)
-    pressure, velocity = call(field_kernel, [flat, flat], flops=5000000)(back, mat, offsets, w)
-    section_loads = call(section_kernel, [(3, SEC_DEV)])(loads, loads_pair, loads_other)
+    pressure, velocity, section_loads = call(final_kernel, [flat, flat, (3, SEC_DEV)])(
+        back, mat, offsets, w, loads, loads_pair, loads_other
+    )
     return pressure.reshape(p_star.shape), velocity.reshape(p_star.shape), section_loads
 
 

time: 53.1 us -> 53.1 us (level); the launches traced: 52.8 us -> 52.1 us
  Pallas kernels: 3.96 us -> 3.3 us
    pallas_call x2 -> x1, Pallas kernels: 1.4 us -> 0.74 us  [per_device(): call(final_kernel, [flat, flat, (3, SEC_DEV)])]
  transfers between devices with their start and end apart: 2 -> 2, of which waited for: 0 -> 0; matrix products, arithmetic and copies ran while one was open for 0% -> 0% of each run, Pallas kernels for 2% -> 1%
where the time goes in v10:
time: 53.1 us; the launch traced here: 52.1 us
  blocking collectives  28.8 us (54%)
  starting transfers between devices  19.4 us (37%)
  Pallas kernels  3.3 us (6%)
  between operations  0.67 us (1%)
    all_to_all x2, blocking collectives, exchange(): x = lax.all_to_all(x, 'col', 0, 0, axis_index_groups=groups, tiled=True)  25.2 us
    ppermute x1, starting transfers between devices, per_device(): from_other = lax.ppermute(to_other, 'slab', others)  10.2 us
    ppermute x1, starting transfers between devices, per_device(): loads_other = lax.ppermute(loads, 'slab', others)  9.16 us
    all_gather x1, blocking collectives, per_device(): from_pair = lax.all_gather(to_pair, 'slab', axis_index_groups=cores)  1.81 us
    all_gather x1, blocking collectives, per_device(): loads_pair = lax.all_gather(loads, 'slab', axis_index_groups=cores)  1.77 us
    pallas_call x1, Pallas kernels, per_device(): pl.pallas_call(fetch_kernel, out_shape=[jax.ShapeDtypeStruct(x.shape, x.d...  1.14 us
  transfers between devices with their start and end apart: 2, of which 0 were waited for; matrix products, arithmetic and copies ran while one was open for 0% of the time, Pallas kernels for 1%

profile of v10, /device:TPU:1, one launch (start us, length us, event | category | flops | bytes accessed | tf_op | source)
XLA Modules:
  0.0 52.1 jit_solution(12006093845213112381)
XLA Ops:
  0.6 1.1 %shard_map.103 = (f32[64,256]{1,0:T(8,128)S(1)}, f32[64,256]{1,0:T(8,128)S(1)}, f32[64,256]{1,0:T(8,128)S(1)}, f32[64,256]{1,0:T(8,128)S(1)}, s32[64,256]{1,0:T(...) custom-call(f32[64,256]{1,0:T(8,128)} %bitcast.22, ...), custom_call_target="tpu_custom_call" | custom-call | flops 20000 | bytes 500000 | tf_op jit(solution)/shard_map/pallas_call | solution.py:503
  1.8 10.2 %collective-permute-start = (f32[8,256]{1,0:T(8,128)S(1)}, f32[8,256]{1,0:T(8,128)S(1)}, u32[]{:S(2)}, u32[]{:S(2)}) collective-permute-start(f32[8,256]{1,0:T(8,128)S(1)} %get-tuple-element.29), channel_id=1, source_target_pairs={{1,2},{3,4},{5,6},{7,8},{9,10},{11,12},{13,14},{15,16},{17,18},{19... | collective-permute-start | bytes 24584 | tf_op jit(solution)/shard_map/ppermute | solution.py:513
  12.0 0.4 shard_map.104
  12.4 1.8 %all-gather = f32[16,256]{1,0:T(8,128)S(1)} all-gather(f32[8,256]{1,0:T(8,128)S(1)} %get-tuple-element.30), channel_id=2, replica_groups={{0,1},{2,3},{4,5},{6,7},{8,9},{10,11},{12,13},{14,15},{16,17},{18,19},{..., dimensions={0}, use_global_device_ids=true | all-gather | bytes 24576 | tf_op jit(solution)/shard_map/all_gather | solution.py:514
  14.2 0.0 collective-permute-done.other_ref
  14.2 0.4 shard_map.105
  14.6 17.7 %all_to_all.10 = f32[16,1,3712]{2,1,0:T(1,128)S(1)} all-to-all(f32[16,1,3712]{2,1,0:T(1,128)S(1)} %bitcast.18), channel_id=1, replica_groups=mesh['col'=16,'slab'=32] {'col'}, dimensions={0} | all-to-all | bytes 475136 | tf_op jit(solution)/shard_map/all_to_all | solution.py:486
  32.3 0.7 %shard_map.106 = f32[72,128]{1,0:T(8,128)S(1)} custom-call(f32[464,128]{1,0:T(8,128)S(1)} %bitcast.15), custom_call_target="tpu_custom_call" | custom-call | flops 20000 | bytes 500000 | tf_op jit(solution)/shard_map/pallas_call | solution.py:522
  32.9 7.5 %all_to_all.11 = f32[8,1,1152]{2,1,0:T(1,128)S(1)} all-to-all(f32[8,1,1152]{2,1,0:T(1,128)S(1)} %bitcast.19), channel_id=1, replica_groups={{0,32,64,96,128,160,192,224},{256,288,320,352,384,416,448,480},{1,33,65..., dimensions={0} | all-to-all | bytes 73728 | tf_op jit(solution)/shard_map/all_to_all | solution.py:486
  40.4 9.2 %collective-permute-start.1 = (f32[1,128]{1,0:T(1,128)S(1)}, f32[1,128]{1,0:T(1,128)S(1)}, u32[]{:S(2)}, u32[]{:S(2)}) collective-permute-start(f32[1,128]{1,0:T(1,128)S(1)} %shard_map.107.load_ref), channel_id=1, source_target_pairs={{1,2},{3,4},{5,6},{7,8},{9,10},{11,12},{13,14},{15,16},{17,18},{19... | collective-permute-start | bytes 1544 | tf_op jit(solution)/shard_map/ppermute | solution.py:537
  49.6 1.8 %all-gather.2.pair_ref = f32[2,1,128]{2,1,0:T(1,128)S(1)} all-gather(f32[1,1,128]{2,1,0:T(1,128)S(1)} %bitcast.21), channel_id=3, replica_groups={{0,1},{2,3},{4,5},{6,7},{8,9},{10,11},{12,13},{14,15},{16,17},{18,19},{..., dimensions={0}, use_global_device_ids=true | all-gather | bytes 1536 | tf_op jit(solution)/shard_map/all_gather | solution.py:538
  51.4 0.0 collective-permute-done.1.other_ref
  51.4 0.7 %shard_map.108 = (f32[64,256]{1,0:T(8,128)}, f32[64,256]{1,0:T(8,128)}, f32[3,4]{1,0:T(4,128)}) custom-call(f32[72,128]{1,0:T(8,128)S(1)} %bitcast.17, f32[240,256]{1,0:T(8,128)S(1)} %get-tuple-element.27.mat_ref, f32[48,256]{1,0:T(8,128)S(1)} %get-tuple-element.33.offset_ref, f32[64,256]{1,0:T(8,128)S(1)} %get-tuple-element.23.w_ref, ...), custom_call_target="tpu_custom_call" | custom-call | flops 20000 | bytes 500000 | tf_op jit(solution)/shard_map/pallas_call | solution.py:539
  (1 shorter events, 0.0 us)
Async XLA Ops:
  1.8 12.4 %collective-permute-start = (f32[8,256]{1,0:T(8,128)S(1)}, f32[8,256]{1,0:T(8,128)S(1)}, u32[]{:S(2)}, u32[]{:S(2)}) collective-permute-start(f32[8,256]{1,0:T(8,128)S(1)} %get-tuple-element.29), channel_id=1, source_target_pairs={{1,2},{3,4},{5,6},{7,8},{9,10},{11,12},{13,14},{15,16},{17,18},{19... | collective-permute-start | bytes 24584 | tf_op jit(solution)/shard_map/ppermute | solution.py:513
  40.4 10.9 %collective-permute-start.1 = (f32[1,128]{1,0:T(1,128)S(1)}, f32[1,128]{1,0:T(1,128)S(1)}, u32[]{:S(2)}, u32[]{:S(2)}) collective-permute-start(f32[1,128]{1,0:T(1,128)S(1)} %shard_map.107.load_ref), channel_id=1, source_target_pairs={{1,2},{3,4},{5,6},{7,8},{9,10},{11,12},{13,14},{15,16},{17,18},{19... | collective-permute-start | bytes 1544 | tf_op jit(solution)/shard_map/ppermute | solution.py:537

commit v11 on v10

--- a/solution.py
+++ b/solution.py
@@ -357,7 +357,6 @@
         for end in range(2):
             for at, part in enumerate(split_three(nodes[2 * x + end])):
                 put(parts_ref, 16, half * 8 + 3 * end + at, x, part.astype(F32))
-            put(parts_ref, 16, half * 8 + 6 + end, x, jnp.zeros((4, LANES), F32))
 
 
 def owner_kernel(

time: 53.1 us -> 53.1 us (level)
  no operation moved by 1% of the time
where the time goes in v11:
time: 53.1 us; the launch traced here: 52.1 us
  blocking collectives  28.8 us (54%)
  starting transfers between devices  19.4 us (37%)
  Pallas kernels  3.28 us (6%)
  between operations  0.67 us (1%)
    all_to_all x2, blocking collectives, exchange(): x = lax.all_to_all(x, 'col', 0, 0, axis_index_groups=groups, tiled=True)  25.2 us
    ppermute x1, starting transfers between devices, per_device(): from_other = lax.ppermute(to_other, 'slab', others)  10.2 us
    ppermute x1, starting transfers between devices, per_device(): loads_other = lax.ppermute(loads, 'slab', others)  9.16 us
    all_gather x1, blocking collectives, per_device(): from_pair = lax.all_gather(to_pair, 'slab', axis_index_groups=cores)  1.81 us
    all_gather x1, blocking collectives, per_device(): loads_pair = lax.all_gather(loads, 'slab', axis_index_groups=cores)  1.77 us
    pallas_call x1, Pallas kernels, per_device(): pl.pallas_call(fetch_kernel, out_shape=[jax.ShapeDtypeStruct(x.shape, x.d...  1.14 us
  transfers between devices with their start and end apart: 2, of which 0 were waited for; matrix products, arithmetic and copies ran while one was open for 0% of the time, Pallas kernels for 1%

profile of v11, /device:TPU:1, one launch (start us, length us, event | category | flops | bytes accessed | tf_op | source)
XLA Modules:
  0.0 52.1 jit_solution(6188241041412685732)
XLA Ops:
  0.6 1.1 %shard_map.103 = (f32[64,256]{1,0:T(8,128)S(1)}, f32[64,256]{1,0:T(8,128)S(1)}, f32[64,256]{1,0:T(8,128)S(1)}, f32[64,256]{1,0:T(8,128)S(1)}, s32[64,256]{1,0:T(...) custom-call(f32[64,256]{1,0:T(8,128)} %bitcast.22, ...), custom_call_target="tpu_custom_call" | custom-call | flops 20000 | bytes 500000 | tf_op jit(solution)/shard_map/pallas_call | solution.py:502
  1.8 10.2 %collective-permute-start = (f32[8,256]{1,0:T(8,128)S(1)}, f32[8,256]{1,0:T(8,128)S(1)}, u32[]{:S(2)}, u32[]{:S(2)}) collective-permute-start(f32[8,256]{1,0:T(8,128)S(1)} %get-tuple-element.29), channel_id=1, source_target_pairs={{1,2},{3,4},{5,6},{7,8},{9,10},{11,12},{13,14},{15,16},{17,18},{19... | collective-permute-start | bytes 24584 | tf_op jit(solution)/shard_map/ppermute | solution.py:512
  12.0 0.4 shard_map.104
  12.4 1.8 %all-gather = f32[16,256]{1,0:T(8,128)S(1)} all-gather(f32[8,256]{1,0:T(8,128)S(1)} %get-tuple-element.30), channel_id=2, replica_groups={{0,1},{2,3},{4,5},{6,7},{8,9},{10,11},{12,13},{14,15},{16,17},{18,19},{..., dimensions={0}, use_global_device_ids=true | all-gather | bytes 24576 | tf_op jit(solution)/shard_map/all_gather | solution.py:513
  14.2 0.0 collective-permute-done.other_ref
  14.2 0.4 shard_map.105
  14.6 17.7 %all_to_all.10 = f32[16,1,3712]{2,1,0:T(1,128)S(1)} all-to-all(f32[16,1,3712]{2,1,0:T(1,128)S(1)} %bitcast.18), channel_id=1, replica_groups=mesh['col'=16,'slab'=32] {'col'}, dimensions={0} | all-to-all | bytes 475136 | tf_op jit(solution)/shard_map/all_to_all | solution.py:485
  32.3 0.7 %shard_map.106 = f32[72,128]{1,0:T(8,128)S(1)} custom-call(f32[464,128]{1,0:T(8,128)S(1)} %bitcast.15), custom_call_target="tpu_custom_call" | custom-call | flops 20000 | bytes 500000 | tf_op jit(solution)/shard_map/pallas_call | solution.py:521
  32.9 7.5 %all_to_all.11 = f32[8,1,1152]{2,1,0:T(1,128)S(1)} all-to-all(f32[8,1,1152]{2,1,0:T(1,128)S(1)} %bitcast.19), channel_id=1, replica_groups={{0,32,64,96,128,160,192,224},{256,288,320,352,384,416,448,480},{1,33,65..., dimensions={0} | all-to-all | bytes 73728 | tf_op jit(solution)/shard_map/all_to_all | solution.py:485
  40.4 9.2 %collective-permute-start.1 = (f32[1,128]{1,0:T(1,128)S(1)}, f32[1,128]{1,0:T(1,128)S(1)}, u32[]{:S(2)}, u32[]{:S(2)}) collective-permute-start(f32[1,128]{1,0:T(1,128)S(1)} %shard_map.107.load_ref), channel_id=1, source_target_pairs={{1,2},{3,4},{5,6},{7,8},{9,10},{11,12},{13,14},{15,16},{17,18},{19... | collective-permute-start | bytes 1544 | tf_op jit(solution)/shard_map/ppermute | solution.py:536
  49.6 1.8 %all-gather.2.pair_ref = f32[2,1,128]{2,1,0:T(1,128)S(1)} all-gather(f32[1,1,128]{2,1,0:T(1,128)S(1)} %bitcast.21), channel_id=3, replica_groups={{0,1},{2,3},{4,5},{6,7},{8,9},{10,11},{12,13},{14,15},{16,17},{18,19},{..., dimensions={0}, use_global_device_ids=true | all-gather | bytes 1536 | tf_op jit(solution)/shard_map/all_gather | solution.py:537
  51.4 0.0 collective-permute-done.1.other_ref
  51.4 0.7 %shard_map.108 = (f32[64,256]{1,0:T(8,128)}, f32[64,256]{1,0:T(8,128)}, f32[3,4]{1,0:T(4,128)}) custom-call(f32[72,128]{1,0:T(8,128)S(1)} %bitcast.17, f32[240,256]{1,0:T(8,128)S(1)} %get-tuple-element.27.mat_ref, f32[48,256]{1,0:T(8,128)S(1)} %get-tuple-element.33.offset_ref, f32[64,256]{1,0:T(8,128)S(1)} %get-tuple-element.23.w_ref, ...), custom_call_target="tpu_custom_call" | custom-call | flops 20000 | bytes 500000 | tf_op jit(solution)/shard_map/pallas_call | solution.py:538
  (1 shorter events, 0.0 us)
Async XLA Ops:
  1.8 12.4 %collective-permute-start = (f32[8,256]{1,0:T(8,128)S(1)}, f32[8,256]{1,0:T(8,128)S(1)}, u32[]{:S(2)}, u32[]{:S(2)}) collective-permute-start(f32[8,256]{1,0:T(8,128)S(1)} %get-tuple-element.29), channel_id=1, source_target_pairs={{1,2},{3,4},{5,6},{7,8},{9,10},{11,12},{13,14},{15,16},{17,18},{19... | collective-permute-start | bytes 24584 | tf_op jit(solution)/shard_map/ppermute | solution.py:512
  40.4 10.9 %collective-permute-start.1 = (f32[1,128]{1,0:T(1,128)S(1)}, f32[1,128]{1,0:T(1,128)S(1)}, u32[]{:S(2)}, u32[]{:S(2)}) collective-permute-start(f32[1,128]{1,0:T(1,128)S(1)} %shard_map.107.load_ref), channel_id=1, source_target_pairs={{1,2},{3,4},{5,6},{7,8},{9,10},{11,12},{13,14},{15,16},{17,18},{19... | collective-permute-start | bytes 1544 | tf_op jit(solution)/shard_map/ppermute | solution.py:536
